TPU v7x, 32 devices: a whole 2x2x4 slice. The times are simulated.
32 devices in a mesh: row: 4 (over z), col: 8 (over y, x, core).
Axes of the slice: x: 2, y: 2, z: 4, core: 2. Of those that a mesh axis runs over, the one named last changes fastest.
Arguments:
- points: float32 [4096, 128], P('row'), may hold values from -6 to 6
- panel_pool: float32 [4096, 128], P('col'), may hold values from -6 to 6
- order: int32 [512], replicated, may hold values from 0 to 511, each once
- panel_index: int32 [1], replicated, may hold values from 0 to 7
- inv_factor: float32 [512, 512], replicated, as said below
- ard_weights: float32 [128], replicated, may hold values from 0.001 to 0.1
- noise: float32 [4096], P('row'), may hold values from 0.05 to 1
Outputs:
- schur: float32 [4096, 4096], P('row', 'col')
Inputs may be any that keep to these rules, and one draw needn't show every extreme that they name: `order`: a permutation of 0 to 511. `inv_factor`: lower triangular: zero above the diagonal.
All inputs are finite; a program needn't handle non-finite values.
Results may differ from a plain program's by a relative error of at most 0.0003.
Values sent between devices are 32-bit elements; how exact they have to be, the bound alone decides.
No kernel may reach another device: no remote copies, remote signals or barrier semaphores. Data moves between devices by JAX's collectives and lax.ppermute only.
A program may use at most 64 MiB of HBM per device.

v0:
```python
import collections
import functools
import math
import random

import jax
import jax.numpy as jnp
from jax import lax
from jax.experimental import pallas as pl
from jax.experimental.pallas import tpu as pltpu
from jax.sharding import PartitionSpec as P

log2_e = 1.4426950408889634
vmem_bytes = 32 * 1024 * 1024
f32, bf16 = jnp.float32, jnp.bfloat16
block = 256


def halves_of(value):
    high = value.astype(bf16)
    low = (value - high.astype(f32)).astype(bf16)
    return high, low


def pack_left(high, low):
    return jnp.concatenate([high, low, high, low], axis=1)


def pack_right(high, low):
    return jnp.concatenate([high, low, low, high], axis=0)


def half_square(high, low, axis):
    value = high.astype(f32) + low.astype(f32)
    return 0.5 * jnp.sum(value * value, axis=axis, keepdims=True)


def product(left, right):
    return lax.dot_general(left, right, (((1,), (0,)), ((), ())), preferred_element_type=f32)


def store_left(ref, rows, first, value):
    high, low = halves_of(value)
    for start in range(0, value.shape[1], block):
        now, at = slice(start, start + block), 3 * (first + start)
        ref[rows, at : at + block] = high[:, now]
        ref[rows, at + block : at + 2 * block] = high[:, now]
        ref[rows, at + 2 * block : at + 3 * block] = low[:, now]


def store_right(ref, first, value):
    high, low = halves_of(value)
    for start in range(0, value.shape[0], block):
        now, at = slice(start, start + block), 3 * (first + start)
        ref[at : at + block, :] = high[now]
        ref[at + block : at + 2 * block, :] = low[now]
        ref[at + 2 * block : at + 3 * block, :] = high[now]


def kern(crossed, left_half, right_half):
    return jnp.exp2((crossed - left_half) - (right_half - 1.0))


def scale_of(vectors_ref, panel, features):
    return jnp.sqrt(vectors_ref[:, panel : panel + features] * log2_e)


def parts_kernel(
    factor_ref, points_ref, vectors_ref, factor_left_ref, factor_right_ref, pick_ref, left_ref,
    left_half_ref,
):
    factor = factor_ref[...]
    store_left(factor_left_ref, slice(None), 0, factor)
    store_right(factor_right_ref, 0, jnp.transpose(factor))
    panel = factor.shape[0]
    core = lax.axis_index("col") % 2
    place = lax.broadcasted_iota(jnp.int32, (panel, panel), 0) + core * (panel // 2)
    place = jnp.where(place >= panel, place - panel, place).astype(f32)
    hit = jnp.where(place == vectors_ref[:, :panel], 1.0, 0.0).astype(f32)
    pick_ref[...] = jnp.transpose(hit).astype(bf16)
    high, low = halves_of(points_ref[...] * scale_of(vectors_ref, panel, points_ref.shape[1]))
    left_ref[...] = pack_left(high, low)
    left_half_ref[...] = half_square(high, low, 1)


def rows_kernel(
    own_ref, other_ref, vectors_ref, factor_right_ref, pick_ref, left_ref, left_half_ref,
    rows_ref, chosen_ref, chosen_half_ref, kern_ref,
):
    panel = pick_ref.shape[0]
    features = own_ref.shape[1]
    held = jnp.concatenate([own_ref[...], other_ref[...]], axis=0) * scale_of(vectors_ref, panel, features)
    chosen = product(pick_ref[...], jnp.concatenate(halves_of(held), axis=1))
    high, low = chosen[:, :features].astype(bf16), chosen[:, features:].astype(bf16)
    chosen_ref[...] = pack_left(high, low)
    chosen_half_ref[...] = half_square(high, low, 1)
    turned = jnp.transpose(chosen)
    high, low = turned[:features].astype(bf16), turned[features:].astype(bf16)
    right = pack_right(high, low)
    right_half = half_square(high, low, 0)
    chunks = 2
    count = left_ref.shape[0] // chunks
    places = [slice(number * count, (number + 1) * count) for number in range(chunks)]
    crossed = [product(left_ref[place, :], right) for place in places]
    for number, place in enumerate(places):
        store_left(kern_ref, place, 0, kern(crossed[number], left_half_ref[place, :], right_half))
        for first in range(0, panel, block):
            last = first + block
            part = product(kern_ref[place, : 3 * last], factor_right_ref[: 3 * last, first:last])
            store_left(rows_ref, place, first, part)


def update_kernel(
    rows, cols, sent_ref, vectors_ref, factor_left_ref, left_ref, left_half_ref, rows_ref, chosen_ref,
    chosen_half_ref, out_ref, block_ref, kern_ref, cols_ref, sems,
):
    row_place, col_place = lax.axis_index("row"), lax.axis_index("col")
    halves = cols // rows
    count = sent_ref.shape[0]
    part = col_place % halves
    own = row_place == col_place // halves
    panel, features = factor_left_ref.shape[0], sent_ref.shape[1]

    high, low = halves_of(jnp.transpose(sent_ref[...] * scale_of(vectors_ref, panel, features)))
    right = pack_right(high, low)
    right_half = half_square(high, low, 0)
    chunks, chunk = block_ref.shape[:2]
    places = [slice(number * chunk, (number + 1) * chunk) for number in range(chunks)]
    at = pl.multiple_of(panel + features + part * count, 128)
    noise = jnp.where(own, vectors_ref[:, pl.ds(at, count)], 0.0)
    ids = (chunk, count)
    below = lax.broadcasted_iota(jnp.int32, ids, 0) - lax.broadcasted_iota(jnp.int32, ids, 1)

    crossed = product(chosen_ref[...], right)
    tiles = [product(left_ref[place, :], right) for place in places]
    store_right(kern_ref, 0, kern(crossed, chosen_half_ref[...], right_half))
    for first in range(0, panel, block):
        last = first + block
        store_right(cols_ref, first, product(factor_left_ref[first:last, : 3 * last], kern_ref[: 3 * last, :]))
    for number, place in enumerate(places):
        tile = kern(tiles[number], left_half_ref[place, :], right_half)
        block_ref[number] = tile + jnp.where(below == part * count - number * chunk, noise, 0.0)

    copies = []
    for number, place in enumerate(places):
        block_ref[number] = block_ref[number] - product(rows_ref[place, :], cols_ref[...])
        copy = pltpu.make_async_copy(block_ref.at[number], out_ref.at[pl.ds(number * chunk, chunk)], sems.at[number])
        copy.start()
        copies.append(copy)
    for copy in copies:
        copy.wait()


def shape(dims, kind=f32):
    return jax.ShapeDtypeStruct(dims, kind)


def compute_params(flops, moved):
    return dict(
        compiler_params=pltpu.CompilerParams(vmem_limit_bytes=vmem_bytes),
        cost_estimate=pl.CostEstimate(flops=flops, bytes_accessed=moved, transcendentals=0),
    )


def links_of(place, group, target_row, across):
    links = []
    step = 1 if target_row > group else -1
    links += [(0, place, z, step) for z in range(group, target_row, step)]
    (x, y), (end_x, end_y) = (place % across, place // across), (group % across, group // across)
    step = 1 if end_x > x else -1
    links += [(1, target_row, y, at, step) for at in range(x, end_x, step)]
    step = 1 if end_y > y else -1
    links += [(2, target_row, end_x, at, step) for at in range(y, end_y, step)]
    return links


def source_places(rows, halves):
    draw = random.Random(5)
    across = math.isqrt(rows)
    places = {}
    load = collections.Counter()

    def move(key, r, sign):
        change = 0
        for link in links_of(places[key][r], key[1], r, across):
            old = load[link]
            load[link] = old + sign
            change += (old + sign) ** 4 - old**4
        return change

    for h in range(halves):
        for g in range(rows):
            places[h, g] = draw.sample(range(rows), rows)
            for r in range(rows):
                move((h, g), r, 1)
    best, total, kept = 0, 0, {key: list(value) for key, value in places.items()}
    tries = 20000
    for number in range(tries):
        key = draw.randrange(halves), draw.randrange(rows)
        one, two = draw.sample(range(rows), 2)
        own = places[key]
        change = move(key, one, -1) + move(key, two, -1)
        own[one], own[two] = own[two], own[one]
        change += move(key, one, 1) + move(key, two, 1)
        heat = 30.0 * (1 - number / tries) + 0.01
        if change <= 0 or draw.random() < math.exp(-change / heat):
            total += change
            if total < best:
                best, kept = total, {key: list(value) for key, value in places.items()}
        else:
            move(key, one, -1), move(key, two, -1)
            own[one], own[two] = own[two], own[one]
            move(key, one, 1), move(key, two, 1)
    return kept


def column_pairs(rows, cols):
    halves = cols // rows
    places = source_places(rows, halves)
    return [
        (g * cols + places[h, g][r] * halves + h, r * cols + g * halves + h)
        for h in range(halves)
        for g in range(rows)
        for r in range(rows)
    ]


def swap(value, bit, cols):
    return lax.ppermute(value, "col", [(i, i ^ bit) for i in range(cols)])


def gather_panel(panel_pool, panel_block, cols, beside):
    col_place = lax.axis_index("col")
    core = col_place % 2
    half_rows = panel_pool.shape[0] // 2
    mine = lax.dynamic_slice_in_dim(panel_pool, core * half_rows, half_rows, 0)
    got, mine, beside = lax.optimization_barrier((swap(panel_pool, 1, cols), mine, beside))
    got = lax.dynamic_slice_in_dim(got, core * half_rows, half_rows, 0)
    held = jnp.where(panel_block % 2 == core, mine, got)
    apart = panel_block ^ col_place
    low = 2
    while low < cols:
        high = min(4 * low, cols)
        away = apart & (high - low)
        received = [swap(held, bits, cols) for bits in range(low, high, low)]
        for bits, value in zip(range(low, high, low), received):
            held = jnp.where(away == bits, value, held)
        low = high
    return [held, swap(held, 1, cols)], beside


def on_device(points, panel_pool, order, panel_index, inv_factor, ard_weights, noise):
    row_count, features = points.shape
    panel = inv_factor.shape[0]
    rows = lax.axis_size("row")
    cols = lax.axis_size("col")
    col_count = row_count * rows // cols
    halves = cols // rows
    col_place = lax.axis_index("col")
    own_half = lax.dynamic_slice_in_dim(points, col_place % halves * col_count, col_count, 0)
    sent = lax.ppermute(own_half, ("row", "col"), column_pairs(rows, cols))
    vectors = jnp.concatenate([order.astype(f32), ard_weights, noise])[None, :]
    pieces, vectors = gather_panel(panel_pool, panel_index[0], cols, vectors)

    packed = 4 * features
    factor_left, factor_right, pick, left, left_half = pl.pallas_call(
        parts_kernel,
        out_shape=[
            shape((panel, 3 * panel), bf16),
            shape((3 * panel, panel), bf16),
            shape((panel, panel), bf16),
            shape((row_count, packed), bf16),
            shape((row_count, 1)),
        ],
        **compute_params(10**8, 4 * 10**6),
    )(inv_factor, points, vectors)

    rows_left, chosen, chosen_half = pl.pallas_call(
        rows_kernel,
        out_shape=[shape((row_count, 3 * panel), bf16), shape((panel, packed), bf16), shape((panel, 1))],
        scratch_shapes=[pltpu.VMEM((row_count, 3 * panel), bf16)],
        **compute_params(1, 1),
    )(*pieces, vectors, factor_right, pick, left, left_half)

    chunks = 4
    return pl.pallas_call(
        functools.partial(update_kernel, rows, cols),
        out_shape=shape((row_count, col_count)),
        out_specs=pl.BlockSpec(memory_space=pl.ANY),
        scratch_shapes=[
            pltpu.VMEM((chunks, row_count // chunks, col_count), f32),
            pltpu.VMEM((3 * panel, col_count), bf16),
            pltpu.VMEM((3 * panel, col_count), bf16),
            pltpu.SemaphoreType.DMA((chunks,)),
        ],
        **compute_params(4 * 10**9, 8 * 10**6),
    )(sent, vectors, factor_left, left, left_half, rows_left, chosen, chosen_half)


def solution(mesh):
    in_specs = (P("row", None), P("col", None), P(), P(), P(), P(), P("row"))
    out_specs = P("row", "col")
    return jax.shard_map(
        on_device, mesh=mesh, in_specs=in_specs, out_specs=out_specs, check_vma=False
    )
```

profile of v0, /device:TPU:12, one launch (start us, length us, event | category | flops | bytes accessed | tf_op | source)
XLA Modules:
  0.0 24.9 jit_solution(5795029115377265153)
XLA Ops:
  0.0 0.0 copy-start
  0.0 0.0 copy-start.1
  0.0 0.0 collective-permute-start.1
  0.8 0.7 %convert_element_type.3 = f32[512]{0:T(512)S(1)} convert(s32[512]{0:T(512)} %param.9) | non-fusion elementwise | flops 512 | bytes 4096 | tf_op jit(solution)/shard_map/convert_element_type | solution.py:262
  1.5 0.7 %pad_maximum_fusion = f32[1664]{0:T(1024)S(1)} fusion(f32[1024]{0:T(1024)} %param.13, f32[128]{0:T(128)} %param.12, f32[512]{0:T(512)S(1)} %convert_element_type.3), kind=kLoop, calls=%fused_computation.2 | loop fusion | flops 3328 | bytes 13312 | tf_op jit(solution)/shard_map/concatenate | solution.py:262
  2.2 0.9 %constant_dynamic-slice_fusion = f32[256,128]{1,0:T(8,128)S(1)} fusion(f32[512,128]{1,0:T(8,128)} %param.8, s32[]{:T(128)S(6)} %select_n.48), kind=kLoop, calls=%fused_computation.3 | loop fusion | bytes 262148 | tf_op jit(solution)/shard_map/dynamic_slice | solution.py:236
  3.1 0.0 collective-permute-done.1
  3.2 1.5 %collective-permute-start.2 = (f32[256,128]{1,0:T(8,128)S(1)}, f32[256,128]{1,0:T(8,128)S(1)}, u32[]{:S(2)}, u32[]{:S(2)}) collective-permute-start(f32[256,128]{1,0:T(8,128)S(1)} %dynamic-slice_select_fusion), channel_id=1, source_target_pairs={{0,6},{1,7},{2,4},{3,5},{4,2},{5,3},{6,0},{7,1},{8,14},{9,15},{10,... | collective-permute-start | bytes 393224 | tf_op jit(solution)/shard_map/ppermute | solution.py:229
  4.7 1.5 %collective-permute-start.3 = (f32[256,128]{1,0:T(8,128)S(1)}, f32[256,128]{1,0:T(8,128)S(1)}, u32[]{:S(2)}, u32[]{:S(2)}) collective-permute-start(f32[256,128]{1,0:T(8,128)S(1)} %dynamic-slice_select_fusion), channel_id=1, source_target_pairs={{0,4},{1,5},{2,6},{3,7},{4,0},{5,1},{6,2},{7,3},{8,12},{9,13},{10,... | collective-permute-start | bytes 393224 | tf_op jit(solution)/shard_map/ppermute | solution.py:229
  6.2 0.5 %collective-permute-start.4 = (f32[256,128]{1,0:T(8,128)S(1)}, f32[256,128]{1,0:T(8,128)S(1)}, u32[]{:S(2)}, u32[]{:S(2)}) collective-permute-start(f32[256,128]{1,0:T(8,128)S(1)} %dynamic-slice_select_fusion), channel_id=1, source_target_pairs={{0,2},{1,3},{2,0},{3,1},{4,6},{5,7},{6,4},{7,5},{8,10},{9,11},{10,... | collective-permute-start | bytes 393224 | tf_op jit(solution)/shard_map/ppermute | solution.py:229
  6.8 1.0 %constant_dynamic-slice_fusion.1 = f32[512,128]{1,0:T(8,128)S(1)} fusion(f32[1024,128]{1,0:T(8,128)} %points_ref.1, s32[]{:T(128)S(6)} %select_n.47), kind=kLoop, calls=%fused_computation.4 | loop fusion | bytes 524292 | tf_op jit(solution)/shard_map/dynamic_slice | solution.py:260
  7.7 4.4 %collective-permute-start = (f32[512,128]{1,0:T(8,128)S(1)}, f32[512,128]{1,0:T(8,128)S(1)}, u32[]{:S(2)}, u32[]{:S(2)}) collective-permute-start(f32[512,128]{1,0:T(8,128)S(1)} %constant_dynamic-slice_fusion.1), channel_id=1, source_target_pairs={{4,0},{6,8},{0,16},{2,24},{8,2},{10,10},{12,18},{14,26},{22,4},{18... | collective-permute-start | bytes 786440 | tf_op jit(solution)/shard_map/ppermute | solution.py:261
  12.1 0.0 collective-permute-done.2
  12.1 0.6 %collective-permute-done.3 = f32[256,128]{1,0:T(8,128)S(1)} collective-permute-done((f32[256,128]{1,0:T(8,128)S(1)}, f32[256,128]{1,0:T(8,128)S(1)}, u32[]{:S(2)}, u32[]{:S(2)}) %collective-permute-start.3) | collective-permute-done | bytes 131104 | tf_op jit(solution)/shard_map/ppermute | solution.py:229
  12.7 0.0 collective-permute-done.4
  12.8 0.1 collective-permute-start.5
  12.9 0.0 copy-done
  12.9 0.0 copy-done.1
  12.9 0.7 %shard_map.73 = (bf16[512,1536]{1,0:T(8,128)(2,1)S(1)}, bf16[1536,512]{1,0:T(8,128)(2,1)S(1)}, bf16[512,512]{1,0:T(8,128)(2,1)S(1)}, bf16[1024,512]{1,0:T(8,128)(2,1)S(1)}, f32[1024,1]{1,0:T(8,128)S(1)}) custom-call(f32[512,512]{1,0:T(8,128)S(1)} %copy-done.1, f32[1024,128]{1,0:T(8,128)S(1)} %copy-done, f32[1,1664]{1,0:T(1,128)S(1)} %broadcast_in_dim.3.vectors_ref), custom_call_target="tpu_custom_call" | custom-call | flops 100000000 | bytes 4000000 | tf_op jit(solution)/shard_map/pallas_call | solution.py:266
  13.6 0.6 %collective-permute-done.5.other_ref = f32[256,128]{1,0:T(8,128)S(1)} collective-permute-done((f32[256,128]{1,0:T(8,128)S(1)}, f32[256,128]{1,0:T(8,128)S(1)}, u32[]{:S(2)}, u32[]{:S(2)}) %collective-permute-start.5) | collective-permute-done | bytes 131104 | tf_op jit(solution)/shard_map/ppermute | solution.py:229
  14.2 2.5 %shard_map.74 = (bf16[1024,1536]{1,0:T(8,128)(2,1)S(1)}, bf16[512,512]{1,0:T(8,128)(2,1)S(1)}, f32[512,1]{1,0:T(8,128)S(1)}) custom-call(f32[256,128]{1,0:T(8,128)S(1)} %select_select_fusion.own_ref, f32[256,128]{1,0:T(8,128)S(1)} %collective-permute-done.5.other_ref, f32[1,1664]{1,0:T(1,128)S(1)} %broadcast_in_dim.3.vectors_ref, ...), custom_call_target="tpu_custom_call" | custom-call | flops 1 | bytes 1 | tf_op jit(solution)/shard_map/pallas_call | solution.py:278
  16.7 3.9 %collective-permute-done.sent_ref = f32[512,128]{1,0:T(8,128)S(1)} collective-permute-done((f32[512,128]{1,0:T(8,128)S(1)}, f32[512,128]{1,0:T(8,128)S(1)}, u32[]{:S(2)}, u32[]{:S(2)}) %collective-permute-start) | collective-permute-done | bytes 262176 | tf_op jit(solution)/shard_map/ppermute | solution.py:261
  20.6 4.3 %shard_map.75 = f32[1024,512]{1,0:T(8,128)} custom-call(f32[512,128]{1,0:T(8,128)S(1)} %collective-permute-done.sent_ref, f32[1,1664]{1,0:T(1,128)S(1)} %broadcast_in_dim.3.vectors_ref, bf16[512,1536]{1,0:T(8,128)(2,1)S(1)} %get-tuple-element.17.factor_left_ref, bf16[1024,512]{1,0:T(8,128)(2,1)S(1)} %get-tuple-element.18.left_ref, ...), custom_call_target="tpu_custom_call" | custom-call | flops 4000000000 | bytes 8000000 | tf_op jit(solution)/shard_map/pallas_call | solution.py:286
  (3 shorter events, 0.1 us)
Async XLA Ops:
  0.0 12.9 %copy-start = (f32[1024,128]{1,0:T(8,128)S(1)}, f32[1024,128]{1,0:T(8,128)}, u32[]{:S(2)}) copy-start(f32[1024,128]{1,0:T(8,128)} %points_ref.1) | copy-start | bytes 1572868
  0.0 12.9 %copy-start.1 = (f32[512,512]{1,0:T(8,128)S(1)}, f32[512,512]{1,0:T(8,128)}, u32[]{:S(2)}) copy-start(f32[512,512]{1,0:T(8,128)} %factor_ref.1) | copy-start | bytes 3145732
  0.0 3.1 %collective-permute-start.1 = (f32[512,128]{1,0:T(8,128)}, f32[512,128]{1,0:T(8,128)S(1)}, u32[]{:S(2)}, u32[]{:S(2)}) collective-permute-start(f32[512,128]{1,0:T(8,128)} %param.8), channel_id=1, source_target_pairs={{0,1},{1,0},{2,3},{3,2},{4,5},{5,4},{6,7},{7,6},{8,9},{9,8},{10,11... | collective-permute-start | bytes 786440 | tf_op jit(solution)/shard_map/ppermute | solution.py:229
  3.2 8.9 %collective-permute-start.2 = (f32[256,128]{1,0:T(8,128)S(1)}, f32[256,128]{1,0:T(8,128)S(1)}, u32[]{:S(2)}, u32[]{:S(2)}) collective-permute-start(f32[256,128]{1,0:T(8,128)S(1)} %dynamic-slice_select_fusion), channel_id=1, source_target_pairs={{0,6},{1,7},{2,4},{3,5},{4,2},{5,3},{6,0},{7,1},{8,14},{9,15},{10,... | collective-permute-start | bytes 393224 | tf_op jit(solution)/shard_map/ppermute | solution.py:229
  4.7 8.0 %collective-permute-start.3 = (f32[256,128]{1,0:T(8,128)S(1)}, f32[256,128]{1,0:T(8,128)S(1)}, u32[]{:S(2)}, u32[]{:S(2)}) collective-permute-start(f32[256,128]{1,0:T(8,128)S(1)} %dynamic-slice_select_fusion), channel_id=1, source_target_pairs={{0,4},{1,5},{2,6},{3,7},{4,0},{5,1},{6,2},{7,3},{8,12},{9,13},{10,... | collective-permute-start | bytes 393224 | tf_op jit(solution)/shard_map/ppermute | solution.py:229
  6.2 6.5 %collective-permute-start.4 = (f32[256,128]{1,0:T(8,128)S(1)}, f32[256,128]{1,0:T(8,128)S(1)}, u32[]{:S(2)}, u32[]{:S(2)}) collective-permute-start(f32[256,128]{1,0:T(8,128)S(1)} %dynamic-slice_select_fusion), channel_id=1, source_target_pairs={{0,2},{1,3},{2,0},{3,1},{4,6},{5,7},{6,4},{7,5},{8,10},{9,11},{10,... | collective-permute-start | bytes 393224 | tf_op jit(solution)/shard_map/ppermute | solution.py:229
  7.7 12.9 %collective-permute-start = (f32[512,128]{1,0:T(8,128)S(1)}, f32[512,128]{1,0:T(8,128)S(1)}, u32[]{:S(2)}, u32[]{:S(2)}) collective-permute-start(f32[512,128]{1,0:T(8,128)S(1)} %constant_dynamic-slice_fusion.1), channel_id=1, source_target_pairs={{4,0},{6,8},{0,16},{2,24},{8,2},{10,10},{12,18},{14,26},{22,4},{18... | collective-permute-start | bytes 786440 | tf_op jit(solution)/shard_map/ppermute | solution.py:261
  12.8 1.4 %collective-permute-start.5 = (f32[256,128]{1,0:T(8,128)S(1)}, f32[256,128]{1,0:T(8,128)S(1)}, u32[]{:S(2)}, u32[]{:S(2)}) collective-permute-start(f32[256,128]{1,0:T(8,128)S(1)} %select_select_fusion.own_ref), channel_id=1, source_target_pairs={{0,1},{1,0},{2,3},{3,2},{4,5},{5,4},{6,7},{7,6},{8,9},{9,8},{10,11... | collective-permute-start | bytes 393224 | tf_op jit(solution)/shard_map/ppermute | solution.py:229
where the time goes:
time: 25.1 us; the launch traced here: 24.9 us
  starting transfers between devices  8.02 us (32%)
  Pallas kernels  7.56 us (30%)
  waiting for transfers between devices  5.08 us (20%)
  local copies, waits for them, and re-layouts  1.9 us (8%)
  other arithmetic  1.43 us (6%)
  between operations  0.89 us (4%)
    ppermute x1, starting transfers between devices, on_device(): sent = lax.ppermute(own_half, ('row', 'col'), column_pairs(rows, cols))  4.35 us
    pallas_call x1, Pallas kernels, on_device(): pl.pallas_call(functools.partial(update_kernel, rows, cols), out_shape=sh...  4.29 us
    ppermute x1, waiting for transfers between devices, on_device(): sent = lax.ppermute(own_half, ('row', 'col'), column_pairs(rows, cols))  3.88 us
    ppermute x5, starting transfers between devices, swap(): return lax.ppermute(value, 'col', [(i, i ^ bit) for i in range(cols)])  3.67 us
    pallas_call x1, Pallas kernels, on_device(): pl.pallas_call(rows_kernel, out_shape=[shape((row_count, 3 * panel), bf16...  2.53 us
    ppermute x5, waiting for transfers between devices, swap(): return lax.ppermute(value, 'col', [(i, i ^ bit) for i in range(cols)])  1.21 us
    dynamic_slice x1, local copies, waits for them, and re-layouts, on_device(): lax.dynamic_slice_in_dim(points, col_place % halves * col_count, col_coun...  0.97 us
    dynamic_slice x1, local copies, waits for them, and re-layouts, gather_panel(): mine = lax.dynamic_slice_in_dim(panel_pool, core * half_rows, half_rows, 0)  0.92 us
  transfers between devices with their start and end apart: 6, of which 3 were waited for; matrix products, arithmetic and copies ran while one was open for 13% of the time, Pallas kernels for 13%

commit v1 on v0

--- a/solution.py
+++ b/solution.py
@@ -234,7 +234,7 @@
     core = col_place % 2
     half_rows = panel_pool.shape[0] // 2
     mine = lax.dynamic_slice_in_dim(panel_pool, core * half_rows, half_rows, 0)
-    got, mine, beside = lax.optimization_barrier((swap(panel_pool, 1, cols), mine, beside))
+    got, mine = lax.optimization_barrier((swap(panel_pool, 1, cols), mine))
     got = lax.dynamic_slice_in_dim(got, core * half_rows, half_rows, 0)
     held = jnp.where(panel_block % 2 == core, mine, got)
     apart = panel_block ^ col_place
@@ -242,8 +242,10 @@
     while low < cols:
         high = min(4 * low, cols)
         away = apart & (high - low)
-        received = [swap(held, bits, cols) for bits in range(low, high, low)]
-        for bits, value in zip(range(low, high, low), received):
+        steps = range(high - low, 0, -low)
+        received = [swap(held, bits, cols) for bits in steps]
+        received, beside = lax.optimization_barrier((received, beside))
+        for bits, value in zip(steps, received):
             held = jnp.where(away == bits, value, held)
         low = high
     return [held, swap(held, 1, cols)], beside

time: 25.1 us -> 23.7 us (0.944)
  waiting for transfers between devices: 5.08 us -> 3.66 us
    ppermute x1, waiting for transfers between devices: 3.88 us -> 3.07 us  [on_device(): sent = lax.ppermute(own_half, ('row', 'col'), column_pairs(rows, cols))]
    ppermute x5, waiting for transfers between devices: 1.21 us -> 0.59 us  [swap(): return lax.ppermute(value, 'col', [(i, i ^ bit) for i in range(cols)])]
  transfers between devices with their start and end apart: 6 -> 6, of which waited for: 3 -> 2; matrix products, arithmetic and copies ran while one was open for 13% -> 14% of each run, Pallas kernels for 13% -> 14%
where the time goes in v1:
time: 23.7 us; the launch traced here: 23.5 us
  starting transfers between devices  8 us (34%)
  Pallas kernels  7.57 us (32%)
  waiting for transfers between devices  3.66 us (15%)
  local copies, waits for them, and re-layouts  1.9 us (8%)
  other arithmetic  1.43 us (6%)
  between operations  0.91 us (4%)
    ppermute x1, starting transfers between devices, on_device(): sent = lax.ppermute(own_half, ('row', 'col'), column_pairs(rows, cols))  4.35 us
    pallas_call x1, Pallas kernels, on_device(): pl.pallas_call(functools.partial(update_kernel, rows, cols), out_shape=sh...  4.29 us
    ppermute x5, starting transfers between devices, swap(): return lax.ppermute(value, 'col', [(i, i ^ bit) for i in range(cols)])  3.65 us
    ppermute x1, waiting for transfers between devices, on_device(): sent = lax.ppermute(own_half, ('row', 'col'), column_pairs(rows, cols))  3.07 us
    pallas_call x1, Pallas kernels, on_device(): pl.pallas_call(rows_kernel, out_shape=[shape((row_count, 3 * panel), bf16...  2.54 us
    dynamic_slice x1, local copies, waits for them, and re-layouts, on_device(): lax.dynamic_slice_in_dim(points, col_place % halves * col_count, col_coun...  0.97 us
    dynamic_slice x1, local copies, waits for them, and re-layouts, gather_panel(): mine = lax.dynamic_slice_in_dim(panel_pool, core * half_rows, half_rows, 0)  0.92 us
    pallas_call x1, Pallas kernels, on_device(): pl.pallas_call(parts_kernel, out_shape=[shape((panel, 3 * panel), bf16),...  0.74 us
  transfers between devices with their start and end apart: 6, of which 2 were waited for; matrix products, arithmetic and copies ran while one was open for 14% of the time, Pallas kernels for 14%

profile of v1, /device:TPU:12, one launch (start us, length us, event | category | flops | bytes accessed | tf_op | source)
XLA Modules:
  0.0 23.5 jit_solution(14393654699415055529)
XLA Ops:
  0.0 0.0 copy-start
  0.0 0.0 copy-start.1
  0.0 0.0 collective-permute-start.1
  0.8 0.9 %constant_dynamic-slice_fusion = f32[256,128]{1,0:T(8,128)S(1)} fusion(f32[512,128]{1,0:T(8,128)} %param.8, s32[]{:T(128)S(6)} %select_n.50), kind=kLoop, calls=%fused_computation.3 | loop fusion | bytes 262148 | tf_op jit(solution)/shard_map/dynamic_slice | solution.py:236
  1.7 0.0 collective-permute-done.1
  1.8 1.5 %collective-permute-start.2 = (f32[256,128]{1,0:T(8,128)S(1)}, f32[256,128]{1,0:T(8,128)S(1)}, u32[]{:S(2)}, u32[]{:S(2)}) collective-permute-start(f32[256,128]{1,0:T(8,128)S(1)} %dynamic-slice_select_fusion), channel_id=1, source_target_pairs={{0,6},{1,7},{2,4},{3,5},{4,2},{5,3},{6,0},{7,1},{8,14},{9,15},{10,... | collective-permute-start | bytes 393224 | tf_op jit(solution)/shard_map/ppermute | solution.py:229
  3.3 1.5 %collective-permute-start.3 = (f32[256,128]{1,0:T(8,128)S(1)}, f32[256,128]{1,0:T(8,128)S(1)}, u32[]{:S(2)}, u32[]{:S(2)}) collective-permute-start(f32[256,128]{1,0:T(8,128)S(1)} %dynamic-slice_select_fusion), channel_id=1, source_target_pairs={{0,4},{1,5},{2,6},{3,7},{4,0},{5,1},{6,2},{7,3},{8,12},{9,13},{10,... | collective-permute-start | bytes 393224 | tf_op jit(solution)/shard_map/ppermute | solution.py:229
  4.8 0.5 %collective-permute-start.4 = (f32[256,128]{1,0:T(8,128)S(1)}, f32[256,128]{1,0:T(8,128)S(1)}, u32[]{:S(2)}, u32[]{:S(2)}) collective-permute-start(f32[256,128]{1,0:T(8,128)S(1)} %dynamic-slice_select_fusion), channel_id=1, source_target_pairs={{0,2},{1,3},{2,0},{3,1},{4,6},{5,7},{6,4},{7,5},{8,10},{9,11},{10,... | collective-permute-start | bytes 393224 | tf_op jit(solution)/shard_map/ppermute | solution.py:229
  5.4 1.0 %constant_dynamic-slice_fusion.1 = f32[512,128]{1,0:T(8,128)S(1)} fusion(f32[1024,128]{1,0:T(8,128)} %points_ref.1, s32[]{:T(128)S(6)} %select_n.47), kind=kLoop, calls=%fused_computation.4 | loop fusion | bytes 524292 | tf_op jit(solution)/shard_map/dynamic_slice | solution.py:262
  6.3 4.4 %collective-permute-start = (f32[512,128]{1,0:T(8,128)S(1)}, f32[512,128]{1,0:T(8,128)S(1)}, u32[]{:S(2)}, u32[]{:S(2)}) collective-permute-start(f32[512,128]{1,0:T(8,128)S(1)} %constant_dynamic-slice_fusion.1), channel_id=1, source_target_pairs={{4,0},{6,8},{0,16},{2,24},{8,2},{10,10},{12,18},{14,26},{22,4},{18... | collective-permute-start | bytes 786440 | tf_op jit(solution)/shard_map/ppermute | solution.py:263
  10.7 0.7 %convert_element_type.3 = f32[512]{0:T(512)S(1)} convert(s32[512]{0:T(512)} %param.9) | non-fusion elementwise | flops 512 | bytes 4096 | tf_op jit(solution)/shard_map/convert_element_type | solution.py:264
  11.4 0.7 %pad_maximum_fusion = f32[1664]{0:T(1024)S(1)} fusion(f32[1024]{0:T(1024)} %param.13, f32[128]{0:T(128)} %param.12, f32[512]{0:T(512)S(1)} %convert_element_type.3), kind=kLoop, calls=%fused_computation.2 | loop fusion | flops 3328 | bytes 13312 | tf_op jit(solution)/shard_map/concatenate | solution.py:264
  12.1 0.0 collective-permute-done.2
  12.1 0.0 collective-permute-done.3
  12.1 0.0 collective-permute-done.4
  12.2 0.1 collective-permute-start.5
  12.2 0.0 copy-done
  12.2 0.0 copy-done.1
  12.3 0.7 %shard_map.73 = (bf16[512,1536]{1,0:T(8,128)(2,1)S(1)}, bf16[1536,512]{1,0:T(8,128)(2,1)S(1)}, bf16[512,512]{1,0:T(8,128)(2,1)S(1)}, bf16[1024,512]{1,0:T(8,128)(2,1)S(1)}, f32[1024,1]{1,0:T(8,128)S(1)}) custom-call(f32[512,512]{1,0:T(8,128)S(1)} %copy-done.1, f32[1024,128]{1,0:T(8,128)S(1)} %copy-done, f32[1,1664]{1,0:T(1,128)S(1)} %broadcast_in_dim.3.vectors_ref), custom_call_target="tpu_custom_call" | custom-call | flops 100000000 | bytes 4000000 | tf_op jit(solution)/shard_map/pallas_call | solution.py:268
  13.0 0.6 %collective-permute-done.5.other_ref = f32[256,128]{1,0:T(8,128)S(1)} collective-permute-done((f32[256,128]{1,0:T(8,128)S(1)}, f32[256,128]{1,0:T(8,128)S(1)}, u32[]{:S(2)}, u32[]{:S(2)}) %collective-permute-start.5) | collective-permute-done | bytes 131104 | tf_op jit(solution)/shard_map/ppermute | solution.py:229
  13.6 2.5 %shard_map.74 = (bf16[1024,1536]{1,0:T(8,128)(2,1)S(1)}, bf16[512,512]{1,0:T(8,128)(2,1)S(1)}, f32[512,1]{1,0:T(8,128)S(1)}) custom-call(f32[256,128]{1,0:T(8,128)S(1)} %select_select_fusion.own_ref, f32[256,128]{1,0:T(8,128)S(1)} %collective-permute-done.5.other_ref, f32[1,1664]{1,0:T(1,128)S(1)} %broadcast_in_dim.3.vectors_ref, ...), custom_call_target="tpu_custom_call" | custom-call | flops 1 | bytes 1 | tf_op jit(solution)/shard_map/pallas_call | solution.py:280
  16.1 3.1 %collective-permute-done.sent_ref = f32[512,128]{1,0:T(8,128)S(1)} collective-permute-done((f32[512,128]{1,0:T(8,128)S(1)}, f32[512,128]{1,0:T(8,128)S(1)}, u32[]{:S(2)}, u32[]{:S(2)}) %collective-permute-start) | collective-permute-done | bytes 262176 | tf_op jit(solution)/shard_map/ppermute | solution.py:263
  19.2 4.3 %shard_map.75 = f32[1024,512]{1,0:T(8,128)} custom-call(f32[512,128]{1,0:T(8,128)S(1)} %collective-permute-done.sent_ref, f32[1,1664]{1,0:T(1,128)S(1)} %broadcast_in_dim.3.vectors_ref, bf16[512,1536]{1,0:T(8,128)(2,1)S(1)} %get-tuple-element.22.factor_left_ref, bf16[1024,512]{1,0:T(8,128)(2,1)S(1)} %get-tuple-element.23.left_ref, ...), custom_call_target="tpu_custom_call" | custom-call | flops 4000000000 | bytes 8000000 | tf_op jit(solution)/shard_map/pallas_call | solution.py:288
  (3 shorter events, 0.1 us)
Async XLA Ops:
  0.0 12.2 %copy-start = (f32[1024,128]{1,0:T(8,128)S(1)}, f32[1024,128]{1,0:T(8,128)}, u32[]{:S(2)}) copy-start(f32[1024,128]{1,0:T(8,128)} %points_ref.1) | copy-start | bytes 1572868
  0.0 12.2 %copy-start.1 = (f32[512,512]{1,0:T(8,128)S(1)}, f32[512,512]{1,0:T(8,128)}, u32[]{:S(2)}) copy-start(f32[512,512]{1,0:T(8,128)} %factor_ref.1) | copy-start | bytes 3145732
  0.0 1.7 %collective-permute-start.1 = (f32[512,128]{1,0:T(8,128)}, f32[512,128]{1,0:T(8,128)S(1)}, u32[]{:S(2)}, u32[]{:S(2)}) collective-permute-start(f32[512,128]{1,0:T(8,128)} %param.8), channel_id=1, source_target_pairs={{0,1},{1,0},{2,3},{3,2},{4,5},{5,4},{6,7},{7,6},{8,9},{9,8},{10,11... | collective-permute-start | bytes 786440 | tf_op jit(solution)/shard_map/ppermute | solution.py:229
  1.8 10.3 %collective-permute-start.2 = (f32[256,128]{1,0:T(8,128)S(1)}, f32[256,128]{1,0:T(8,128)S(1)}, u32[]{:S(2)}, u32[]{:S(2)}) collective-permute-start(f32[256,128]{1,0:T(8,128)S(1)} %dynamic-slice_select_fusion), channel_id=1, source_target_pairs={{0,6},{1,7},{2,4},{3,5},{4,2},{5,3},{6,0},{7,1},{8,14},{9,15},{10,... | collective-permute-start | bytes 393224 | tf_op jit(solution)/shard_map/ppermute | solution.py:229
  3.3 8.8 %collective-permute-start.3 = (f32[256,128]{1,0:T(8,128)S(1)}, f32[256,128]{1,0:T(8,128)S(1)}, u32[]{:S(2)}, u32[]{:S(2)}) collective-permute-start(f32[256,128]{1,0:T(8,128)S(1)} %dynamic-slice_select_fusion), channel_id=1, source_target_pairs={{0,4},{1,5},{2,6},{3,7},{4,0},{5,1},{6,2},{7,3},{8,12},{9,13},{10,... | collective-permute-start | bytes 393224 | tf_op jit(solution)/shard_map/ppermute | solution.py:229
  4.8 7.3 %collective-permute-start.4 = (f32[256,128]{1,0:T(8,128)S(1)}, f32[256,128]{1,0:T(8,128)S(1)}, u32[]{:S(2)}, u32[]{:S(2)}) collective-permute-start(f32[256,128]{1,0:T(8,128)S(1)} %dynamic-slice_select_fusion), channel_id=1, source_target_pairs={{0,2},{1,3},{2,0},{3,1},{4,6},{5,7},{6,4},{7,5},{8,10},{9,11},{10,... | collective-permute-start | bytes 393224 | tf_op jit(solution)/shard_map/ppermute | solution.py:229
  6.3 12.9 %collective-permute-start = (f32[512,128]{1,0:T(8,128)S(1)}, f32[512,128]{1,0:T(8,128)S(1)}, u32[]{:S(2)}, u32[]{:S(2)}) collective-permute-start(f32[512,128]{1,0:T(8,128)S(1)} %constant_dynamic-slice_fusion.1), channel_id=1, source_target_pairs={{4,0},{6,8},{0,16},{2,24},{8,2},{10,10},{12,18},{14,26},{22,4},{18... | collective-permute-start | bytes 786440 | tf_op jit(solution)/shard_map/ppermute | solution.py:263
  12.2 1.4 %collective-permute-start.5 = (f32[256,128]{1,0:T(8,128)S(1)}, f32[256,128]{1,0:T(8,128)S(1)}, u32[]{:S(2)}, u32[]{:S(2)}) collective-permute-start(f32[256,128]{1,0:T(8,128)S(1)} %select_select_fusion.own_ref), channel_id=1, source_target_pairs={{0,1},{1,0},{2,3},{3,2},{4,5},{5,4},{6,7},{7,6},{8,9},{9,8},{10,11... | collective-permute-start | bytes 393224 | tf_op jit(solution)/shard_map/ppermute | solution.py:229

commit v2 on v1

--- a/solution.py
+++ b/solution.py
@@ -218,7 +218,7 @@
     halves = cols // rows
     places = source_places(rows, halves)
     return [
-        (g * cols + places[h, g][r] * halves + h, r * cols + g * halves + h)
+        (g * cols + places[h, g][r] * halves + h, r * cols + g * halves + halves - 1 - h)
         for h in range(halves)
         for g in range(rows)
         for r in range(rows)
@@ -259,7 +259,8 @@
     col_count = row_count * rows // cols
     halves = cols // rows
     col_place = lax.axis_index("col")
-    own_half = lax.dynamic_slice_in_dim(points, col_place % halves * col_count, col_count, 0)
+    part = halves - 1 - col_place % halves
+    own_half = lax.dynamic_slice_in_dim(points, part * col_count, col_count, 0)
     sent = lax.ppermute(own_half, ("row", "col"), column_pairs(rows, cols))
     vectors = jnp.concatenate([order.astype(f32), ard_weights, noise])[None, :]
     pieces, vectors = gather_panel(panel_pool, panel_index[0], cols, vectors)

time: 23.7 us -> 23 us (0.970)
  the two profiles are of different devices: /device:TPU:12 before, /device:TPU:29 now
where the time goes in v2:
time: 23 us; the launch traced here: 22.7 us
  Pallas kernels  7.57 us (33%)
  starting transfers between devices  5.73 us (25%)
  waiting for transfers between devices  5.38 us (23%)
  local copies, waits for them, and re-layouts  1.9 us (8%)
  other arithmetic  1.42 us (6%)
  between operations  0.75 us (3%)
    ppermute x5, waiting for transfers between devices, swap(): return lax.ppermute(value, 'col', [(i, i ^ bit) for i in range(cols)])  5.37 us
    pallas_call x1, Pallas kernels, on_device(): pl.pallas_call(functools.partial(update_kernel, rows, cols), out_shape=sh...  4.29 us
    ppermute x5, starting transfers between devices, swap(): return lax.ppermute(value, 'col', [(i, i ^ bit) for i in range(cols)])  3.94 us
    pallas_call x1, Pallas kernels, on_device(): pl.pallas_call(rows_kernel, out_shape=[shape((row_count, 3 * panel), bf16...  2.53 us
    ppermute x1, starting transfers between devices, on_device(): sent = lax.ppermute(own_half, ('row', 'col'), column_pairs(rows, cols))  1.79 us
    dynamic_slice x1, local copies, waits for them, and re-layouts, on_device(): own_half = lax.dynamic_slice_in_dim(points, part * col_count, col_count, 0)  0.97 us
    dynamic_slice x1, local copies, waits for them, and re-layouts, gather_panel(): mine = lax.dynamic_slice_in_dim(panel_pool, core * half_rows, half_rows, 0)  0.92 us
    pallas_call x1, Pallas kernels, on_device(): pl.pallas_call(parts_kernel, out_shape=[shape((panel, 3 * panel), bf16),...  0.74 us
  transfers between devices with their start and end apart: 6, of which 2 were waited for; matrix products, arithmetic and copies ran while one was open for 15% of the time, Pallas kernels for 14%

profile of v2, /device:TPU:29, one launch (start us, length us, event | category | flops | bytes accessed | tf_op | source)
XLA Modules:
  0.0 22.7 jit_solution(6454884866318004362)
XLA Ops:
  0.0 0.0 copy-start
  0.0 0.0 copy-start.1
  0.0 0.7 %collective-permute-start.1 = (f32[512,128]{1,0:T(8,128)}, f32[512,128]{1,0:T(8,128)S(1)}, u32[]{:S(2)}, u32[]{:S(2)}) collective-permute-start(f32[512,128]{1,0:T(8,128)} %param.8), channel_id=1, source_target_pairs={{0,1},{1,0},{2,3},{3,2},{4,5},{5,4},{6,7},{7,6},{8,9},{9,8},{10,11... | collective-permute-start | bytes 786440 | tf_op jit(solution)/shard_map/ppermute | solution.py:229
  1.4 0.9 %constant_dynamic-slice_fusion = f32[256,128]{1,0:T(8,128)S(1)} fusion(f32[512,128]{1,0:T(8,128)} %param.8, s32[]{:T(128)S(6)} %select_n.50), kind=kLoop, calls=%fused_computation.3 | loop fusion | bytes 262148 | tf_op jit(solution)/shard_map/dynamic_slice | solution.py:236
  2.3 0.0 collective-permute-done.1
  2.3 1.2 %collective-permute-start.2 = (f32[256,128]{1,0:T(8,128)S(1)}, f32[256,128]{1,0:T(8,128)S(1)}, u32[]{:S(2)}, u32[]{:S(2)}) collective-permute-start(f32[256,128]{1,0:T(8,128)S(1)} %dynamic-slice_select_fusion), channel_id=1, source_target_pairs={{0,6},{1,7},{2,4},{3,5},{4,2},{5,3},{6,0},{7,1},{8,14},{9,15},{10,... | collective-permute-start | bytes 393224 | tf_op jit(solution)/shard_map/ppermute | solution.py:229
  3.5 1.2 %collective-permute-start.3 = (f32[256,128]{1,0:T(8,128)S(1)}, f32[256,128]{1,0:T(8,128)S(1)}, u32[]{:S(2)}, u32[]{:S(2)}) collective-permute-start(f32[256,128]{1,0:T(8,128)S(1)} %dynamic-slice_select_fusion), channel_id=1, source_target_pairs={{0,4},{1,5},{2,6},{3,7},{4,0},{5,1},{6,2},{7,3},{8,12},{9,13},{10,... | collective-permute-start | bytes 393224 | tf_op jit(solution)/shard_map/ppermute | solution.py:229
  4.8 0.3 %collective-permute-start.4 = (f32[256,128]{1,0:T(8,128)S(1)}, f32[256,128]{1,0:T(8,128)S(1)}, u32[]{:S(2)}, u32[]{:S(2)}) collective-permute-start(f32[256,128]{1,0:T(8,128)S(1)} %dynamic-slice_select_fusion), channel_id=1, source_target_pairs={{0,2},{1,3},{2,0},{3,1},{4,6},{5,7},{6,4},{7,5},{8,10},{9,11},{10,... | collective-permute-start | bytes 393224 | tf_op jit(solution)/shard_map/ppermute | solution.py:229
  5.0 1.0 %constant_dynamic-slice_fusion.1 = f32[512,128]{1,0:T(8,128)S(1)} fusion(f32[1024,128]{1,0:T(8,128)} %points_ref.1, s32[]{:T(128)S(6)} %select_n.47), kind=kLoop, calls=%fused_computation.4 | loop fusion | bytes 524292 | tf_op jit(solution)/shard_map/dynamic_slice | solution.py:263
  6.0 1.8 %collective-permute-start = (f32[512,128]{1,0:T(8,128)S(1)}, f32[512,128]{1,0:T(8,128)S(1)}, u32[]{:S(2)}, u32[]{:S(2)}) collective-permute-start(f32[512,128]{1,0:T(8,128)S(1)} %constant_dynamic-slice_fusion.1), channel_id=1, source_target_pairs={{4,1},{6,9},{0,17},{2,25},{8,3},{10,11},{12,19},{14,27},{22,5},{18... | collective-permute-start | bytes 786440 | tf_op jit(solution)/shard_map/ppermute | solution.py:264
  7.8 0.7 %convert_element_type.3 = f32[512]{0:T(512)S(1)} convert(s32[512]{0:T(512)} %param.9) | non-fusion elementwise | flops 512 | bytes 4096 | tf_op jit(solution)/shard_map/convert_element_type | solution.py:265
  8.5 0.7 %pad_maximum_fusion = f32[1664]{0:T(1024)S(1)} fusion(f32[1024]{0:T(1024)} %param.13, f32[128]{0:T(128)} %param.12, f32[512]{0:T(512)S(1)} %convert_element_type.3), kind=kLoop, calls=%fused_computation.2 | loop fusion | flops 3328 | bytes 13312 | tf_op jit(solution)/shard_map/concatenate | solution.py:265
  9.2 0.0 collective-permute-done.2
  9.2 5.1 %collective-permute-done.3 = f32[256,128]{1,0:T(8,128)S(1)} collective-permute-done((f32[256,128]{1,0:T(8,128)S(1)}, f32[256,128]{1,0:T(8,128)S(1)}, u32[]{:S(2)}, u32[]{:S(2)}) %collective-permute-start.3) | collective-permute-done | bytes 131104 | tf_op jit(solution)/shard_map/ppermute | solution.py:229
  14.3 0.0 collective-permute-done.4
  14.4 0.5 %collective-permute-start.5 = (f32[256,128]{1,0:T(8,128)S(1)}, f32[256,128]{1,0:T(8,128)S(1)}, u32[]{:S(2)}, u32[]{:S(2)}) collective-permute-start(f32[256,128]{1,0:T(8,128)S(1)} %select_select_fusion.own_ref), channel_id=1, source_target_pairs={{0,1},{1,0},{2,3},{3,2},{4,5},{5,4},{6,7},{7,6},{8,9},{9,8},{10,11... | collective-permute-start | bytes 393224 | tf_op jit(solution)/shard_map/ppermute | solution.py:229
  14.9 0.0 copy-done
  14.9 0.0 copy-done.1
  14.9 0.7 %shard_map.73 = (bf16[512,1536]{1,0:T(8,128)(2,1)S(1)}, bf16[1536,512]{1,0:T(8,128)(2,1)S(1)}, bf16[512,512]{1,0:T(8,128)(2,1)S(1)}, bf16[1024,512]{1,0:T(8,128)(2,1)S(1)}, f32[1024,1]{1,0:T(8,128)S(1)}) custom-call(f32[512,512]{1,0:T(8,128)S(1)} %copy-done.1, f32[1024,128]{1,0:T(8,128)S(1)} %copy-done, f32[1,1664]{1,0:T(1,128)S(1)} %broadcast_in_dim.3.vectors_ref), custom_call_target="tpu_custom_call" | custom-call | flops 100000000 | bytes 4000000 | tf_op jit(solution)/shard_map/pallas_call | solution.py:269
  15.7 0.2 %collective-permute-done.5.other_ref = f32[256,128]{1,0:T(8,128)S(1)} collective-permute-done((f32[256,128]{1,0:T(8,128)S(1)}, f32[256,128]{1,0:T(8,128)S(1)}, u32[]{:S(2)}, u32[]{:S(2)}) %collective-permute-start.5) | collective-permute-done | bytes 131104 | tf_op jit(solution)/shard_map/ppermute | solution.py:229
  15.9 2.5 %shard_map.74 = (bf16[1024,1536]{1,0:T(8,128)(2,1)S(1)}, bf16[512,512]{1,0:T(8,128)(2,1)S(1)}, f32[512,1]{1,0:T(8,128)S(1)}) custom-call(f32[256,128]{1,0:T(8,128)S(1)} %select_select_fusion.own_ref, f32[256,128]{1,0:T(8,128)S(1)} %collective-permute-done.5.other_ref, f32[1,1664]{1,0:T(1,128)S(1)} %broadcast_in_dim.3.vectors_ref, ...), custom_call_target="tpu_custom_call" | custom-call | flops 1 | bytes 1 | tf_op jit(solution)/shard_map/pallas_call | solution.py:281
  18.4 0.0 collective-permute-done.sent_ref
  18.5 4.3 %shard_map.75 = f32[1024,512]{1,0:T(8,128)} custom-call(f32[512,128]{1,0:T(8,128)S(1)} %collective-permute-done.sent_ref, f32[1,1664]{1,0:T(1,128)S(1)} %broadcast_in_dim.3.vectors_ref, bf16[512,1536]{1,0:T(8,128)(2,1)S(1)} %get-tuple-element.22.factor_left_ref, bf16[1024,512]{1,0:T(8,128)(2,1)S(1)} %get-tuple-element.23.left_ref, ...), custom_call_target="tpu_custom_call" | custom-call | flops 4000000000 | bytes 8000000 | tf_op jit(solution)/shard_map/pallas_call | solution.py:289
  (3 shorter events, 0.1 us)
Async XLA Ops:
  0.0 14.9 %copy-start = (f32[1024,128]{1,0:T(8,128)S(1)}, f32[1024,128]{1,0:T(8,128)}, u32[]{:S(2)}) copy-start(f32[1024,128]{1,0:T(8,128)} %points_ref.1) | copy-start | bytes 1572868
  0.0 14.9 %copy-start.1 = (f32[512,512]{1,0:T(8,128)S(1)}, f32[512,512]{1,0:T(8,128)}, u32[]{:S(2)}) copy-start(f32[512,512]{1,0:T(8,128)} %factor_ref.1) | copy-start | bytes 3145732
  0.0 2.3 %collective-permute-start.1 = (f32[512,128]{1,0:T(8,128)}, f32[512,128]{1,0:T(8,128)S(1)}, u32[]{:S(2)}, u32[]{:S(2)}) collective-permute-start(f32[512,128]{1,0:T(8,128)} %param.8), channel_id=1, source_target_pairs={{0,1},{1,0},{2,3},{3,2},{4,5},{5,4},{6,7},{7,6},{8,9},{9,8},{10,11... | collective-permute-start | bytes 786440 | tf_op jit(solution)/shard_map/ppermute | solution.py:229
  2.3 6.9 %collective-permute-start.2 = (f32[256,128]{1,0:T(8,128)S(1)}, f32[256,128]{1,0:T(8,128)S(1)}, u32[]{:S(2)}, u32[]{:S(2)}) collective-permute-start(f32[256,128]{1,0:T(8,128)S(1)} %dynamic-slice_select_fusion), channel_id=1, source_target_pairs={{0,6},{1,7},{2,4},{3,5},{4,2},{5,3},{6,0},{7,1},{8,14},{9,15},{10,... | collective-permute-start | bytes 393224 | tf_op jit(solution)/shard_map/ppermute | solution.py:229
  3.5 10.8 %collective-permute-start.3 = (f32[256,128]{1,0:T(8,128)S(1)}, f32[256,128]{1,0:T(8,128)S(1)}, u32[]{:S(2)}, u32[]{:S(2)}) collective-permute-start(f32[256,128]{1,0:T(8,128)S(1)} %dynamic-slice_select_fusion), channel_id=1, source_target_pairs={{0,4},{1,5},{2,6},{3,7},{4,0},{5,1},{6,2},{7,3},{8,12},{9,13},{10,... | collective-permute-start | bytes 393224 | tf_op jit(solution)/shard_map/ppermute | solution.py:229
  4.8 9.6 %collective-permute-start.4 = (f32[256,128]{1,0:T(8,128)S(1)}, f32[256,128]{1,0:T(8,128)S(1)}, u32[]{:S(2)}, u32[]{:S(2)}) collective-permute-start(f32[256,128]{1,0:T(8,128)S(1)} %dynamic-slice_select_fusion), channel_id=1, source_target_pairs={{0,2},{1,3},{2,0},{3,1},{4,6},{5,7},{6,4},{7,5},{8,10},{9,11},{10,... | collective-permute-start | bytes 393224 | tf_op jit(solution)/shard_map/ppermute | solution.py:229
  6.0 12.4 %collective-permute-start = (f32[512,128]{1,0:T(8,128)S(1)}, f32[512,128]{1,0:T(8,128)S(1)}, u32[]{:S(2)}, u32[]{:S(2)}) collective-permute-start(f32[512,128]{1,0:T(8,128)S(1)} %constant_dynamic-slice_fusion.1), channel_id=1, source_target_pairs={{4,1},{6,9},{0,17},{2,25},{8,3},{10,11},{12,19},{14,27},{22,5},{18... | collective-permute-start | bytes 786440 | tf_op jit(solution)/shard_map/ppermute | solution.py:264
  14.4 1.5 %collective-permute-start.5 = (f32[256,128]{1,0:T(8,128)S(1)}, f32[256,128]{1,0:T(8,128)S(1)}, u32[]{:S(2)}, u32[]{:S(2)}) collective-permute-start(f32[256,128]{1,0:T(8,128)S(1)} %select_select_fusion.own_ref), channel_id=1, source_target_pairs={{0,1},{1,0},{2,3},{3,2},{4,5},{5,4},{6,7},{7,6},{8,9},{9,8},{10,11... | collective-permute-start | bytes 393224 | tf_op jit(solution)/shard_map/ppermute | solution.py:229

commit v3 on v2

--- a/solution.py
+++ b/solution.py
@@ -111,7 +111,7 @@
 
 
 def update_kernel(
-    rows, cols, sent_ref, vectors_ref, factor_left_ref, left_ref, left_half_ref, rows_ref, chosen_ref,
+    rows, cols, sent_ref, points_ref, vectors_ref, factor_left_ref, left_ref, left_half_ref, rows_ref, chosen_ref,
     chosen_half_ref, out_ref, block_ref, kern_ref, cols_ref, sems,
 ):
     row_place, col_place = lax.axis_index("row"), lax.axis_index("col")
@@ -121,7 +121,9 @@
     own = row_place == col_place // halves
     panel, features = factor_left_ref.shape[0], sent_ref.shape[1]
 
-    high, low = halves_of(jnp.transpose(sent_ref[...] * scale_of(vectors_ref, panel, features)))
+    own_points = points_ref[pl.ds(pl.multiple_of(part * count, count), count), :]
+    col_points = jnp.where(own, own_points, sent_ref[...])
+    high, low = halves_of(jnp.transpose(col_points * scale_of(vectors_ref, panel, features)))
     right = pack_right(high, low)
     right_half = half_square(high, low, 0)
     chunks, chunk = block_ref.shape[:2]
@@ -175,13 +177,15 @@
 
 
 def source_places(rows, halves):
-    draw = random.Random(5)
+    draw = random.Random(0)
     across = math.isqrt(rows)
     places = {}
     load = collections.Counter()
 
     def move(key, r, sign):
         change = 0
+        if r == key[1]:
+            return change
         for link in links_of(places[key][r], key[1], r, across):
             old = load[link]
             load[link] = old + sign
@@ -222,6 +226,7 @@
         for h in range(halves)
         for g in range(rows)
         for r in range(rows)
+        if r != g
     ]
 
 
@@ -297,7 +302,7 @@
             pltpu.SemaphoreType.DMA((chunks,)),
         ],
         **compute_params(4 * 10**9, 8 * 10**6),
-    )(sent, vectors, factor_left, left, left_half, rows_left, chosen, chosen_half)
+    )(sent, points, vectors, factor_left, left, left_half, rows_left, chosen, chosen_half)
 
 
 def solution(mesh):

time: 23 us -> 23.4 us (1.017)
  the two profiles are of different devices: /device:TPU:29 before, /device:TPU:7 now
where the time goes in v3:
time: 23.4 us; the launch traced here: 23.2 us
  Pallas kernels  7.57 us (32%)
  starting transfers between devices  7.45 us (32%)
  waiting for transfers between devices  4.02 us (17%)
  local copies, waits for them, and re-layouts  1.9 us (8%)
  other arithmetic  1.43 us (6%)
  between operations  0.81 us (3%)
    pallas_call x1, Pallas kernels, on_device(): pl.pallas_call(functools.partial(update_kernel, rows, cols), out_shape=sh...  4.29 us
    ppermute x1, starting transfers between devices, on_device(): sent = lax.ppermute(own_half, ('row', 'col'), column_pairs(rows, cols))  3.99 us
    ppermute x5, starting transfers between devices, swap(): return lax.ppermute(value, 'col', [(i, i ^ bit) for i in range(cols)])  3.45 us
    ppermute x1, waiting for transfers between devices, on_device(): sent = lax.ppermute(own_half, ('row', 'col'), column_pairs(rows, cols))  3.44 us
    pallas_call x1, Pallas kernels, on_device(): pl.pallas_call(rows_kernel, out_shape=[shape((row_count, 3 * panel), bf16...  2.53 us
    dynamic_slice x1, local copies, waits for them, and re-layouts, on_device(): own_half = lax.dynamic_slice_in_dim(points, part * col_count, col_count, 0)  0.97 us
    dynamic_slice x1, local copies, waits for them, and re-layouts, gather_panel(): mine = lax.dynamic_slice_in_dim(panel_pool, core * half_rows, half_rows, 0)  0.92 us
    pallas_call x1, Pallas kernels, on_device(): pl.pallas_call(parts_kernel, out_shape=[shape((panel, 3 * panel), bf16),...  0.74 us
  transfers between devices with their start and end apart: 6, of which 2 were waited for; matrix products, arithmetic and copies ran while one was open for 14% of the time, Pallas kernels for 14%

profile of v3, /device:TPU:7, one launch (start us, length us, event | category | flops | bytes accessed | tf_op | source)
XLA Modules:
  0.0 23.2 jit_solution(16733360555046014691)
XLA Ops:
  0.0 0.0 copy-start
  0.0 0.0 copy-start.1
  0.0 0.7 %collective-permute-start.1 = (f32[512,128]{1,0:T(8,128)}, f32[512,128]{1,0:T(8,128)S(1)}, u32[]{:S(2)}, u32[]{:S(2)}) collective-permute-start(f32[512,128]{1,0:T(8,128)} %param.8), channel_id=1, source_target_pairs={{0,1},{1,0},{2,3},{3,2},{4,5},{5,4},{6,7},{7,6},{8,9},{9,8},{10,11... | collective-permute-start | bytes 786440 | tf_op jit(solution)/shard_map/ppermute | solution.py:234
  1.4 0.9 %constant_dynamic-slice_fusion = f32[256,128]{1,0:T(8,128)S(1)} fusion(f32[512,128]{1,0:T(8,128)} %param.8, s32[]{:T(128)S(6)} %select_n.50), kind=kLoop, calls=%fused_computation.3 | loop fusion | bytes 262148 | tf_op jit(solution)/shard_map/dynamic_slice | solution.py:241
  2.3 0.0 collective-permute-done.1
  2.3 0.1 collective-permute-start.2
  2.4 1.4 %collective-permute-start.3 = (f32[256,128]{1,0:T(8,128)S(1)}, f32[256,128]{1,0:T(8,128)S(1)}, u32[]{:S(2)}, u32[]{:S(2)}) collective-permute-start(f32[256,128]{1,0:T(8,128)S(1)} %dynamic-slice_select_fusion), channel_id=1, source_target_pairs={{0,4},{1,5},{2,6},{3,7},{4,0},{5,1},{6,2},{7,3},{8,12},{9,13},{10,... | collective-permute-start | bytes 393224 | tf_op jit(solution)/shard_map/ppermute | solution.py:234
  3.8 1.2 %collective-permute-start.4 = (f32[256,128]{1,0:T(8,128)S(1)}, f32[256,128]{1,0:T(8,128)S(1)}, u32[]{:S(2)}, u32[]{:S(2)}) collective-permute-start(f32[256,128]{1,0:T(8,128)S(1)} %dynamic-slice_select_fusion), channel_id=1, source_target_pairs={{0,2},{1,3},{2,0},{3,1},{4,6},{5,7},{6,4},{7,5},{8,10},{9,11},{10,... | collective-permute-start | bytes 393224 | tf_op jit(solution)/shard_map/ppermute | solution.py:234
  5.0 1.0 %constant_dynamic-slice_fusion.1 = f32[512,128]{1,0:T(8,128)S(1)} fusion(f32[1024,128]{1,0:T(8,128)} %points_ref.3, s32[]{:T(128)S(6)} %select_n.47), kind=kLoop, calls=%fused_computation.4 | loop fusion | bytes 524292 | tf_op jit(solution)/shard_map/dynamic_slice | solution.py:268
  6.0 4.0 %collective-permute-start = (f32[512,128]{1,0:T(8,128)S(1)}, f32[512,128]{1,0:T(8,128)S(1)}, u32[]{:S(2)}, u32[]{:S(2)}) collective-permute-start(f32[512,128]{1,0:T(8,128)S(1)} %constant_dynamic-slice_fusion.1), channel_id=1, source_target_pairs={{2,9},{0,17},{4,25},{8,3},{10,19},{14,27},{22,5},{16,13},{20,29},{... | collective-permute-start | bytes 786440 | tf_op jit(solution)/shard_map/ppermute | solution.py:269
  10.0 0.7 %convert_element_type.3 = f32[512]{0:T(512)S(1)} convert(s32[512]{0:T(512)} %param.9) | non-fusion elementwise | flops 512 | bytes 4096 | tf_op jit(solution)/shard_map/convert_element_type | solution.py:270
  10.7 0.7 %pad_maximum_fusion = f32[1664]{0:T(1024)S(1)} fusion(f32[1024]{0:T(1024)} %param.13, f32[128]{0:T(128)} %param.12, f32[512]{0:T(512)S(1)} %convert_element_type.3), kind=kLoop, calls=%fused_computation.2 | loop fusion | flops 3328 | bytes 13312 | tf_op jit(solution)/shard_map/concatenate | solution.py:270
  11.4 0.0 collective-permute-done.2
  11.4 0.0 collective-permute-done.3
  11.4 0.0 collective-permute-done.4
  11.5 0.1 collective-permute-start.5
  11.6 0.0 copy-done
  11.6 0.0 copy-done.1
  11.6 0.7 %shard_map.73 = (bf16[512,1536]{1,0:T(8,128)(2,1)S(1)}, bf16[1536,512]{1,0:T(8,128)(2,1)S(1)}, bf16[512,512]{1,0:T(8,128)(2,1)S(1)}, bf16[1024,512]{1,0:T(8,128)(2,1)S(1)}, f32[1024,1]{1,0:T(8,128)S(1)}) custom-call(f32[512,512]{1,0:T(8,128)S(1)} %copy-done.1, f32[1024,128]{1,0:T(8,128)S(1)} %copy-done, f32[1,1664]{1,0:T(1,128)S(1)} %broadcast_in_dim.3.vectors_ref), custom_call_target="tpu_custom_call" | custom-call | flops 100000000 | bytes 4000000 | tf_op jit(solution)/shard_map/pallas_call | solution.py:274
  12.3 0.6 %collective-permute-done.5.other_ref = f32[256,128]{1,0:T(8,128)S(1)} collective-permute-done((f32[256,128]{1,0:T(8,128)S(1)}, f32[256,128]{1,0:T(8,128)S(1)}, u32[]{:S(2)}, u32[]{:S(2)}) %collective-permute-start.5) | collective-permute-done | bytes 131104 | tf_op jit(solution)/shard_map/ppermute | solution.py:234
  12.9 2.5 %shard_map.74 = (bf16[1024,1536]{1,0:T(8,128)(2,1)S(1)}, bf16[512,512]{1,0:T(8,128)(2,1)S(1)}, f32[512,1]{1,0:T(8,128)S(1)}) custom-call(f32[256,128]{1,0:T(8,128)S(1)} %select_select_fusion.own_ref, f32[256,128]{1,0:T(8,128)S(1)} %collective-permute-done.5.other_ref, f32[1,1664]{1,0:T(1,128)S(1)} %broadcast_in_dim.3.vectors_ref, ...), custom_call_target="tpu_custom_call" | custom-call | flops 1 | bytes 1 | tf_op jit(solution)/shard_map/pallas_call | solution.py:286
  15.4 3.4 %collective-permute-done.sent_ref = f32[512,128]{1,0:T(8,128)S(1)} collective-permute-done((f32[512,128]{1,0:T(8,128)S(1)}, f32[512,128]{1,0:T(8,128)S(1)}, u32[]{:S(2)}, u32[]{:S(2)}) %collective-permute-start) | collective-permute-done | bytes 262176 | tf_op jit(solution)/shard_map/ppermute | solution.py:269
  18.9 4.3 %shard_map.75 = f32[1024,512]{1,0:T(8,128)} custom-call(f32[512,128]{1,0:T(8,128)S(1)} %collective-permute-done.sent_ref, f32[1024,128]{1,0:T(8,128)S(1)} %copy-done, f32[1,1664]{1,0:T(1,128)S(1)} %broadcast_in_dim.3.vectors_ref, bf16[512,1536]{1,0:T(8,128)(2,1)S(1)} %get-tuple-element.22.factor_left_ref, bf16[1024,512]{1,0:T(8,128)(2,1)S(1)} %get-tuple-element.23.left_ref, ...), custom_call_target="tpu_custom_call" | custom-call | flops 4000000000 | bytes 8000000 | tf_op jit(solution)/shard_map/pallas_call | solution.py:294
  (3 shorter events, 0.1 us)
Async XLA Ops:
  0.0 11.6 %copy-start = (f32[1024,128]{1,0:T(8,128)S(1)}, f32[1024,128]{1,0:T(8,128)}, u32[]{:S(2)}) copy-start(f32[1024,128]{1,0:T(8,128)} %points_ref.3) | copy-start | bytes 1572868
  0.0 11.6 %copy-start.1 = (f32[512,512]{1,0:T(8,128)S(1)}, f32[512,512]{1,0:T(8,128)}, u32[]{:S(2)}) copy-start(f32[512,512]{1,0:T(8,128)} %factor_ref.1) | copy-start | bytes 3145732
  0.0 2.3 %collective-permute-start.1 = (f32[512,128]{1,0:T(8,128)}, f32[512,128]{1,0:T(8,128)S(1)}, u32[]{:S(2)}, u32[]{:S(2)}) collective-permute-start(f32[512,128]{1,0:T(8,128)} %param.8), channel_id=1, source_target_pairs={{0,1},{1,0},{2,3},{3,2},{4,5},{5,4},{6,7},{7,6},{8,9},{9,8},{10,11... | collective-permute-start | bytes 786440 | tf_op jit(solution)/shard_map/ppermute | solution.py:234
  2.3 9.1 %collective-permute-start.2 = (f32[256,128]{1,0:T(8,128)S(1)}, f32[256,128]{1,0:T(8,128)S(1)}, u32[]{:S(2)}, u32[]{:S(2)}) collective-permute-start(f32[256,128]{1,0:T(8,128)S(1)} %dynamic-slice_select_fusion), channel_id=1, source_target_pairs={{0,6},{1,7},{2,4},{3,5},{4,2},{5,3},{6,0},{7,1},{8,14},{9,15},{10,... | collective-permute-start | bytes 393224 | tf_op jit(solution)/shard_map/ppermute | solution.py:234
  2.4 9.0 %collective-permute-start.3 = (f32[256,128]{1,0:T(8,128)S(1)}, f32[256,128]{1,0:T(8,128)S(1)}, u32[]{:S(2)}, u32[]{:S(2)}) collective-permute-start(f32[256,128]{1,0:T(8,128)S(1)} %dynamic-slice_select_fusion), channel_id=1, source_target_pairs={{0,4},{1,5},{2,6},{3,7},{4,0},{5,1},{6,2},{7,3},{8,12},{9,13},{10,... | collective-permute-start | bytes 393224 | tf_op jit(solution)/shard_map/ppermute | solution.py:234
  3.8 7.6 %collective-permute-start.4 = (f32[256,128]{1,0:T(8,128)S(1)}, f32[256,128]{1,0:T(8,128)S(1)}, u32[]{:S(2)}, u32[]{:S(2)}) collective-permute-start(f32[256,128]{1,0:T(8,128)S(1)} %dynamic-slice_select_fusion), channel_id=1, source_target_pairs={{0,2},{1,3},{2,0},{3,1},{4,6},{5,7},{6,4},{7,5},{8,10},{9,11},{10,... | collective-permute-start | bytes 393224 | tf_op jit(solution)/shard_map/ppermute | solution.py:234
  6.0 12.9 %collective-permute-start = (f32[512,128]{1,0:T(8,128)S(1)}, f32[512,128]{1,0:T(8,128)S(1)}, u32[]{:S(2)}, u32[]{:S(2)}) collective-permute-start(f32[512,128]{1,0:T(8,128)S(1)} %constant_dynamic-slice_fusion.1), channel_id=1, source_target_pairs={{2,9},{0,17},{4,25},{8,3},{10,19},{14,27},{22,5},{16,13},{20,29},{... | collective-permute-start | bytes 786440 | tf_op jit(solution)/shard_map/ppermute | solution.py:269
  11.5 1.4 %collective-permute-start.5 = (f32[256,128]{1,0:T(8,128)S(1)}, f32[256,128]{1,0:T(8,128)S(1)}, u32[]{:S(2)}, u32[]{:S(2)}) collective-permute-start(f32[256,128]{1,0:T(8,128)S(1)} %select_select_fusion.own_ref), channel_id=1, source_target_pairs={{0,1},{1,0},{2,3},{3,2},{4,5},{5,4},{6,7},{7,6},{8,9},{9,8},{10,11... | collective-permute-start | bytes 393224 | tf_op jit(solution)/shard_map/ppermute | solution.py:234

commit v4 on v2

--- a/solution.py
+++ b/solution.py
@@ -61,12 +61,12 @@
     return jnp.exp2((crossed - left_half) - (right_half - 1.0))
 
 
-def scale_of(vectors_ref, panel, features):
-    return jnp.sqrt(vectors_ref[:, panel : panel + features] * log2_e)
+def scale_of(vectors_ref, features):
+    return jnp.sqrt(vectors_ref[:, :features] * log2_e)
 
 
 def parts_kernel(
-    factor_ref, points_ref, vectors_ref, factor_left_ref, factor_right_ref, pick_ref, left_ref,
+    factor_ref, order_ref, points_ref, vectors_ref, factor_left_ref, factor_right_ref, pick_ref, left_ref,
     left_half_ref,
 ):
     factor = factor_ref[...]
@@ -75,10 +75,10 @@
     panel = factor.shape[0]
     core = lax.axis_index("col") % 2
     place = lax.broadcasted_iota(jnp.int32, (panel, panel), 0) + core * (panel // 2)
-    place = jnp.where(place >= panel, place - panel, place).astype(f32)
-    hit = jnp.where(place == vectors_ref[:, :panel], 1.0, 0.0).astype(f32)
+    place = jnp.where(place >= panel, place - panel, place)
+    hit = jnp.where(place == order_ref[...], 1.0, 0.0).astype(f32)
     pick_ref[...] = jnp.transpose(hit).astype(bf16)
-    high, low = halves_of(points_ref[...] * scale_of(vectors_ref, panel, points_ref.shape[1]))
+    high, low = halves_of(points_ref[...] * scale_of(vectors_ref, points_ref.shape[1]))
     left_ref[...] = pack_left(high, low)
     left_half_ref[...] = half_square(high, low, 1)
 
@@ -89,7 +89,7 @@
 ):
     panel = pick_ref.shape[0]
     features = own_ref.shape[1]
-    held = jnp.concatenate([own_ref[...], other_ref[...]], axis=0) * scale_of(vectors_ref, panel, features)
+    held = jnp.concatenate([own_ref[...], other_ref[...]], axis=0) * scale_of(vectors_ref, features)
     chosen = product(pick_ref[...], jnp.concatenate(halves_of(held), axis=1))
     high, low = chosen[:, :features].astype(bf16), chosen[:, features:].astype(bf16)
     chosen_ref[...] = pack_left(high, low)
@@ -121,12 +121,12 @@
     own = row_place == col_place // halves
     panel, features = factor_left_ref.shape[0], sent_ref.shape[1]
 
-    high, low = halves_of(jnp.transpose(sent_ref[...] * scale_of(vectors_ref, panel, features)))
+    high, low = halves_of(jnp.transpose(sent_ref[...] * scale_of(vectors_ref, features)))
     right = pack_right(high, low)
     right_half = half_square(high, low, 0)
     chunks, chunk = block_ref.shape[:2]
     places = [slice(number * chunk, (number + 1) * chunk) for number in range(chunks)]
-    at = pl.multiple_of(panel + features + part * count, 128)
+    at = pl.multiple_of(features + part * count, 128)
     noise = jnp.where(own, vectors_ref[:, pl.ds(at, count)], 0.0)
     ids = (chunk, count)
     below = lax.broadcasted_iota(jnp.int32, ids, 0) - lax.broadcasted_iota(jnp.int32, ids, 1)
@@ -242,7 +242,7 @@
     while low < cols:
         high = min(4 * low, cols)
         away = apart & (high - low)
-        steps = range(high - low, 0, -low)
+        steps = range(low, high, low)
         received = [swap(held, bits, cols) for bits in steps]
         received, beside = lax.optimization_barrier((received, beside))
         for bits, value in zip(steps, received):
@@ -261,8 +261,9 @@
     col_place = lax.axis_index("col")
     part = halves - 1 - col_place % halves
     own_half = lax.dynamic_slice_in_dim(points, part * col_count, col_count, 0)
+    vectors = jnp.concatenate([ard_weights, noise])[None, :]
+    own_half, vectors = lax.optimization_barrier((own_half, vectors))
     sent = lax.ppermute(own_half, ("row", "col"), column_pairs(rows, cols))
-    vectors = jnp.concatenate([order.astype(f32), ard_weights, noise])[None, :]
     pieces, vectors = gather_panel(panel_pool, panel_index[0], cols, vectors)
 
     packed = 4 * features
@@ -276,7 +277,7 @@
             shape((row_count, 1)),
         ],
         **compute_params(10**8, 4 * 10**6),
-    )(inv_factor, points, vectors)
+    )(inv_factor, order[None, :], points, vectors)
 
     rows_left, chosen, chosen_half = pl.pallas_call(
         rows_kernel,

time: 23 us -> 23.4 us (1.017)
  local copies, waits for them, and re-layouts: 1.9 us -> 2.59 us
  other arithmetic: 1.42 us -> 0.74 us
  waiting for transfers between devices: 5.38 us -> 5.83 us
    convert_element_type x1 -> x0, other arithmetic: 0.68 us -> none  [on_device(): vectors = jnp.concatenate([order.astype(f32), ard_weights, noise])[None, :]]
    unnamed x4 -> x6, local copies, waits for them, and re-layouts: 0.01 us -> 0.69 us
    ppermute x5, waiting for transfers between devices: 5.37 us -> 5.83 us  [swap(): return lax.ppermute(value, 'col', [(i, i ^ bit) for i in range(cols)])]
  transfers between devices with their start and end apart: 6 -> 6, of which waited for: 2 -> 1; matrix products, arithmetic and copies ran while one was open for 15% -> 11% of each run, Pallas kernels for 14% -> 14%
where the time goes in v4:
time: 23.4 us; the launch traced here: 23.2 us
  Pallas kernels  7.56 us (32%)
  waiting for transfers between devices  5.83 us (25%)
  starting transfers between devices  5.73 us (24%)
  local copies, waits for them, and re-layouts  2.59 us (11%)
  between operations  0.75 us (3%)
  other arithmetic  0.74 us (3%)
    ppermute x5, waiting for transfers between devices, swap(): return lax.ppermute(value, 'col', [(i, i ^ bit) for i in range(cols)])  5.83 us
    pallas_call x1, Pallas kernels, on_device(): pl.pallas_call(functools.partial(update_kernel, rows, cols), out_shape=sh...  4.29 us
    ppermute x5, starting transfers between devices, swap(): return lax.ppermute(value, 'col', [(i, i ^ bit) for i in range(cols)])  3.94 us
    pallas_call x1, Pallas kernels, on_device(): pl.pallas_call(rows_kernel, out_shape=[shape((row_count, 3 * panel), bf16...  2.53 us
    ppermute x1, starting transfers between devices, on_device(): sent = lax.ppermute(own_half, ('row', 'col'), column_pairs(rows, cols))  1.79 us
    dynamic_slice x1, local copies, waits for them, and re-layouts, on_device(): own_half = lax.dynamic_slice_in_dim(points, part * col_count, col_count, 0)  0.97 us
    dynamic_slice x1, local copies, waits for them, and re-layouts, gather_panel(): mine = lax.dynamic_slice_in_dim(panel_pool, core * half_rows, half_rows, 0)  0.92 us
    pallas_call x1, Pallas kernels, on_device(): pl.pallas_call(parts_kernel, out_shape=[shape((panel, 3 * panel), bf16),...  0.74 us
  transfers between devices with their start and end apart: 6, of which 1 were waited for; matrix products, arithmetic and copies ran while one was open for 11% of the time, Pallas kernels for 14%

profile of v4, /device:TPU:29, one launch (start us, length us, event | category | flops | bytes accessed | tf_op | source)
XLA Modules:
  0.0 23.2 jit_solution(2826557784598371357)
XLA Ops:
  0.0 0.0 copy-start
  0.0 0.0 copy-start.1
  0.0 0.7 %collective-permute-start.1 = (f32[512,128]{1,0:T(8,128)}, f32[512,128]{1,0:T(8,128)S(1)}, u32[]{:S(2)}, u32[]{:S(2)}) collective-permute-start(f32[512,128]{1,0:T(8,128)} %param.8), channel_id=1, source_target_pairs={{0,1},{1,0},{2,3},{3,2},{4,5},{5,4},{6,7},{7,6},{8,9},{9,8},{10,11... | collective-permute-start | bytes 786440 | tf_op jit(solution)/shard_map/ppermute | solution.py:229
  1.4 0.9 %constant_dynamic-slice_fusion = f32[256,128]{1,0:T(8,128)S(1)} fusion(f32[512,128]{1,0:T(8,128)} %param.8, s32[]{:T(128)S(6)} %select_n.50), kind=kLoop, calls=%fused_computation.3 | loop fusion | bytes 262148 | tf_op jit(solution)/shard_map/dynamic_slice | solution.py:236
  2.3 0.0 collective-permute-done.1
  2.3 1.2 %collective-permute-start.4 = (f32[256,128]{1,0:T(8,128)S(1)}, f32[256,128]{1,0:T(8,128)S(1)}, u32[]{:S(2)}, u32[]{:S(2)}) collective-permute-start(f32[256,128]{1,0:T(8,128)S(1)} %dynamic-slice_select_fusion), channel_id=1, source_target_pairs={{0,6},{1,7},{2,4},{3,5},{4,2},{5,3},{6,0},{7,1},{8,14},{9,15},{10,... | collective-permute-start | bytes 393224 | tf_op jit(solution)/shard_map/ppermute | solution.py:229
  3.5 1.2 %collective-permute-start.3 = (f32[256,128]{1,0:T(8,128)S(1)}, f32[256,128]{1,0:T(8,128)S(1)}, u32[]{:S(2)}, u32[]{:S(2)}) collective-permute-start(f32[256,128]{1,0:T(8,128)S(1)} %dynamic-slice_select_fusion), channel_id=1, source_target_pairs={{0,4},{1,5},{2,6},{3,7},{4,0},{5,1},{6,2},{7,3},{8,12},{9,13},{10,... | collective-permute-start | bytes 393224 | tf_op jit(solution)/shard_map/ppermute | solution.py:229
  4.8 0.3 %collective-permute-start.2 = (f32[256,128]{1,0:T(8,128)S(1)}, f32[256,128]{1,0:T(8,128)S(1)}, u32[]{:S(2)}, u32[]{:S(2)}) collective-permute-start(f32[256,128]{1,0:T(8,128)S(1)} %dynamic-slice_select_fusion), channel_id=1, source_target_pairs={{0,2},{1,3},{2,0},{3,1},{4,6},{5,7},{6,4},{7,5},{8,10},{9,11},{10,... | collective-permute-start | bytes 393224 | tf_op jit(solution)/shard_map/ppermute | solution.py:229
  5.0 0.7 %pad_maximum_fusion = f32[1152]{0:T(1024)S(1)} fusion(f32[1024]{0:T(1024)} %param.13, f32[128]{0:T(128)} %param.12), kind=kLoop, calls=%fused_computation.2 | loop fusion | flops 1152 | bytes 9216 | tf_op jit(solution)/shard_map/concatenate | solution.py:264
  5.7 1.0 %constant_dynamic-slice_fusion.1 = f32[512,128]{1,0:T(8,128)S(1)} fusion(f32[1024,128]{1,0:T(8,128)} %points_ref.1, s32[]{:T(128)S(6)} %select_n.47), kind=kLoop, calls=%fused_computation.4 | loop fusion | bytes 524292 | tf_op jit(solution)/shard_map/dynamic_slice | solution.py:263
  6.7 1.8 %collective-permute-start = (f32[512,128]{1,0:T(8,128)S(1)}, f32[512,128]{1,0:T(8,128)S(1)}, u32[]{:S(2)}, u32[]{:S(2)}) collective-permute-start(f32[512,128]{1,0:T(8,128)S(1)} %constant_dynamic-slice_fusion.1), channel_id=1, source_target_pairs={{4,1},{6,9},{0,17},{2,25},{8,3},{10,11},{12,19},{14,27},{22,5},{18... | collective-permute-start | bytes 786440 | tf_op jit(solution)/shard_map/ppermute | solution.py:266
  8.5 0.0 collective-permute-done.4
  8.5 5.8 %collective-permute-done.3 = f32[256,128]{1,0:T(8,128)S(1)} collective-permute-done((f32[256,128]{1,0:T(8,128)S(1)}, f32[256,128]{1,0:T(8,128)S(1)}, u32[]{:S(2)}, u32[]{:S(2)}) %collective-permute-start.3) | collective-permute-done | bytes 131104 | tf_op jit(solution)/shard_map/ppermute | solution.py:229
  14.3 0.0 collective-permute-done.2
  14.4 0.5 %collective-permute-start.5 = (f32[256,128]{1,0:T(8,128)S(1)}, f32[256,128]{1,0:T(8,128)S(1)}, u32[]{:S(2)}, u32[]{:S(2)}) collective-permute-start(f32[256,128]{1,0:T(8,128)S(1)} %select_select_fusion.own_ref), channel_id=1, source_target_pairs={{0,1},{1,0},{2,3},{3,2},{4,5},{5,4},{6,7},{7,6},{8,9},{9,8},{10,11... | collective-permute-start | bytes 393224 | tf_op jit(solution)/shard_map/ppermute | solution.py:229
  14.9 0.0 copy-done
  14.9 0.0 copy-done.1
  14.9 0.0 copy-start.2
  14.9 0.7 %copy-done.2 = s32[512]{0:T(512)S(1)} copy-done((s32[512]{0:T(512)S(1)}, s32[512]{0:T(512)}, u32[]{:S(2)}) %copy-start.2) | copy-done | bytes 2072
  15.6 0.7 %shard_map.73 = (bf16[512,1536]{1,0:T(8,128)(2,1)S(1)}, bf16[1536,512]{1,0:T(8,128)(2,1)S(1)}, bf16[512,512]{1,0:T(8,128)(2,1)S(1)}, bf16[1024,512]{1,0:T(8,128)(2,1)S(1)}, f32[1024,1]{1,0:T(8,128)S(1)}) custom-call(f32[512,512]{1,0:T(8,128)S(1)} %copy-done.1, s32[1,512]{1,0:T(1,128)S(1)} %bitcast.6, f32[1024,128]{1,0:T(8,128)S(1)} %copy-done, ...), custom_call_target="tpu_custom_call" | custom-call | flops 100000000 | bytes 4000000 | tf_op jit(solution)/shard_map/pallas_call | solution.py:270
  16.3 0.0 collective-permute-done.5.other_ref
  16.4 2.5 %shard_map.74 = (bf16[1024,1536]{1,0:T(8,128)(2,1)S(1)}, bf16[512,512]{1,0:T(8,128)(2,1)S(1)}, f32[512,1]{1,0:T(8,128)S(1)}) custom-call(f32[256,128]{1,0:T(8,128)S(1)} %select_select_fusion.own_ref, f32[256,128]{1,0:T(8,128)S(1)} %collective-permute-done.5.other_ref, f32[1,1152]{1,0:T(1,128)S(1)} %broadcast_in_dim.6.vectors_ref, ...), custom_call_target="tpu_custom_call" | custom-call | flops 1 | bytes 1 | tf_op jit(solution)/shard_map/pallas_call | solution.py:282
  18.9 0.0 collective-permute-done.sent_ref
  18.9 4.3 %shard_map.75 = f32[1024,512]{1,0:T(8,128)} custom-call(f32[512,128]{1,0:T(8,128)S(1)} %collective-permute-done.sent_ref, f32[1,1152]{1,0:T(1,128)S(1)} %broadcast_in_dim.6.vectors_ref, bf16[512,1536]{1,0:T(8,128)(2,1)S(1)} %get-tuple-element.26.factor_left_ref, bf16[1024,512]{1,0:T(8,128)(2,1)S(1)} %get-tuple-element.27.left_ref, ...), custom_call_target="tpu_custom_call" | custom-call | flops 4000000000 | bytes 8000000 | tf_op jit(solution)/shard_map/pallas_call | solution.py:290
  (3 shorter events, 0.1 us)
Async XLA Ops:
  0.0 14.9 %copy-start = (f32[1024,128]{1,0:T(8,128)S(1)}, f32[1024,128]{1,0:T(8,128)}, u32[]{:S(2)}) copy-start(f32[1024,128]{1,0:T(8,128)} %points_ref.1) | copy-start | bytes 1572868
  0.0 14.9 %copy-start.1 = (f32[512,512]{1,0:T(8,128)S(1)}, f32[512,512]{1,0:T(8,128)}, u32[]{:S(2)}) copy-start(f32[512,512]{1,0:T(8,128)} %factor_ref.1) | copy-start | bytes 3145732
  0.0 2.3 %collective-permute-start.1 = (f32[512,128]{1,0:T(8,128)}, f32[512,128]{1,0:T(8,128)S(1)}, u32[]{:S(2)}, u32[]{:S(2)}) collective-permute-start(f32[512,128]{1,0:T(8,128)} %param.8), channel_id=1, source_target_pairs={{0,1},{1,0},{2,3},{3,2},{4,5},{5,4},{6,7},{7,6},{8,9},{9,8},{10,11... | collective-permute-start | bytes 786440 | tf_op jit(solution)/shard_map/ppermute | solution.py:229
  2.3 6.2 %collective-permute-start.4 = (f32[256,128]{1,0:T(8,128)S(1)}, f32[256,128]{1,0:T(8,128)S(1)}, u32[]{:S(2)}, u32[]{:S(2)}) collective-permute-start(f32[256,128]{1,0:T(8,128)S(1)} %dynamic-slice_select_fusion), channel_id=1, source_target_pairs={{0,6},{1,7},{2,4},{3,5},{4,2},{5,3},{6,0},{7,1},{8,14},{9,15},{10,... | collective-permute-start | bytes 393224 | tf_op jit(solution)/shard_map/ppermute | solution.py:229
  3.5 10.8 %collective-permute-start.3 = (f32[256,128]{1,0:T(8,128)S(1)}, f32[256,128]{1,0:T(8,128)S(1)}, u32[]{:S(2)}, u32[]{:S(2)}) collective-permute-start(f32[256,128]{1,0:T(8,128)S(1)} %dynamic-slice_select_fusion), channel_id=1, source_target_pairs={{0,4},{1,5},{2,6},{3,7},{4,0},{5,1},{6,2},{7,3},{8,12},{9,13},{10,... | collective-permute-start | bytes 393224 | tf_op jit(solution)/shard_map/ppermute | solution.py:229
  4.8 9.6 %collective-permute-start.2 = (f32[256,128]{1,0:T(8,128)S(1)}, f32[256,128]{1,0:T(8,128)S(1)}, u32[]{:S(2)}, u32[]{:S(2)}) collective-permute-start(f32[256,128]{1,0:T(8,128)S(1)} %dynamic-slice_select_fusion), channel_id=1, source_target_pairs={{0,2},{1,3},{2,0},{3,1},{4,6},{5,7},{6,4},{7,5},{8,10},{9,11},{10,... | collective-permute-start | bytes 393224 | tf_op jit(solution)/shard_map/ppermute | solution.py:229
  6.7 12.2 %collective-permute-start = (f32[512,128]{1,0:T(8,128)S(1)}, f32[512,128]{1,0:T(8,128)S(1)}, u32[]{:S(2)}, u32[]{:S(2)}) collective-permute-start(f32[512,128]{1,0:T(8,128)S(1)} %constant_dynamic-slice_fusion.1), channel_id=1, source_target_pairs={{4,1},{6,9},{0,17},{2,25},{8,3},{10,11},{12,19},{14,27},{22,5},{18... | collective-permute-start | bytes 786440 | tf_op jit(solution)/shard_map/ppermute | solution.py:266
  14.4 2.0 %collective-permute-start.5 = (f32[256,128]{1,0:T(8,128)S(1)}, f32[256,128]{1,0:T(8,128)S(1)}, u32[]{:S(2)}, u32[]{:S(2)}) collective-permute-start(f32[256,128]{1,0:T(8,128)S(1)} %select_select_fusion.own_ref), channel_id=1, source_target_pairs={{0,1},{1,0},{2,3},{3,2},{4,5},{5,4},{6,7},{7,6},{8,9},{9,8},{10,11... | collective-permute-start | bytes 393224 | tf_op jit(solution)/shard_map/ppermute | solution.py:229
  14.9 0.7 %copy-start.2 = (s32[512]{0:T(512)S(1)}, s32[512]{0:T(512)}, u32[]{:S(2)}) copy-start(s32[512]{0:T(512)} %param.9) | copy-start | bytes 6148

commit v5 on v2

--- a/solution.py
+++ b/solution.py
@@ -13,7 +13,7 @@
 log2_e = 1.4426950408889634
 vmem_bytes = 32 * 1024 * 1024
 f32, bf16 = jnp.float32, jnp.bfloat16
-block = 256
+block, square = 256, 128
 
 
 def halves_of(value):
@@ -128,8 +128,8 @@
     places = [slice(number * chunk, (number + 1) * chunk) for number in range(chunks)]
     at = pl.multiple_of(panel + features + part * count, 128)
     noise = jnp.where(own, vectors_ref[:, pl.ds(at, count)], 0.0)
-    ids = (chunk, count)
-    below = lax.broadcasted_iota(jnp.int32, ids, 0) - lax.broadcasted_iota(jnp.int32, ids, 1)
+    ids = (square, square)
+    on_diagonal = lax.broadcasted_iota(jnp.int32, ids, 0) == lax.broadcasted_iota(jnp.int32, ids, 1)
 
     crossed = product(chosen_ref[...], right)
     tiles = [product(left_ref[place, :], right) for place in places]
@@ -137,13 +137,15 @@
     for first in range(0, panel, block):
         last = first + block
         store_right(cols_ref, first, product(factor_left_ref[first:last, : 3 * last], kern_ref[: 3 * last, :]))
-    for number, place in enumerate(places):
-        tile = kern(tiles[number], left_half_ref[place, :], right_half)
-        block_ref[number] = tile + jnp.where(below == part * count - number * chunk, noise, 0.0)
-
     copies = []
     for number, place in enumerate(places):
-        block_ref[number] = block_ref[number] - product(rows_ref[place, :], cols_ref[...])
+        update = product(rows_ref[place, :], cols_ref[...])
+        block_ref[number] = kern(tiles[number], left_half_ref[place, :], right_half) - update
+        here = jnp.where(part == place.start // count, noise, 0.0)
+        for start in range(0, chunk, square):
+            first = place.start % count + start
+            now, across = slice(start, start + square), slice(first, first + square)
+            block_ref[number, now, across] += jnp.where(on_diagonal, here[:, across], 0.0)
         copy = pltpu.make_async_copy(block_ref.at[number], out_ref.at[pl.ds(number * chunk, chunk)], sems.at[number])
         copy.start()
         copies.append(copy)
@@ -175,7 +177,7 @@
 
 
 def source_places(rows, halves):
-    draw = random.Random(5)
+    draw = random.Random(1)
     across = math.isqrt(rows)
     places = {}
     load = collections.Counter()

time: 23 us -> 23.1 us (level)
  the two profiles are of different devices: /device:TPU:29 before, /device:TPU:0 now
where the time goes in v5:
time: 23.1 us; the launch traced here: 22.9 us
  Pallas kernels  7.48 us (32%)
  waiting for transfers between devices  6.43 us (28%)
  starting transfers between devices  4.85 us (21%)
  local copies, waits for them, and re-layouts  1.9 us (8%)
  other arithmetic  1.43 us (6%)
  between operations  0.81 us (4%)
    ppermute x5, waiting for transfers between devices, swap(): return lax.ppermute(value, 'col', [(i, i ^ bit) for i in range(cols)])  6.43 us
    ppermute x5, starting transfers between devices, swap(): return lax.ppermute(value, 'col', [(i, i ^ bit) for i in range(cols)])  4.79 us
    pallas_call x1, Pallas kernels, on_device(): pl.pallas_call(functools.partial(update_kernel, rows, cols), out_shape=sh...  4.19 us
    pallas_call x1, Pallas kernels, on_device(): pl.pallas_call(rows_kernel, out_shape=[shape((row_count, 3 * panel), bf16...  2.54 us
    dynamic_slice x1, local copies, waits for them, and re-layouts, on_device(): own_half = lax.dynamic_slice_in_dim(points, part * col_count, col_count, 0)  0.97 us
    dynamic_slice x1, local copies, waits for them, and re-layouts, gather_panel(): mine = lax.dynamic_slice_in_dim(panel_pool, core * half_rows, half_rows, 0)  0.92 us
    pallas_call x1, Pallas kernels, on_device(): pl.pallas_call(parts_kernel, out_shape=[shape((panel, 3 * panel), bf16),...  0.74 us
    concatenate x1, other arithmetic, on_device(): vectors = jnp.concatenate([order.astype(f32), ard_weights, noise])[None, :]  0.7 us
  transfers between devices with their start and end apart: 6, of which 4 were waited for; matrix products, arithmetic and copies ran while one was open for 14% of the time, Pallas kernels for 14%

profile of v5, /device:TPU:0, one launch (start us, length us, event | category | flops | bytes accessed | tf_op | source)
XLA Modules:
  0.0 22.9 jit_solution(5232269081820363578)
XLA Ops:
  0.0 0.0 copy-start
  0.0 0.0 copy-start.1
  0.0 0.5 %collective-permute-start.1 = (f32[512,128]{1,0:T(8,128)}, f32[512,128]{1,0:T(8,128)S(1)}, u32[]{:S(2)}, u32[]{:S(2)}) collective-permute-start(f32[512,128]{1,0:T(8,128)} %param.8), channel_id=1, source_target_pairs={{0,1},{1,0},{2,3},{3,2},{4,5},{5,4},{6,7},{7,6},{8,9},{9,8},{10,11... | collective-permute-start | bytes 786440 | tf_op jit(solution)/shard_map/ppermute | solution.py:231
  1.2 0.9 %constant_dynamic-slice_fusion = f32[256,128]{1,0:T(8,128)S(1)} fusion(f32[512,128]{1,0:T(8,128)} %param.8, s32[]{:T(128)S(6)} %select_n.50), kind=kLoop, calls=%fused_computation.3 | loop fusion | bytes 262148 | tf_op jit(solution)/shard_map/dynamic_slice | solution.py:238
  2.1 0.0 collective-permute-done.1
  2.1 3.6 %collective-permute-start.2 = (f32[256,128]{1,0:T(8,128)S(1)}, f32[256,128]{1,0:T(8,128)S(1)}, u32[]{:S(2)}, u32[]{:S(2)}) collective-permute-start(f32[256,128]{1,0:T(8,128)S(1)} %dynamic-slice_select_fusion), channel_id=1, source_target_pairs={{0,6},{1,7},{2,4},{3,5},{4,2},{5,3},{6,0},{7,1},{8,14},{9,15},{10,... | collective-permute-start | bytes 393224 | tf_op jit(solution)/shard_map/ppermute | solution.py:231
  5.8 0.5 %collective-permute-start.3 = (f32[256,128]{1,0:T(8,128)S(1)}, f32[256,128]{1,0:T(8,128)S(1)}, u32[]{:S(2)}, u32[]{:S(2)}) collective-permute-start(f32[256,128]{1,0:T(8,128)S(1)} %dynamic-slice_select_fusion), channel_id=1, source_target_pairs={{0,4},{1,5},{2,6},{3,7},{4,0},{5,1},{6,2},{7,3},{8,12},{9,13},{10,... | collective-permute-start | bytes 393224 | tf_op jit(solution)/shard_map/ppermute | solution.py:231
  6.3 0.1 collective-permute-start.4
  6.4 1.0 %constant_dynamic-slice_fusion.1 = f32[512,128]{1,0:T(8,128)S(1)} fusion(f32[1024,128]{1,0:T(8,128)} %points_ref.1, s32[]{:T(128)S(6)} %select_n.47), kind=kLoop, calls=%fused_computation.4 | loop fusion | bytes 524292 | tf_op jit(solution)/shard_map/dynamic_slice | solution.py:265
  7.4 0.1 collective-permute-start
  7.4 0.7 %convert_element_type.3 = f32[512]{0:T(512)S(1)} convert(s32[512]{0:T(512)} %param.9) | non-fusion elementwise | flops 512 | bytes 4096 | tf_op jit(solution)/shard_map/convert_element_type | solution.py:267
  8.1 0.7 %pad_maximum_fusion = f32[1664]{0:T(1024)S(1)} fusion(f32[1024]{0:T(1024)} %param.13, f32[128]{0:T(128)} %param.12, f32[512]{0:T(512)S(1)} %convert_element_type.3), kind=kLoop, calls=%fused_computation.2 | loop fusion | flops 3328 | bytes 13312 | tf_op jit(solution)/shard_map/concatenate | solution.py:267
  8.8 1.0 %collective-permute-done.2 = f32[256,128]{1,0:T(8,128)S(1)} collective-permute-done((f32[256,128]{1,0:T(8,128)S(1)}, f32[256,128]{1,0:T(8,128)S(1)}, u32[]{:S(2)}, u32[]{:S(2)}) %collective-permute-start.2) | collective-permute-done | bytes 131104 | tf_op jit(solution)/shard_map/ppermute | solution.py:231
  9.9 3.7 %collective-permute-done.3 = f32[256,128]{1,0:T(8,128)S(1)} collective-permute-done((f32[256,128]{1,0:T(8,128)S(1)}, f32[256,128]{1,0:T(8,128)S(1)}, u32[]{:S(2)}, u32[]{:S(2)}) %collective-permute-start.3) | collective-permute-done | bytes 131104 | tf_op jit(solution)/shard_map/ppermute | solution.py:231
  13.6 1.1 %collective-permute-done.4 = f32[256,128]{1,0:T(8,128)S(1)} collective-permute-done((f32[256,128]{1,0:T(8,128)S(1)}, f32[256,128]{1,0:T(8,128)S(1)}, u32[]{:S(2)}, u32[]{:S(2)}) %collective-permute-start.4) | collective-permute-done | bytes 131104 | tf_op jit(solution)/shard_map/ppermute | solution.py:231
  14.7 0.1 collective-permute-start.5
  14.8 0.0 copy-done
  14.8 0.0 copy-done.1
  14.8 0.7 %shard_map.73 = (bf16[512,1536]{1,0:T(8,128)(2,1)S(1)}, bf16[1536,512]{1,0:T(8,128)(2,1)S(1)}, bf16[512,512]{1,0:T(8,128)(2,1)S(1)}, bf16[1024,512]{1,0:T(8,128)(2,1)S(1)}, f32[1024,1]{1,0:T(8,128)S(1)}) custom-call(f32[512,512]{1,0:T(8,128)S(1)} %copy-done.1, f32[1024,128]{1,0:T(8,128)S(1)} %copy-done, f32[1,1664]{1,0:T(1,128)S(1)} %broadcast_in_dim.3.vectors_ref), custom_call_target="tpu_custom_call" | custom-call | flops 100000000 | bytes 4000000 | tf_op jit(solution)/shard_map/pallas_call | solution.py:271
  15.6 0.6 %collective-permute-done.5.other_ref = f32[256,128]{1,0:T(8,128)S(1)} collective-permute-done((f32[256,128]{1,0:T(8,128)S(1)}, f32[256,128]{1,0:T(8,128)S(1)}, u32[]{:S(2)}, u32[]{:S(2)}) %collective-permute-start.5) | collective-permute-done | bytes 131104 | tf_op jit(solution)/shard_map/ppermute | solution.py:231
  16.1 2.5 %shard_map.74 = (bf16[1024,1536]{1,0:T(8,128)(2,1)S(1)}, bf16[512,512]{1,0:T(8,128)(2,1)S(1)}, f32[512,1]{1,0:T(8,128)S(1)}) custom-call(f32[256,128]{1,0:T(8,128)S(1)} %select_select_fusion.own_ref, f32[256,128]{1,0:T(8,128)S(1)} %collective-permute-done.5.other_ref, f32[1,1664]{1,0:T(1,128)S(1)} %broadcast_in_dim.3.vectors_ref, ...), custom_call_target="tpu_custom_call" | custom-call | flops 1 | bytes 1 | tf_op jit(solution)/shard_map/pallas_call | solution.py:283
  18.7 0.0 collective-permute-done.sent_ref
  18.7 4.2 %shard_map.75 = f32[1024,512]{1,0:T(8,128)} custom-call(f32[512,128]{1,0:T(8,128)S(1)} %collective-permute-done.sent_ref, f32[1,1664]{1,0:T(1,128)S(1)} %broadcast_in_dim.3.vectors_ref, bf16[512,1536]{1,0:T(8,128)(2,1)S(1)} %get-tuple-element.22.factor_left_ref, bf16[1024,512]{1,0:T(8,128)(2,1)S(1)} %get-tuple-element.23.left_ref, ...), custom_call_target="tpu_custom_call" | custom-call | flops 4000000000 | bytes 8000000 | tf_op jit(solution)/shard_map/pallas_call | solution.py:291
  (3 shorter events, 0.1 us)
Async XLA Ops:
  0.0 14.8 %copy-start = (f32[1024,128]{1,0:T(8,128)S(1)}, f32[1024,128]{1,0:T(8,128)}, u32[]{:S(2)}) copy-start(f32[1024,128]{1,0:T(8,128)} %points_ref.1) | copy-start | bytes 1572868
  0.0 14.8 %copy-start.1 = (f32[512,512]{1,0:T(8,128)S(1)}, f32[512,512]{1,0:T(8,128)}, u32[]{:S(2)}) copy-start(f32[512,512]{1,0:T(8,128)} %factor_ref.1) | copy-start | bytes 3145732
  0.0 2.1 %collective-permute-start.1 = (f32[512,128]{1,0:T(8,128)}, f32[512,128]{1,0:T(8,128)S(1)}, u32[]{:S(2)}, u32[]{:S(2)}) collective-permute-start(f32[512,128]{1,0:T(8,128)} %param.8), channel_id=1, source_target_pairs={{0,1},{1,0},{2,3},{3,2},{4,5},{5,4},{6,7},{7,6},{8,9},{9,8},{10,11... | collective-permute-start | bytes 786440 | tf_op jit(solution)/shard_map/ppermute | solution.py:231
  2.1 7.8 %collective-permute-start.2 = (f32[256,128]{1,0:T(8,128)S(1)}, f32[256,128]{1,0:T(8,128)S(1)}, u32[]{:S(2)}, u32[]{:S(2)}) collective-permute-start(f32[256,128]{1,0:T(8,128)S(1)} %dynamic-slice_select_fusion), channel_id=1, source_target_pairs={{0,6},{1,7},{2,4},{3,5},{4,2},{5,3},{6,0},{7,1},{8,14},{9,15},{10,... | collective-permute-start | bytes 393224 | tf_op jit(solution)/shard_map/ppermute | solution.py:231
  5.8 7.9 %collective-permute-start.3 = (f32[256,128]{1,0:T(8,128)S(1)}, f32[256,128]{1,0:T(8,128)S(1)}, u32[]{:S(2)}, u32[]{:S(2)}) collective-permute-start(f32[256,128]{1,0:T(8,128)S(1)} %dynamic-slice_select_fusion), channel_id=1, source_target_pairs={{0,4},{1,5},{2,6},{3,7},{4,0},{5,1},{6,2},{7,3},{8,12},{9,13},{10,... | collective-permute-start | bytes 393224 | tf_op jit(solution)/shard_map/ppermute | solution.py:231
  6.3 8.4 %collective-permute-start.4 = (f32[256,128]{1,0:T(8,128)S(1)}, f32[256,128]{1,0:T(8,128)S(1)}, u32[]{:S(2)}, u32[]{:S(2)}) collective-permute-start(f32[256,128]{1,0:T(8,128)S(1)} %dynamic-slice_select_fusion), channel_id=1, source_target_pairs={{0,2},{1,3},{2,0},{3,1},{4,6},{5,7},{6,4},{7,5},{8,10},{9,11},{10,... | collective-permute-start | bytes 393224 | tf_op jit(solution)/shard_map/ppermute | solution.py:231
  7.4 11.3 %collective-permute-start = (f32[512,128]{1,0:T(8,128)S(1)}, f32[512,128]{1,0:T(8,128)S(1)}, u32[]{:S(2)}, u32[]{:S(2)}) collective-permute-start(f32[512,128]{1,0:T(8,128)S(1)} %constant_dynamic-slice_fusion.1), channel_id=1, source_target_pairs={{0,1},{2,9},{4,17},{6,25},{12,3},{10,11},{14,19},{8,27},{20,5},{22... | collective-permute-start | bytes 786440 | tf_op jit(solution)/shard_map/ppermute | solution.py:266
  14.7 1.4 %collective-permute-start.5 = (f32[256,128]{1,0:T(8,128)S(1)}, f32[256,128]{1,0:T(8,128)S(1)}, u32[]{:S(2)}, u32[]{:S(2)}) collective-permute-start(f32[256,128]{1,0:T(8,128)S(1)} %select_select_fusion.own_ref), channel_id=1, source_target_pairs={{0,1},{1,0},{2,3},{3,2},{4,5},{5,4},{6,7},{7,6},{8,9},{9,8},{10,11... | collective-permute-start | bytes 393224 | tf_op jit(solution)/shard_map/ppermute | solution.py:231

commit v6 on v5

--- a/solution.py
+++ b/solution.py
@@ -177,7 +177,7 @@
 
 
 def source_places(rows, halves):
-    draw = random.Random(1)
+    draw = random.Random(5)
     across = math.isqrt(rows)
     places = {}
     load = collections.Counter()
@@ -244,7 +244,7 @@
     while low < cols:
         high = min(4 * low, cols)
         away = apart & (high - low)
-        steps = range(high - low, 0, -low)
+        steps = [2 * low, 3 * low, low] if high == 4 * low else [low]
         received = [swap(held, bits, cols) for bits in steps]
         received, beside = lax.optimization_barrier((received, beside))
         for bits, value in zip(steps, received):

time: 23.1 us -> 23.2 us (level)
  the two profiles are of different devices: /device:TPU:0 before, /device:TPU:13 now
where the time goes in v6:
time: 23.2 us; the launch traced here: 23 us
  starting transfers between devices  7.47 us (32%)
  Pallas kernels  7.47 us (32%)
  waiting for transfers between devices  3.97 us (17%)
  local copies, waits for them, and re-layouts  1.9 us (8%)
  other arithmetic  1.42 us (6%)
  between operations  0.74 us (3%)
    ppermute x5, starting transfers between devices, swap(): return lax.ppermute(value, 'col', [(i, i ^ bit) for i in range(cols)])  5.39 us
    pallas_call x1, Pallas kernels, on_device(): pl.pallas_call(functools.partial(update_kernel, rows, cols), out_shape=sh...  4.19 us
    ppermute x5, waiting for transfers between devices, swap(): return lax.ppermute(value, 'col', [(i, i ^ bit) for i in range(cols)])  3.97 us
    pallas_call x1, Pallas kernels, on_device(): pl.pallas_call(rows_kernel, out_shape=[shape((row_count, 3 * panel), bf16...  2.54 us
    ppermute x1, starting transfers between devices, on_device(): sent = lax.ppermute(own_half, ('row', 'col'), column_pairs(rows, cols))  2.08 us
    dynamic_slice x1, local copies, waits for them, and re-layouts, on_device(): own_half = lax.dynamic_slice_in_dim(points, part * col_count, col_count, 0)  0.97 us
    dynamic_slice x1, local copies, waits for them, and re-layouts, gather_panel(): mine = lax.dynamic_slice_in_dim(panel_pool, core * half_rows, half_rows, 0)  0.92 us
    pallas_call x1, Pallas kernels, on_device(): pl.pallas_call(parts_kernel, out_shape=[shape((panel, 3 * panel), bf16),...  0.74 us
  transfers between devices with their start and end apart: 6, of which 3 were waited for; matrix products, arithmetic and copies ran while one was open for 14% of the time, Pallas kernels for 14%

profile of v6, /device:TPU:13, one launch (start us, length us, event | category | flops | bytes accessed | tf_op | source)
XLA Modules:
  0.0 23.0 jit_solution(590340742908226171)
XLA Ops:
  0.0 0.0 copy-start
  0.0 0.0 copy-start.1
  0.0 0.7 %collective-permute-start.1 = (f32[512,128]{1,0:T(8,128)}, f32[512,128]{1,0:T(8,128)S(1)}, u32[]{:S(2)}, u32[]{:S(2)}) collective-permute-start(f32[512,128]{1,0:T(8,128)} %param.8), channel_id=1, source_target_pairs={{0,1},{1,0},{2,3},{3,2},{4,5},{5,4},{6,7},{7,6},{8,9},{9,8},{10,11... | collective-permute-start | bytes 786440 | tf_op jit(solution)/shard_map/ppermute | solution.py:231
  1.4 0.9 %constant_dynamic-slice_fusion = f32[256,128]{1,0:T(8,128)S(1)} fusion(f32[512,128]{1,0:T(8,128)} %param.8, s32[]{:T(128)S(6)} %select_n.50), kind=kLoop, calls=%fused_computation.3 | loop fusion | bytes 262148 | tf_op jit(solution)/shard_map/dynamic_slice | solution.py:238
  2.3 0.0 collective-permute-done.1
  2.3 0.3 %collective-permute-start.2 = (f32[256,128]{1,0:T(8,128)S(1)}, f32[256,128]{1,0:T(8,128)S(1)}, u32[]{:S(2)}, u32[]{:S(2)}) collective-permute-start(f32[256,128]{1,0:T(8,128)S(1)} %dynamic-slice_select_fusion), channel_id=1, source_target_pairs={{0,4},{1,5},{2,6},{3,7},{4,0},{5,1},{6,2},{7,3},{8,12},{9,13},{10,... | collective-permute-start | bytes 393224 | tf_op jit(solution)/shard_map/ppermute | solution.py:231
  2.6 2.2 %collective-permute-start.3 = (f32[256,128]{1,0:T(8,128)S(1)}, f32[256,128]{1,0:T(8,128)S(1)}, u32[]{:S(2)}, u32[]{:S(2)}) collective-permute-start(f32[256,128]{1,0:T(8,128)S(1)} %dynamic-slice_select_fusion), channel_id=1, source_target_pairs={{0,6},{1,7},{2,4},{3,5},{4,2},{5,3},{6,0},{7,1},{8,14},{9,15},{10,... | collective-permute-start | bytes 393224 | tf_op jit(solution)/shard_map/ppermute | solution.py:231
  4.8 0.3 %collective-permute-start.4 = (f32[256,128]{1,0:T(8,128)S(1)}, f32[256,128]{1,0:T(8,128)S(1)}, u32[]{:S(2)}, u32[]{:S(2)}) collective-permute-start(f32[256,128]{1,0:T(8,128)S(1)} %dynamic-slice_select_fusion), channel_id=1, source_target_pairs={{0,2},{1,3},{2,0},{3,1},{4,6},{5,7},{6,4},{7,5},{8,10},{9,11},{10,... | collective-permute-start | bytes 393224 | tf_op jit(solution)/shard_map/ppermute | solution.py:231
  5.0 1.0 %constant_dynamic-slice_fusion.1 = f32[512,128]{1,0:T(8,128)S(1)} fusion(f32[1024,128]{1,0:T(8,128)} %points_ref.1, s32[]{:T(128)S(6)} %select_n.47), kind=kLoop, calls=%fused_computation.4 | loop fusion | bytes 524292 | tf_op jit(solution)/shard_map/dynamic_slice | solution.py:265
  6.0 2.1 %collective-permute-start = (f32[512,128]{1,0:T(8,128)S(1)}, f32[512,128]{1,0:T(8,128)S(1)}, u32[]{:S(2)}, u32[]{:S(2)}) collective-permute-start(f32[512,128]{1,0:T(8,128)S(1)} %constant_dynamic-slice_fusion.1), channel_id=1, source_target_pairs={{4,1},{6,9},{0,17},{2,25},{8,3},{10,11},{12,19},{14,27},{22,5},{18... | collective-permute-start | bytes 786440 | tf_op jit(solution)/shard_map/ppermute | solution.py:266
  8.1 0.7 %convert_element_type.3 = f32[512]{0:T(512)S(1)} convert(s32[512]{0:T(512)} %param.9) | non-fusion elementwise | flops 512 | bytes 4096 | tf_op jit(solution)/shard_map/convert_element_type | solution.py:267
  8.8 0.7 %pad_maximum_fusion = f32[1664]{0:T(1024)S(1)} fusion(f32[1024]{0:T(1024)} %param.13, f32[128]{0:T(128)} %param.12, f32[512]{0:T(512)S(1)} %convert_element_type.3), kind=kLoop, calls=%fused_computation.2 | loop fusion | flops 3328 | bytes 13312 | tf_op jit(solution)/shard_map/concatenate | solution.py:267
  9.5 0.7 %collective-permute-done.2 = f32[256,128]{1,0:T(8,128)S(1)} collective-permute-done((f32[256,128]{1,0:T(8,128)S(1)}, f32[256,128]{1,0:T(8,128)S(1)}, u32[]{:S(2)}, u32[]{:S(2)}) %collective-permute-start.2) | collective-permute-done | bytes 131104 | tf_op jit(solution)/shard_map/ppermute | solution.py:231
  10.2 0.0 collective-permute-done.3
  10.2 3.0 %collective-permute-done.4 = f32[256,128]{1,0:T(8,128)S(1)} collective-permute-done((f32[256,128]{1,0:T(8,128)S(1)}, f32[256,128]{1,0:T(8,128)S(1)}, u32[]{:S(2)}, u32[]{:S(2)}) %collective-permute-start.4) | collective-permute-done | bytes 131104 | tf_op jit(solution)/shard_map/ppermute | solution.py:231
  13.2 2.0 %collective-permute-start.5 = (f32[256,128]{1,0:T(8,128)S(1)}, f32[256,128]{1,0:T(8,128)S(1)}, u32[]{:S(2)}, u32[]{:S(2)}) collective-permute-start(f32[256,128]{1,0:T(8,128)S(1)} %select_select_fusion.own_ref), channel_id=1, source_target_pairs={{0,1},{1,0},{2,3},{3,2},{4,5},{5,4},{6,7},{7,6},{8,9},{9,8},{10,11... | collective-permute-start | bytes 393224 | tf_op jit(solution)/shard_map/ppermute | solution.py:231
  15.2 0.0 copy-done
  15.2 0.0 copy-done.1
  15.2 0.7 %shard_map.73 = (bf16[512,1536]{1,0:T(8,128)(2,1)S(1)}, bf16[1536,512]{1,0:T(8,128)(2,1)S(1)}, bf16[512,512]{1,0:T(8,128)(2,1)S(1)}, bf16[1024,512]{1,0:T(8,128)(2,1)S(1)}, f32[1024,1]{1,0:T(8,128)S(1)}) custom-call(f32[512,512]{1,0:T(8,128)S(1)} %copy-done.1, f32[1024,128]{1,0:T(8,128)S(1)} %copy-done, f32[1,1664]{1,0:T(1,128)S(1)} %broadcast_in_dim.3.vectors_ref), custom_call_target="tpu_custom_call" | custom-call | flops 100000000 | bytes 4000000 | tf_op jit(solution)/shard_map/pallas_call | solution.py:271
  16.0 0.2 %collective-permute-done.5.other_ref = f32[256,128]{1,0:T(8,128)S(1)} collective-permute-done((f32[256,128]{1,0:T(8,128)S(1)}, f32[256,128]{1,0:T(8,128)S(1)}, u32[]{:S(2)}, u32[]{:S(2)}) %collective-permute-start.5) | collective-permute-done | bytes 131104 | tf_op jit(solution)/shard_map/ppermute | solution.py:231
  16.2 2.5 %shard_map.74 = (bf16[1024,1536]{1,0:T(8,128)(2,1)S(1)}, bf16[512,512]{1,0:T(8,128)(2,1)S(1)}, f32[512,1]{1,0:T(8,128)S(1)}) custom-call(f32[256,128]{1,0:T(8,128)S(1)} %select_select_fusion.own_ref, f32[256,128]{1,0:T(8,128)S(1)} %collective-permute-done.5.other_ref, f32[1,1664]{1,0:T(1,128)S(1)} %broadcast_in_dim.3.vectors_ref, ...), custom_call_target="tpu_custom_call" | custom-call | flops 1 | bytes 1 | tf_op jit(solution)/shard_map/pallas_call | solution.py:283
  18.8 0.0 collective-permute-done.sent_ref
  18.8 4.2 %shard_map.75 = f32[1024,512]{1,0:T(8,128)} custom-call(f32[512,128]{1,0:T(8,128)S(1)} %collective-permute-done.sent_ref, f32[1,1664]{1,0:T(1,128)S(1)} %broadcast_in_dim.3.vectors_ref, bf16[512,1536]{1,0:T(8,128)(2,1)S(1)} %get-tuple-element.22.factor_left_ref, bf16[1024,512]{1,0:T(8,128)(2,1)S(1)} %get-tuple-element.23.left_ref, ...), custom_call_target="tpu_custom_call" | custom-call | flops 4000000000 | bytes 8000000 | tf_op jit(solution)/shard_map/pallas_call | solution.py:291
  (3 shorter events, 0.1 us)
Async XLA Ops:
  0.0 15.2 %copy-start = (f32[1024,128]{1,0:T(8,128)S(1)}, f32[1024,128]{1,0:T(8,128)}, u32[]{:S(2)}) copy-start(f32[1024,128]{1,0:T(8,128)} %points_ref.1) | copy-start | bytes 1572868
  0.0 15.2 %copy-start.1 = (f32[512,512]{1,0:T(8,128)S(1)}, f32[512,512]{1,0:T(8,128)}, u32[]{:S(2)}) copy-start(f32[512,512]{1,0:T(8,128)} %factor_ref.1) | copy-start | bytes 3145732
  0.0 2.3 %collective-permute-start.1 = (f32[512,128]{1,0:T(8,128)}, f32[512,128]{1,0:T(8,128)S(1)}, u32[]{:S(2)}, u32[]{:S(2)}) collective-permute-start(f32[512,128]{1,0:T(8,128)} %param.8), channel_id=1, source_target_pairs={{0,1},{1,0},{2,3},{3,2},{4,5},{5,4},{6,7},{7,6},{8,9},{9,8},{10,11... | collective-permute-start | bytes 786440 | tf_op jit(solution)/shard_map/ppermute | solution.py:231
  2.3 7.8 %collective-permute-start.2 = (f32[256,128]{1,0:T(8,128)S(1)}, f32[256,128]{1,0:T(8,128)S(1)}, u32[]{:S(2)}, u32[]{:S(2)}) collective-permute-start(f32[256,128]{1,0:T(8,128)S(1)} %dynamic-slice_select_fusion), channel_id=1, source_target_pairs={{0,4},{1,5},{2,6},{3,7},{4,0},{5,1},{6,2},{7,3},{8,12},{9,13},{10,... | collective-permute-start | bytes 393224 | tf_op jit(solution)/shard_map/ppermute | solution.py:231
  2.6 7.5 %collective-permute-start.3 = (f32[256,128]{1,0:T(8,128)S(1)}, f32[256,128]{1,0:T(8,128)S(1)}, u32[]{:S(2)}, u32[]{:S(2)}) collective-permute-start(f32[256,128]{1,0:T(8,128)S(1)} %dynamic-slice_select_fusion), channel_id=1, source_target_pairs={{0,6},{1,7},{2,4},{3,5},{4,2},{5,3},{6,0},{7,1},{8,14},{9,15},{10,... | collective-permute-start | bytes 393224 | tf_op jit(solution)/shard_map/ppermute | solution.py:231
  4.8 8.4 %collective-permute-start.4 = (f32[256,128]{1,0:T(8,128)S(1)}, f32[256,128]{1,0:T(8,128)S(1)}, u32[]{:S(2)}, u32[]{:S(2)}) collective-permute-start(f32[256,128]{1,0:T(8,128)S(1)} %dynamic-slice_select_fusion), channel_id=1, source_target_pairs={{0,2},{1,3},{2,0},{3,1},{4,6},{5,7},{6,4},{7,5},{8,10},{9,11},{10,... | collective-permute-start | bytes 393224 | tf_op jit(solution)/shard_map/ppermute | solution.py:231
  6.0 12.8 %collective-permute-start = (f32[512,128]{1,0:T(8,128)S(1)}, f32[512,128]{1,0:T(8,128)S(1)}, u32[]{:S(2)}, u32[]{:S(2)}) collective-permute-start(f32[512,128]{1,0:T(8,128)S(1)} %constant_dynamic-slice_fusion.1), channel_id=1, source_target_pairs={{4,1},{6,9},{0,17},{2,25},{8,3},{10,11},{12,19},{14,27},{22,5},{18... | collective-permute-start | bytes 786440 | tf_op jit(solution)/shard_map/ppermute | solution.py:266
  13.2 3.0 %collective-permute-start.5 = (f32[256,128]{1,0:T(8,128)S(1)}, f32[256,128]{1,0:T(8,128)S(1)}, u32[]{:S(2)}, u32[]{:S(2)}) collective-permute-start(f32[256,128]{1,0:T(8,128)S(1)} %select_select_fusion.own_ref), channel_id=1, source_target_pairs={{0,1},{1,0},{2,3},{3,2},{4,5},{5,4},{6,7},{7,6},{8,9},{9,8},{10,11... | collective-permute-start | bytes 393224 | tf_op jit(solution)/shard_map/ppermute | solution.py:231

commit v7 on v5

--- a/solution.py
+++ b/solution.py
@@ -177,17 +177,18 @@
 
 
 def source_places(rows, halves):
-    draw = random.Random(1)
+    draw = random.Random(4)
     across = math.isqrt(rows)
     places = {}
     load = collections.Counter()
 
     def move(key, r, sign):
         change = 0
+        early = (1 + 2 * r / rows) * (0 <= r - key[1] <= 1)
         for link in links_of(places[key][r], key[1], r, across):
             old = load[link]
             load[link] = old + sign
-            change += (old + sign) ** 4 - old**4
+            change += (old + sign) ** 4 - old**4 + sign * early * (link[0] == 2)
         return change
 
     for h in range(halves):

time: 23.1 us -> 23 us (level)
  the two profiles are of different devices: /device:TPU:0 before, /device:TPU:29 now
where the time goes in v7:
time: 23 us; the launch traced here: 22.6 us
  starting transfers between devices  8.64 us (38%)
  Pallas kernels  7.46 us (32%)
  waiting for transfers between devices  2.46 us (11%)
  local copies, waits for them, and re-layouts  1.9 us (8%)
  other arithmetic  1.42 us (6%)
  between operations  0.75 us (3%)
    ppermute x5, starting transfers between devices, swap(): return lax.ppermute(value, 'col', [(i, i ^ bit) for i in range(cols)])  6.73 us
    pallas_call x1, Pallas kernels, on_device(): pl.pallas_call(functools.partial(update_kernel, rows, cols), out_shape=sh...  4.19 us
    pallas_call x1, Pallas kernels, on_device(): pl.pallas_call(rows_kernel, out_shape=[shape((row_count, 3 * panel), bf16...  2.53 us
    ppermute x5, waiting for transfers between devices, swap(): return lax.ppermute(value, 'col', [(i, i ^ bit) for i in range(cols)])  2.46 us
    ppermute x1, starting transfers between devices, on_device(): sent = lax.ppermute(own_half, ('row', 'col'), column_pairs(rows, cols))  1.91 us
    dynamic_slice x1, local copies, waits for them, and re-layouts, on_device(): own_half = lax.dynamic_slice_in_dim(points, part * col_count, col_count, 0)  0.97 us
    dynamic_slice x1, local copies, waits for them, and re-layouts, gather_panel(): mine = lax.dynamic_slice_in_dim(panel_pool, core * half_rows, half_rows, 0)  0.92 us
    pallas_call x1, Pallas kernels, on_device(): pl.pallas_call(parts_kernel, out_shape=[shape((panel, 3 * panel), bf16),...  0.74 us
  transfers between devices with their start and end apart: 6, of which 2 were waited for; matrix products, arithmetic and copies ran while one was open for 15% of the time, Pallas kernels for 14%

profile of v7, /device:TPU:29, one launch (start us, length us, event | category | flops | bytes accessed | tf_op | source)
XLA Modules:
  0.0 22.6 jit_solution(9416301424169602146)
XLA Ops:
  0.0 0.0 copy-start
  0.0 0.0 copy-start.1
  0.0 0.7 %collective-permute-start.1 = (f32[512,128]{1,0:T(8,128)}, f32[512,128]{1,0:T(8,128)S(1)}, u32[]{:S(2)}, u32[]{:S(2)}) collective-permute-start(f32[512,128]{1,0:T(8,128)} %param.8), channel_id=1, source_target_pairs={{0,1},{1,0},{2,3},{3,2},{4,5},{5,4},{6,7},{7,6},{8,9},{9,8},{10,11... | collective-permute-start | bytes 786440 | tf_op jit(solution)/shard_map/ppermute | solution.py:232
  1.4 0.9 %constant_dynamic-slice_fusion = f32[256,128]{1,0:T(8,128)S(1)} fusion(f32[512,128]{1,0:T(8,128)} %param.8, s32[]{:T(128)S(6)} %select_n.50), kind=kLoop, calls=%fused_computation.3 | loop fusion | bytes 262148 | tf_op jit(solution)/shard_map/dynamic_slice | solution.py:239
  2.3 0.0 collective-permute-done.1
  2.3 1.2 %collective-permute-start.2 = (f32[256,128]{1,0:T(8,128)S(1)}, f32[256,128]{1,0:T(8,128)S(1)}, u32[]{:S(2)}, u32[]{:S(2)}) collective-permute-start(f32[256,128]{1,0:T(8,128)S(1)} %dynamic-slice_select_fusion), channel_id=1, source_target_pairs={{0,6},{1,7},{2,4},{3,5},{4,2},{5,3},{6,0},{7,1},{8,14},{9,15},{10,... | collective-permute-start | bytes 393224 | tf_op jit(solution)/shard_map/ppermute | solution.py:232
  3.5 1.2 %collective-permute-start.3 = (f32[256,128]{1,0:T(8,128)S(1)}, f32[256,128]{1,0:T(8,128)S(1)}, u32[]{:S(2)}, u32[]{:S(2)}) collective-permute-start(f32[256,128]{1,0:T(8,128)S(1)} %dynamic-slice_select_fusion), channel_id=1, source_target_pairs={{0,4},{1,5},{2,6},{3,7},{4,0},{5,1},{6,2},{7,3},{8,12},{9,13},{10,... | collective-permute-start | bytes 393224 | tf_op jit(solution)/shard_map/ppermute | solution.py:232
  4.8 0.3 %collective-permute-start.4 = (f32[256,128]{1,0:T(8,128)S(1)}, f32[256,128]{1,0:T(8,128)S(1)}, u32[]{:S(2)}, u32[]{:S(2)}) collective-permute-start(f32[256,128]{1,0:T(8,128)S(1)} %dynamic-slice_select_fusion), channel_id=1, source_target_pairs={{0,2},{1,3},{2,0},{3,1},{4,6},{5,7},{6,4},{7,5},{8,10},{9,11},{10,... | collective-permute-start | bytes 393224 | tf_op jit(solution)/shard_map/ppermute | solution.py:232
  5.0 1.0 %constant_dynamic-slice_fusion.1 = f32[512,128]{1,0:T(8,128)S(1)} fusion(f32[1024,128]{1,0:T(8,128)} %points_ref.1, s32[]{:T(128)S(6)} %select_n.47), kind=kLoop, calls=%fused_computation.4 | loop fusion | bytes 524292 | tf_op jit(solution)/shard_map/dynamic_slice | solution.py:266
  6.0 1.9 %collective-permute-start = (f32[512,128]{1,0:T(8,128)S(1)}, f32[512,128]{1,0:T(8,128)S(1)}, u32[]{:S(2)}, u32[]{:S(2)}) collective-permute-start(f32[512,128]{1,0:T(8,128)S(1)} %constant_dynamic-slice_fusion.1), channel_id=1, source_target_pairs={{4,1},{0,9},{2,17},{6,25},{12,3},{14,11},{10,19},{8,27},{22,5},{18... | collective-permute-start | bytes 786440 | tf_op jit(solution)/shard_map/ppermute | solution.py:267
  7.9 0.7 %convert_element_type.3 = f32[512]{0:T(512)S(1)} convert(s32[512]{0:T(512)} %param.9) | non-fusion elementwise | flops 512 | bytes 4096 | tf_op jit(solution)/shard_map/convert_element_type | solution.py:268
  8.6 0.7 %pad_maximum_fusion = f32[1664]{0:T(1024)S(1)} fusion(f32[1024]{0:T(1024)} %param.13, f32[128]{0:T(128)} %param.12, f32[512]{0:T(512)S(1)} %convert_element_type.3), kind=kLoop, calls=%fused_computation.2 | loop fusion | flops 3328 | bytes 13312 | tf_op jit(solution)/shard_map/concatenate | solution.py:268
  9.3 0.0 collective-permute-done.2
  9.3 2.2 %collective-permute-done.3 = f32[256,128]{1,0:T(8,128)S(1)} collective-permute-done((f32[256,128]{1,0:T(8,128)S(1)}, f32[256,128]{1,0:T(8,128)S(1)}, u32[]{:S(2)}, u32[]{:S(2)}) %collective-permute-start.3) | collective-permute-done | bytes 131104 | tf_op jit(solution)/shard_map/ppermute | solution.py:232
  11.5 0.0 collective-permute-done.4
  11.6 3.3 %collective-permute-start.5 = (f32[256,128]{1,0:T(8,128)S(1)}, f32[256,128]{1,0:T(8,128)S(1)}, u32[]{:S(2)}, u32[]{:S(2)}) collective-permute-start(f32[256,128]{1,0:T(8,128)S(1)} %select_select_fusion.own_ref), channel_id=1, source_target_pairs={{0,1},{1,0},{2,3},{3,2},{4,5},{5,4},{6,7},{7,6},{8,9},{9,8},{10,11... | collective-permute-start | bytes 393224 | tf_op jit(solution)/shard_map/ppermute | solution.py:232
  14.9 0.0 copy-done
  14.9 0.0 copy-done.1
  14.9 0.7 %shard_map.73 = (bf16[512,1536]{1,0:T(8,128)(2,1)S(1)}, bf16[1536,512]{1,0:T(8,128)(2,1)S(1)}, bf16[512,512]{1,0:T(8,128)(2,1)S(1)}, bf16[1024,512]{1,0:T(8,128)(2,1)S(1)}, f32[1024,1]{1,0:T(8,128)S(1)}) custom-call(f32[512,512]{1,0:T(8,128)S(1)} %copy-done.1, f32[1024,128]{1,0:T(8,128)S(1)} %copy-done, f32[1,1664]{1,0:T(1,128)S(1)} %broadcast_in_dim.3.vectors_ref), custom_call_target="tpu_custom_call" | custom-call | flops 100000000 | bytes 4000000 | tf_op jit(solution)/shard_map/pallas_call | solution.py:272
  15.7 0.2 %collective-permute-done.5.other_ref = f32[256,128]{1,0:T(8,128)S(1)} collective-permute-done((f32[256,128]{1,0:T(8,128)S(1)}, f32[256,128]{1,0:T(8,128)S(1)}, u32[]{:S(2)}, u32[]{:S(2)}) %collective-permute-start.5) | collective-permute-done | bytes 131104 | tf_op jit(solution)/shard_map/ppermute | solution.py:232
  15.9 2.5 %shard_map.74 = (bf16[1024,1536]{1,0:T(8,128)(2,1)S(1)}, bf16[512,512]{1,0:T(8,128)(2,1)S(1)}, f32[512,1]{1,0:T(8,128)S(1)}) custom-call(f32[256,128]{1,0:T(8,128)S(1)} %select_select_fusion.own_ref, f32[256,128]{1,0:T(8,128)S(1)} %collective-permute-done.5.other_ref, f32[1,1664]{1,0:T(1,128)S(1)} %broadcast_in_dim.3.vectors_ref, ...), custom_call_target="tpu_custom_call" | custom-call | flops 1 | bytes 1 | tf_op jit(solution)/shard_map/pallas_call | solution.py:284
  18.4 0.0 collective-permute-done.sent_ref
  18.5 4.2 %shard_map.75 = f32[1024,512]{1,0:T(8,128)} custom-call(f32[512,128]{1,0:T(8,128)S(1)} %collective-permute-done.sent_ref, f32[1,1664]{1,0:T(1,128)S(1)} %broadcast_in_dim.3.vectors_ref, bf16[512,1536]{1,0:T(8,128)(2,1)S(1)} %get-tuple-element.22.factor_left_ref, bf16[1024,512]{1,0:T(8,128)(2,1)S(1)} %get-tuple-element.23.left_ref, ...), custom_call_target="tpu_custom_call" | custom-call | flops 4000000000 | bytes 8000000 | tf_op jit(solution)/shard_map/pallas_call | solution.py:292
  (3 shorter events, 0.1 us)
Async XLA Ops:
  0.0 14.9 %copy-start = (f32[1024,128]{1,0:T(8,128)S(1)}, f32[1024,128]{1,0:T(8,128)}, u32[]{:S(2)}) copy-start(f32[1024,128]{1,0:T(8,128)} %points_ref.1) | copy-start | bytes 1572868
  0.0 14.9 %copy-start.1 = (f32[512,512]{1,0:T(8,128)S(1)}, f32[512,512]{1,0:T(8,128)}, u32[]{:S(2)}) copy-start(f32[512,512]{1,0:T(8,128)} %factor_ref.1) | copy-start | bytes 3145732
  0.0 2.3 %collective-permute-start.1 = (f32[512,128]{1,0:T(8,128)}, f32[512,128]{1,0:T(8,128)S(1)}, u32[]{:S(2)}, u32[]{:S(2)}) collective-permute-start(f32[512,128]{1,0:T(8,128)} %param.8), channel_id=1, source_target_pairs={{0,1},{1,0},{2,3},{3,2},{4,5},{5,4},{6,7},{7,6},{8,9},{9,8},{10,11... | collective-permute-start | bytes 786440 | tf_op jit(solution)/shard_map/ppermute | solution.py:232
  2.3 7.0 %collective-permute-start.2 = (f32[256,128]{1,0:T(8,128)S(1)}, f32[256,128]{1,0:T(8,128)S(1)}, u32[]{:S(2)}, u32[]{:S(2)}) collective-permute-start(f32[256,128]{1,0:T(8,128)S(1)} %dynamic-slice_select_fusion), channel_id=1, source_target_pairs={{0,6},{1,7},{2,4},{3,5},{4,2},{5,3},{6,0},{7,1},{8,14},{9,15},{10,... | collective-permute-start | bytes 393224 | tf_op jit(solution)/shard_map/ppermute | solution.py:232
  3.5 8.0 %collective-permute-start.3 = (f32[256,128]{1,0:T(8,128)S(1)}, f32[256,128]{1,0:T(8,128)S(1)}, u32[]{:S(2)}, u32[]{:S(2)}) collective-permute-start(f32[256,128]{1,0:T(8,128)S(1)} %dynamic-slice_select_fusion), channel_id=1, source_target_pairs={{0,4},{1,5},{2,6},{3,7},{4,0},{5,1},{6,2},{7,3},{8,12},{9,13},{10,... | collective-permute-start | bytes 393224 | tf_op jit(solution)/shard_map/ppermute | solution.py:232
  4.8 6.8 %collective-permute-start.4 = (f32[256,128]{1,0:T(8,128)S(1)}, f32[256,128]{1,0:T(8,128)S(1)}, u32[]{:S(2)}, u32[]{:S(2)}) collective-permute-start(f32[256,128]{1,0:T(8,128)S(1)} %dynamic-slice_select_fusion), channel_id=1, source_target_pairs={{0,2},{1,3},{2,0},{3,1},{4,6},{5,7},{6,4},{7,5},{8,10},{9,11},{10,... | collective-permute-start | bytes 393224 | tf_op jit(solution)/shard_map/ppermute | solution.py:232
  6.0 12.4 %collective-permute-start = (f32[512,128]{1,0:T(8,128)S(1)}, f32[512,128]{1,0:T(8,128)S(1)}, u32[]{:S(2)}, u32[]{:S(2)}) collective-permute-start(f32[512,128]{1,0:T(8,128)S(1)} %constant_dynamic-slice_fusion.1), channel_id=1, source_target_pairs={{4,1},{0,9},{2,17},{6,25},{12,3},{14,11},{10,19},{8,27},{22,5},{18... | collective-permute-start | bytes 786440 | tf_op jit(solution)/shard_map/ppermute | solution.py:267
  11.6 4.3 %collective-permute-start.5 = (f32[256,128]{1,0:T(8,128)S(1)}, f32[256,128]{1,0:T(8,128)S(1)}, u32[]{:S(2)}, u32[]{:S(2)}) collective-permute-start(f32[256,128]{1,0:T(8,128)S(1)} %select_select_fusion.own_ref), channel_id=1, source_target_pairs={{0,1},{1,0},{2,3},{3,2},{4,5},{5,4},{6,7},{7,6},{8,9},{9,8},{10,11... | collective-permute-start | bytes 393224 | tf_op jit(solution)/shard_map/ppermute | solution.py:232

commit v8 on v6

--- a/solution.py
+++ b/solution.py
@@ -244,7 +244,7 @@
     while low < cols:
         high = min(4 * low, cols)
         away = apart & (high - low)
-        steps = [2 * low, 3 * low, low] if high == 4 * low else [low]
+        steps = range(high - low, 0, -low)
         received = [swap(held, bits, cols) for bits in steps]
         received, beside = lax.optimization_barrier((received, beside))
         for bits, value in zip(steps, received):

time: 23.2 us -> 22.9 us (0.987)
  the two profiles are of different devices: /device:TPU:13 before, /device:TPU:29 now
where the time goes in v8:
time: 22.9 us; the launch traced here: 22.6 us
  Pallas kernels  7.46 us (33%)
  starting transfers between devices  5.73 us (25%)
  waiting for transfers between devices  5.38 us (23%)
  local copies, waits for them, and re-layouts  1.9 us (8%)
  other arithmetic  1.42 us (6%)
  between operations  0.75 us (3%)
    ppermute x5, waiting for transfers between devices, swap(): return lax.ppermute(value, 'col', [(i, i ^ bit) for i in range(cols)])  5.37 us
    pallas_call x1, Pallas kernels, on_device(): pl.pallas_call(functools.partial(update_kernel, rows, cols), out_shape=sh...  4.19 us
    ppermute x5, starting transfers between devices, swap(): return lax.ppermute(value, 'col', [(i, i ^ bit) for i in range(cols)])  3.94 us
    pallas_call x1, Pallas kernels, on_device(): pl.pallas_call(rows_kernel, out_shape=[shape((row_count, 3 * panel), bf16...  2.53 us
    ppermute x1, starting transfers between devices, on_device(): sent = lax.ppermute(own_half, ('row', 'col'), column_pairs(rows, cols))  1.79 us
    dynamic_slice x1, local copies, waits for them, and re-layouts, on_device(): own_half = lax.dynamic_slice_in_dim(points, part * col_count, col_count, 0)  0.97 us
    dynamic_slice x1, local copies, waits for them, and re-layouts, gather_panel(): mine = lax.dynamic_slice_in_dim(panel_pool, core * half_rows, half_rows, 0)  0.92 us
    pallas_call x1, Pallas kernels, on_device(): pl.pallas_call(parts_kernel, out_shape=[shape((panel, 3 * panel), bf16),...  0.74 us
  transfers between devices with their start and end apart: 6, of which 2 were waited for; matrix products, arithmetic and copies ran while one was open for 15% of the time, Pallas kernels for 14%

profile of v8, /device:TPU:29, one launch (start us, length us, event | category | flops | bytes accessed | tf_op | source)
XLA Modules:
  0.0 22.6 jit_solution(15692118375091881900)
XLA Ops:
  0.0 0.0 copy-start
  0.0 0.0 copy-start.1
  0.0 0.7 %collective-permute-start.1 = (f32[512,128]{1,0:T(8,128)}, f32[512,128]{1,0:T(8,128)S(1)}, u32[]{:S(2)}, u32[]{:S(2)}) collective-permute-start(f32[512,128]{1,0:T(8,128)} %param.8), channel_id=1, source_target_pairs={{0,1},{1,0},{2,3},{3,2},{4,5},{5,4},{6,7},{7,6},{8,9},{9,8},{10,11... | collective-permute-start | bytes 786440 | tf_op jit(solution)/shard_map/ppermute | solution.py:231
  1.4 0.9 %constant_dynamic-slice_fusion = f32[256,128]{1,0:T(8,128)S(1)} fusion(f32[512,128]{1,0:T(8,128)} %param.8, s32[]{:T(128)S(6)} %select_n.50), kind=kLoop, calls=%fused_computation.3 | loop fusion | bytes 262148 | tf_op jit(solution)/shard_map/dynamic_slice | solution.py:238
  2.3 0.0 collective-permute-done.1
  2.3 1.2 %collective-permute-start.2 = (f32[256,128]{1,0:T(8,128)S(1)}, f32[256,128]{1,0:T(8,128)S(1)}, u32[]{:S(2)}, u32[]{:S(2)}) collective-permute-start(f32[256,128]{1,0:T(8,128)S(1)} %dynamic-slice_select_fusion), channel_id=1, source_target_pairs={{0,6},{1,7},{2,4},{3,5},{4,2},{5,3},{6,0},{7,1},{8,14},{9,15},{10,... | collective-permute-start | bytes 393224 | tf_op jit(solution)/shard_map/ppermute | solution.py:231
  3.5 1.2 %collective-permute-start.3 = (f32[256,128]{1,0:T(8,128)S(1)}, f32[256,128]{1,0:T(8,128)S(1)}, u32[]{:S(2)}, u32[]{:S(2)}) collective-permute-start(f32[256,128]{1,0:T(8,128)S(1)} %dynamic-slice_select_fusion), channel_id=1, source_target_pairs={{0,4},{1,5},{2,6},{3,7},{4,0},{5,1},{6,2},{7,3},{8,12},{9,13},{10,... | collective-permute-start | bytes 393224 | tf_op jit(solution)/shard_map/ppermute | solution.py:231
  4.8 0.3 %collective-permute-start.4 = (f32[256,128]{1,0:T(8,128)S(1)}, f32[256,128]{1,0:T(8,128)S(1)}, u32[]{:S(2)}, u32[]{:S(2)}) collective-permute-start(f32[256,128]{1,0:T(8,128)S(1)} %dynamic-slice_select_fusion), channel_id=1, source_target_pairs={{0,2},{1,3},{2,0},{3,1},{4,6},{5,7},{6,4},{7,5},{8,10},{9,11},{10,... | collective-permute-start | bytes 393224 | tf_op jit(solution)/shard_map/ppermute | solution.py:231
  5.0 1.0 %constant_dynamic-slice_fusion.1 = f32[512,128]{1,0:T(8,128)S(1)} fusion(f32[1024,128]{1,0:T(8,128)} %points_ref.1, s32[]{:T(128)S(6)} %select_n.47), kind=kLoop, calls=%fused_computation.4 | loop fusion | bytes 524292 | tf_op jit(solution)/shard_map/dynamic_slice | solution.py:265
  6.0 1.8 %collective-permute-start = (f32[512,128]{1,0:T(8,128)S(1)}, f32[512,128]{1,0:T(8,128)S(1)}, u32[]{:S(2)}, u32[]{:S(2)}) collective-permute-start(f32[512,128]{1,0:T(8,128)S(1)} %constant_dynamic-slice_fusion.1), channel_id=1, source_target_pairs={{4,1},{6,9},{0,17},{2,25},{8,3},{10,11},{12,19},{14,27},{22,5},{18... | collective-permute-start | bytes 786440 | tf_op jit(solution)/shard_map/ppermute | solution.py:266
  7.8 0.7 %convert_element_type.3 = f32[512]{0:T(512)S(1)} convert(s32[512]{0:T(512)} %param.9) | non-fusion elementwise | flops 512 | bytes 4096 | tf_op jit(solution)/shard_map/convert_element_type | solution.py:267
  8.5 0.7 %pad_maximum_fusion = f32[1664]{0:T(1024)S(1)} fusion(f32[1024]{0:T(1024)} %param.13, f32[128]{0:T(128)} %param.12, f32[512]{0:T(512)S(1)} %convert_element_type.3), kind=kLoop, calls=%fused_computation.2 | loop fusion | flops 3328 | bytes 13312 | tf_op jit(solution)/shard_map/concatenate | solution.py:267
  9.2 0.0 collective-permute-done.2
  9.2 5.1 %collective-permute-done.3 = f32[256,128]{1,0:T(8,128)S(1)} collective-permute-done((f32[256,128]{1,0:T(8,128)S(1)}, f32[256,128]{1,0:T(8,128)S(1)}, u32[]{:S(2)}, u32[]{:S(2)}) %collective-permute-start.3) | collective-permute-done | bytes 131104 | tf_op jit(solution)/shard_map/ppermute | solution.py:231
  14.3 0.0 collective-permute-done.4
  14.4 0.5 %collective-permute-start.5 = (f32[256,128]{1,0:T(8,128)S(1)}, f32[256,128]{1,0:T(8,128)S(1)}, u32[]{:S(2)}, u32[]{:S(2)}) collective-permute-start(f32[256,128]{1,0:T(8,128)S(1)} %select_select_fusion.own_ref), channel_id=1, source_target_pairs={{0,1},{1,0},{2,3},{3,2},{4,5},{5,4},{6,7},{7,6},{8,9},{9,8},{10,11... | collective-permute-start | bytes 393224 | tf_op jit(solution)/shard_map/ppermute | solution.py:231
  14.9 0.0 copy-done
  14.9 0.0 copy-done.1
  14.9 0.7 %shard_map.73 = (bf16[512,1536]{1,0:T(8,128)(2,1)S(1)}, bf16[1536,512]{1,0:T(8,128)(2,1)S(1)}, bf16[512,512]{1,0:T(8,128)(2,1)S(1)}, bf16[1024,512]{1,0:T(8,128)(2,1)S(1)}, f32[1024,1]{1,0:T(8,128)S(1)}) custom-call(f32[512,512]{1,0:T(8,128)S(1)} %copy-done.1, f32[1024,128]{1,0:T(8,128)S(1)} %copy-done, f32[1,1664]{1,0:T(1,128)S(1)} %broadcast_in_dim.3.vectors_ref), custom_call_target="tpu_custom_call" | custom-call | flops 100000000 | bytes 4000000 | tf_op jit(solution)/shard_map/pallas_call | solution.py:271
  15.7 0.2 %collective-permute-done.5.other_ref = f32[256,128]{1,0:T(8,128)S(1)} collective-permute-done((f32[256,128]{1,0:T(8,128)S(1)}, f32[256,128]{1,0:T(8,128)S(1)}, u32[]{:S(2)}, u32[]{:S(2)}) %collective-permute-start.5) | collective-permute-done | bytes 131104 | tf_op jit(solution)/shard_map/ppermute | solution.py:231
  15.9 2.5 %shard_map.74 = (bf16[1024,1536]{1,0:T(8,128)(2,1)S(1)}, bf16[512,512]{1,0:T(8,128)(2,1)S(1)}, f32[512,1]{1,0:T(8,128)S(1)}) custom-call(f32[256,128]{1,0:T(8,128)S(1)} %select_select_fusion.own_ref, f32[256,128]{1,0:T(8,128)S(1)} %collective-permute-done.5.other_ref, f32[1,1664]{1,0:T(1,128)S(1)} %broadcast_in_dim.3.vectors_ref, ...), custom_call_target="tpu_custom_call" | custom-call | flops 1 | bytes 1 | tf_op jit(solution)/shard_map/pallas_call | solution.py:283
  18.4 0.0 collective-permute-done.sent_ref
  18.5 4.2 %shard_map.75 = f32[1024,512]{1,0:T(8,128)} custom-call(f32[512,128]{1,0:T(8,128)S(1)} %collective-permute-done.sent_ref, f32[1,1664]{1,0:T(1,128)S(1)} %broadcast_in_dim.3.vectors_ref, bf16[512,1536]{1,0:T(8,128)(2,1)S(1)} %get-tuple-element.22.factor_left_ref, bf16[1024,512]{1,0:T(8,128)(2,1)S(1)} %get-tuple-element.23.left_ref, ...), custom_call_target="tpu_custom_call" | custom-call | flops 4000000000 | bytes 8000000 | tf_op jit(solution)/shard_map/pallas_call | solution.py:291
  (3 shorter events, 0.1 us)
Async XLA Ops:
  0.0 14.9 %copy-start = (f32[1024,128]{1,0:T(8,128)S(1)}, f32[1024,128]{1,0:T(8,128)}, u32[]{:S(2)}) copy-start(f32[1024,128]{1,0:T(8,128)} %points_ref.1) | copy-start | bytes 1572868
  0.0 14.9 %copy-start.1 = (f32[512,512]{1,0:T(8,128)S(1)}, f32[512,512]{1,0:T(8,128)}, u32[]{:S(2)}) copy-start(f32[512,512]{1,0:T(8,128)} %factor_ref.1) | copy-start | bytes 3145732
  0.0 2.3 %collective-permute-start.1 = (f32[512,128]{1,0:T(8,128)}, f32[512,128]{1,0:T(8,128)S(1)}, u32[]{:S(2)}, u32[]{:S(2)}) collective-permute-start(f32[512,128]{1,0:T(8,128)} %param.8), channel_id=1, source_target_pairs={{0,1},{1,0},{2,3},{3,2},{4,5},{5,4},{6,7},{7,6},{8,9},{9,8},{10,11... | collective-permute-start | bytes 786440 | tf_op jit(solution)/shard_map/ppermute | solution.py:231
  2.3 6.9 %collective-permute-start.2 = (f32[256,128]{1,0:T(8,128)S(1)}, f32[256,128]{1,0:T(8,128)S(1)}, u32[]{:S(2)}, u32[]{:S(2)}) collective-permute-start(f32[256,128]{1,0:T(8,128)S(1)} %dynamic-slice_select_fusion), channel_id=1, source_target_pairs={{0,6},{1,7},{2,4},{3,5},{4,2},{5,3},{6,0},{7,1},{8,14},{9,15},{10,... | collective-permute-start | bytes 393224 | tf_op jit(solution)/shard_map/ppermute | solution.py:231
  3.5 10.8 %collective-permute-start.3 = (f32[256,128]{1,0:T(8,128)S(1)}, f32[256,128]{1,0:T(8,128)S(1)}, u32[]{:S(2)}, u32[]{:S(2)}) collective-permute-start(f32[256,128]{1,0:T(8,128)S(1)} %dynamic-slice_select_fusion), channel_id=1, source_target_pairs={{0,4},{1,5},{2,6},{3,7},{4,0},{5,1},{6,2},{7,3},{8,12},{9,13},{10,... | collective-permute-start | bytes 393224 | tf_op jit(solution)/shard_map/ppermute | solution.py:231
  4.8 9.6 %collective-permute-start.4 = (f32[256,128]{1,0:T(8,128)S(1)}, f32[256,128]{1,0:T(8,128)S(1)}, u32[]{:S(2)}, u32[]{:S(2)}) collective-permute-start(f32[256,128]{1,0:T(8,128)S(1)} %dynamic-slice_select_fusion), channel_id=1, source_target_pairs={{0,2},{1,3},{2,0},{3,1},{4,6},{5,7},{6,4},{7,5},{8,10},{9,11},{10,... | collective-permute-start | bytes 393224 | tf_op jit(solution)/shard_map/ppermute | solution.py:231
  6.0 12.4 %collective-permute-start = (f32[512,128]{1,0:T(8,128)S(1)}, f32[512,128]{1,0:T(8,128)S(1)}, u32[]{:S(2)}, u32[]{:S(2)}) collective-permute-start(f32[512,128]{1,0:T(8,128)S(1)} %constant_dynamic-slice_fusion.1), channel_id=1, source_target_pairs={{4,1},{6,9},{0,17},{2,25},{8,3},{10,11},{12,19},{14,27},{22,5},{18... | collective-permute-start | bytes 786440 | tf_op jit(solution)/shard_map/ppermute | solution.py:266
  14.4 1.5 %collective-permute-start.5 = (f32[256,128]{1,0:T(8,128)S(1)}, f32[256,128]{1,0:T(8,128)S(1)}, u32[]{:S(2)}, u32[]{:S(2)}) collective-permute-start(f32[256,128]{1,0:T(8,128)S(1)} %select_select_fusion.own_ref), channel_id=1, source_target_pairs={{0,1},{1,0},{2,3},{3,2},{4,5},{5,4},{6,7},{7,6},{8,9},{9,8},{10,11... | collective-permute-start | bytes 393224 | tf_op jit(solution)/shard_map/ppermute | solution.py:231

commit v9 on v5

--- a/solution.py
+++ b/solution.py
@@ -179,15 +179,24 @@
 def source_places(rows, halves):
     draw = random.Random(1)
     across = math.isqrt(rows)
+    fewest = rows * halves // 4
     places = {}
     load = collections.Counter()
 
+    def price(link, count):
+        if link[0] == 0:
+            return 15 * max(0, count - fewest)
+        plane = link[1]
+        return (0.3, 10, 40)[min(plane, 2)] * max(0, count - 1) ** 2
+
     def move(key, r, sign):
         change = 0
+        ahead = r - key[1]
+        early = {-1: 0.7, 0: 0.5, 1: 40 if r == rows - 1 else 2}.get(ahead, 0)
         for link in links_of(places[key][r], key[1], r, across):
             old = load[link]
             load[link] = old + sign
-            change += (old + sign) ** 4 - old**4
+            change += price(link, old + sign) - price(link, old) + sign * early * (link[0] == 2)
         return change
 
     for h in range(halves):
@@ -204,7 +213,7 @@
         change = move(key, one, -1) + move(key, two, -1)
         own[one], own[two] = own[two], own[one]
         change += move(key, one, 1) + move(key, two, 1)
-        heat = 30.0 * (1 - number / tries) + 0.01
+        heat = 6.0 * (1 - number / tries) + 0.02
         if change <= 0 or draw.random() < math.exp(-change / heat):
             total += change
             if total < best:

time: 23.1 us -> 23.8 us (1.030)
  the two profiles are of different devices: /device:TPU:0 before, /device:TPU:4 now
where the time goes in v9:
time: 23.8 us; the launch traced here: 23.6 us
  waiting for transfers between devices  8.21 us (34%)
  Pallas kernels  7.46 us (31%)
  starting transfers between devices  3.71 us (16%)
  local copies, waits for them, and re-layouts  1.9 us (8%)
  other arithmetic  1.42 us (6%)
  between operations  0.89 us (4%)
    ppermute x5, waiting for transfers between devices, swap(): return lax.ppermute(value, 'col', [(i, i ^ bit) for i in range(cols)])  4.3 us
    pallas_call x1, Pallas kernels, on_device(): pl.pallas_call(functools.partial(update_kernel, rows, cols), out_shape=sh...  4.18 us
    ppermute x1, waiting for transfers between devices, on_device(): sent = lax.ppermute(own_half, ('row', 'col'), column_pairs(rows, cols))  3.91 us
    ppermute x5, starting transfers between devices, swap(): return lax.ppermute(value, 'col', [(i, i ^ bit) for i in range(cols)])  3.65 us
    pallas_call x1, Pallas kernels, on_device(): pl.pallas_call(rows_kernel, out_shape=[shape((row_count, 3 * panel), bf16...  2.53 us
    dynamic_slice x1, local copies, waits for them, and re-layouts, on_device(): own_half = lax.dynamic_slice_in_dim(points, part * col_count, col_count, 0)  0.97 us
    dynamic_slice x1, local copies, waits for them, and re-layouts, gather_panel(): mine = lax.dynamic_slice_in_dim(panel_pool, core * half_rows, half_rows, 0)  0.92 us
    pallas_call x1, Pallas kernels, on_device(): pl.pallas_call(parts_kernel, out_shape=[shape((panel, 3 * panel), bf16),...  0.74 us
  transfers between devices with their start and end apart: 6, of which 4 were waited for; matrix products, arithmetic and copies ran while one was open for 14% of the time, Pallas kernels for 14%

profile of v9, /device:TPU:4, one launch (start us, length us, event | category | flops | bytes accessed | tf_op | source)
XLA Modules:
  0.0 23.6 jit_solution(5266498416429440819)
XLA Ops:
  0.0 0.0 copy-start
  0.0 0.0 copy-start.1
  0.0 0.0 collective-permute-start.1
  0.8 0.9 %constant_dynamic-slice_fusion = f32[256,128]{1,0:T(8,128)S(1)} fusion(f32[512,128]{1,0:T(8,128)} %param.8, s32[]{:T(128)S(6)} %select_n.50), kind=kLoop, calls=%fused_computation.3 | loop fusion | bytes 262148 | tf_op jit(solution)/shard_map/dynamic_slice | solution.py:247
  1.7 0.0 collective-permute-done.1
  1.8 1.5 %collective-permute-start.2 = (f32[256,128]{1,0:T(8,128)S(1)}, f32[256,128]{1,0:T(8,128)S(1)}, u32[]{:S(2)}, u32[]{:S(2)}) collective-permute-start(f32[256,128]{1,0:T(8,128)S(1)} %dynamic-slice_select_fusion), channel_id=1, source_target_pairs={{0,6},{1,7},{2,4},{3,5},{4,2},{5,3},{6,0},{7,1},{8,14},{9,15},{10,... | collective-permute-start | bytes 393224 | tf_op jit(solution)/shard_map/ppermute | solution.py:240
  3.3 1.5 %collective-permute-start.3 = (f32[256,128]{1,0:T(8,128)S(1)}, f32[256,128]{1,0:T(8,128)S(1)}, u32[]{:S(2)}, u32[]{:S(2)}) collective-permute-start(f32[256,128]{1,0:T(8,128)S(1)} %dynamic-slice_select_fusion), channel_id=1, source_target_pairs={{0,4},{1,5},{2,6},{3,7},{4,0},{5,1},{6,2},{7,3},{8,12},{9,13},{10,... | collective-permute-start | bytes 393224 | tf_op jit(solution)/shard_map/ppermute | solution.py:240
  4.8 0.5 %collective-permute-start.4 = (f32[256,128]{1,0:T(8,128)S(1)}, f32[256,128]{1,0:T(8,128)S(1)}, u32[]{:S(2)}, u32[]{:S(2)}) collective-permute-start(f32[256,128]{1,0:T(8,128)S(1)} %dynamic-slice_select_fusion), channel_id=1, source_target_pairs={{0,2},{1,3},{2,0},{3,1},{4,6},{5,7},{6,4},{7,5},{8,10},{9,11},{10,... | collective-permute-start | bytes 393224 | tf_op jit(solution)/shard_map/ppermute | solution.py:240
  5.4 1.0 %constant_dynamic-slice_fusion.1 = f32[512,128]{1,0:T(8,128)S(1)} fusion(f32[1024,128]{1,0:T(8,128)} %points_ref.1, s32[]{:T(128)S(6)} %select_n.47), kind=kLoop, calls=%fused_computation.4 | loop fusion | bytes 524292 | tf_op jit(solution)/shard_map/dynamic_slice | solution.py:274
  6.3 0.1 collective-permute-start
  6.4 0.7 %convert_element_type.3 = f32[512]{0:T(512)S(1)} convert(s32[512]{0:T(512)} %param.9) | non-fusion elementwise | flops 512 | bytes 4096 | tf_op jit(solution)/shard_map/convert_element_type | solution.py:276
  7.1 0.7 %pad_maximum_fusion = f32[1664]{0:T(1024)S(1)} fusion(f32[1024]{0:T(1024)} %param.13, f32[128]{0:T(128)} %param.12, f32[512]{0:T(512)S(1)} %convert_element_type.3), kind=kLoop, calls=%fused_computation.2 | loop fusion | flops 3328 | bytes 13312 | tf_op jit(solution)/shard_map/concatenate | solution.py:276
  7.8 1.3 %collective-permute-done.2 = f32[256,128]{1,0:T(8,128)S(1)} collective-permute-done((f32[256,128]{1,0:T(8,128)S(1)}, f32[256,128]{1,0:T(8,128)S(1)}, u32[]{:S(2)}, u32[]{:S(2)}) %collective-permute-start.2) | collective-permute-done | bytes 131104 | tf_op jit(solution)/shard_map/ppermute | solution.py:240
  9.1 2.4 %collective-permute-done.3 = f32[256,128]{1,0:T(8,128)S(1)} collective-permute-done((f32[256,128]{1,0:T(8,128)S(1)}, f32[256,128]{1,0:T(8,128)S(1)}, u32[]{:S(2)}, u32[]{:S(2)}) %collective-permute-start.3) | collective-permute-done | bytes 131104 | tf_op jit(solution)/shard_map/ppermute | solution.py:240
  11.5 0.0 collective-permute-done.4
  11.5 0.1 collective-permute-start.5
  11.6 0.0 copy-done
  11.6 0.0 copy-done.1
  11.6 0.7 %shard_map.73 = (bf16[512,1536]{1,0:T(8,128)(2,1)S(1)}, bf16[1536,512]{1,0:T(8,128)(2,1)S(1)}, bf16[512,512]{1,0:T(8,128)(2,1)S(1)}, bf16[1024,512]{1,0:T(8,128)(2,1)S(1)}, f32[1024,1]{1,0:T(8,128)S(1)}) custom-call(f32[512,512]{1,0:T(8,128)S(1)} %copy-done.1, f32[1024,128]{1,0:T(8,128)S(1)} %copy-done, f32[1,1664]{1,0:T(1,128)S(1)} %broadcast_in_dim.3.vectors_ref), custom_call_target="tpu_custom_call" | custom-call | flops 100000000 | bytes 4000000 | tf_op jit(solution)/shard_map/pallas_call | solution.py:280
  12.4 0.6 %collective-permute-done.5.other_ref = f32[256,128]{1,0:T(8,128)S(1)} collective-permute-done((f32[256,128]{1,0:T(8,128)S(1)}, f32[256,128]{1,0:T(8,128)S(1)}, u32[]{:S(2)}, u32[]{:S(2)}) %collective-permute-start.5) | collective-permute-done | bytes 131104 | tf_op jit(solution)/shard_map/ppermute | solution.py:240
  13.0 2.5 %shard_map.74 = (bf16[1024,1536]{1,0:T(8,128)(2,1)S(1)}, bf16[512,512]{1,0:T(8,128)(2,1)S(1)}, f32[512,1]{1,0:T(8,128)S(1)}) custom-call(f32[256,128]{1,0:T(8,128)S(1)} %select_select_fusion.own_ref, f32[256,128]{1,0:T(8,128)S(1)} %collective-permute-done.5.other_ref, f32[1,1664]{1,0:T(1,128)S(1)} %broadcast_in_dim.3.vectors_ref, ...), custom_call_target="tpu_custom_call" | custom-call | flops 1 | bytes 1 | tf_op jit(solution)/shard_map/pallas_call | solution.py:292
  15.5 3.9 %collective-permute-done.sent_ref = f32[512,128]{1,0:T(8,128)S(1)} collective-permute-done((f32[512,128]{1,0:T(8,128)S(1)}, f32[512,128]{1,0:T(8,128)S(1)}, u32[]{:S(2)}, u32[]{:S(2)}) %collective-permute-start) | collective-permute-done | bytes 262176 | tf_op jit(solution)/shard_map/ppermute | solution.py:275
  19.4 4.2 %shard_map.75 = f32[1024,512]{1,0:T(8,128)} custom-call(f32[512,128]{1,0:T(8,128)S(1)} %collective-permute-done.sent_ref, f32[1,1664]{1,0:T(1,128)S(1)} %broadcast_in_dim.3.vectors_ref, bf16[512,1536]{1,0:T(8,128)(2,1)S(1)} %get-tuple-element.22.factor_left_ref, bf16[1024,512]{1,0:T(8,128)(2,1)S(1)} %get-tuple-element.23.left_ref, ...), custom_call_target="tpu_custom_call" | custom-call | flops 4000000000 | bytes 8000000 | tf_op jit(solution)/shard_map/pallas_call | solution.py:300
  (3 shorter events, 0.0 us)
Async XLA Ops:
  0.0 11.6 %copy-start = (f32[1024,128]{1,0:T(8,128)S(1)}, f32[1024,128]{1,0:T(8,128)}, u32[]{:S(2)}) copy-start(f32[1024,128]{1,0:T(8,128)} %points_ref.1) | copy-start | bytes 1572868
  0.0 11.6 %copy-start.1 = (f32[512,512]{1,0:T(8,128)S(1)}, f32[512,512]{1,0:T(8,128)}, u32[]{:S(2)}) copy-start(f32[512,512]{1,0:T(8,128)} %factor_ref.1) | copy-start | bytes 3145732
  0.0 1.7 %collective-permute-start.1 = (f32[512,128]{1,0:T(8,128)}, f32[512,128]{1,0:T(8,128)S(1)}, u32[]{:S(2)}, u32[]{:S(2)}) collective-permute-start(f32[512,128]{1,0:T(8,128)} %param.8), channel_id=1, source_target_pairs={{0,1},{1,0},{2,3},{3,2},{4,5},{5,4},{6,7},{7,6},{8,9},{9,8},{10,11... | collective-permute-start | bytes 786440 | tf_op jit(solution)/shard_map/ppermute | solution.py:240
  1.8 7.3 %collective-permute-start.2 = (f32[256,128]{1,0:T(8,128)S(1)}, f32[256,128]{1,0:T(8,128)S(1)}, u32[]{:S(2)}, u32[]{:S(2)}) collective-permute-start(f32[256,128]{1,0:T(8,128)S(1)} %dynamic-slice_select_fusion), channel_id=1, source_target_pairs={{0,6},{1,7},{2,4},{3,5},{4,2},{5,3},{6,0},{7,1},{8,14},{9,15},{10,... | collective-permute-start | bytes 393224 | tf_op jit(solution)/shard_map/ppermute | solution.py:240
  3.3 8.2 %collective-permute-start.3 = (f32[256,128]{1,0:T(8,128)S(1)}, f32[256,128]{1,0:T(8,128)S(1)}, u32[]{:S(2)}, u32[]{:S(2)}) collective-permute-start(f32[256,128]{1,0:T(8,128)S(1)} %dynamic-slice_select_fusion), channel_id=1, source_target_pairs={{0,4},{1,5},{2,6},{3,7},{4,0},{5,1},{6,2},{7,3},{8,12},{9,13},{10,... | collective-permute-start | bytes 393224 | tf_op jit(solution)/shard_map/ppermute | solution.py:240
  4.8 6.7 %collective-permute-start.4 = (f32[256,128]{1,0:T(8,128)S(1)}, f32[256,128]{1,0:T(8,128)S(1)}, u32[]{:S(2)}, u32[]{:S(2)}) collective-permute-start(f32[256,128]{1,0:T(8,128)S(1)} %dynamic-slice_select_fusion), channel_id=1, source_target_pairs={{0,2},{1,3},{2,0},{3,1},{4,6},{5,7},{6,4},{7,5},{8,10},{9,11},{10,... | collective-permute-start | bytes 393224 | tf_op jit(solution)/shard_map/ppermute | solution.py:240
  6.3 13.1 %collective-permute-start = (f32[512,128]{1,0:T(8,128)S(1)}, f32[512,128]{1,0:T(8,128)S(1)}, u32[]{:S(2)}, u32[]{:S(2)}) collective-permute-start(f32[512,128]{1,0:T(8,128)S(1)} %constant_dynamic-slice_fusion.1), channel_id=1, source_target_pairs={{4,1},{0,9},{6,17},{2,25},{10,3},{14,11},{12,19},{8,27},{18,5},{16... | collective-permute-start | bytes 786440 | tf_op jit(solution)/shard_map/ppermute | solution.py:275
  11.5 1.4 %collective-permute-start.5 = (f32[256,128]{1,0:T(8,128)S(1)}, f32[256,128]{1,0:T(8,128)S(1)}, u32[]{:S(2)}, u32[]{:S(2)}) collective-permute-start(f32[256,128]{1,0:T(8,128)S(1)} %select_select_fusion.own_ref), channel_id=1, source_target_pairs={{0,1},{1,0},{2,3},{3,2},{4,5},{5,4},{6,7},{7,6},{8,9},{9,8},{10,11... | collective-permute-start | bytes 393224 | tf_op jit(solution)/shard_map/ppermute | solution.py:240

commit v10 on v8

--- a/solution.py
+++ b/solution.py
@@ -98,7 +98,7 @@
     high, low = turned[:features].astype(bf16), turned[features:].astype(bf16)
     right = pack_right(high, low)
     right_half = half_square(high, low, 0)
-    chunks = 2
+    chunks = 4
     count = left_ref.shape[0] // chunks
     places = [slice(number * count, (number + 1) * count) for number in range(chunks)]
     crossed = [product(left_ref[place, :], right) for place in places]
@@ -287,7 +287,7 @@
         **compute_params(1, 1),
     )(*pieces, vectors, factor_right, pick, left, left_half)
 
-    chunks = 4
+    chunks = 8
     return pl.pallas_call(
         functools.partial(update_kernel, rows, cols),
         out_shape=shape((row_count, col_count)),

time: 22.9 us -> 22.7 us (level)
  no operation moved by 1% of the time
where the time goes in v10:
time: 22.7 us; the launch traced here: 22.4 us
  Pallas kernels  7.26 us (32%)
  starting transfers between devices  5.73 us (25%)
  waiting for transfers between devices  5.38 us (24%)
  local copies, waits for them, and re-layouts  1.9 us (8%)
  other arithmetic  1.42 us (6%)
  between operations  0.75 us (3%)
    ppermute x5, waiting for transfers between devices, swap(): return lax.ppermute(value, 'col', [(i, i ^ bit) for i in range(cols)])  5.37 us
    pallas_call x1, Pallas kernels, on_device(): pl.pallas_call(functools.partial(update_kernel, rows, cols), out_shape=sh...  4.16 us
    ppermute x5, starting transfers between devices, swap(): return lax.ppermute(value, 'col', [(i, i ^ bit) for i in range(cols)])  3.94 us
    pallas_call x1, Pallas kernels, on_device(): pl.pallas_call(rows_kernel, out_shape=[shape((row_count, 3 * panel), bf16...  2.36 us
    ppermute x1, starting transfers between devices, on_device(): sent = lax.ppermute(own_half, ('row', 'col'), column_pairs(rows, cols))  1.79 us
    dynamic_slice x1, local copies, waits for them, and re-layouts, on_device(): own_half = lax.dynamic_slice_in_dim(points, part * col_count, col_count, 0)  0.97 us
    dynamic_slice x1, local copies, waits for them, and re-layouts, gather_panel(): mine = lax.dynamic_slice_in_dim(panel_pool, core * half_rows, half_rows, 0)  0.92 us
    pallas_call x1, Pallas kernels, on_device(): pl.pallas_call(parts_kernel, out_shape=[shape((panel, 3 * panel), bf16),...  0.74 us
  transfers between devices with their start and end apart: 6, of which 2 were waited for; matrix products, arithmetic and copies ran while one was open for 15% of the time, Pallas kernels for 14%

profile of v10, /device:TPU:29, one launch (start us, length us, event | category | flops | bytes accessed | tf_op | source)
XLA Modules:
  0.0 22.4 jit_solution(4386055528169094348)
XLA Ops:
  0.0 0.0 copy-start
  0.0 0.0 copy-start.1
  0.0 0.7 %collective-permute-start.1 = (f32[512,128]{1,0:T(8,128)}, f32[512,128]{1,0:T(8,128)S(1)}, u32[]{:S(2)}, u32[]{:S(2)}) collective-permute-start(f32[512,128]{1,0:T(8,128)} %param.8), channel_id=1, source_target_pairs={{0,1},{1,0},{2,3},{3,2},{4,5},{5,4},{6,7},{7,6},{8,9},{9,8},{10,11... | collective-permute-start | bytes 786440 | tf_op jit(solution)/shard_map/ppermute | solution.py:231
  1.4 0.9 %constant_dynamic-slice_fusion = f32[256,128]{1,0:T(8,128)S(1)} fusion(f32[512,128]{1,0:T(8,128)} %param.8, s32[]{:T(128)S(6)} %select_n.50), kind=kLoop, calls=%fused_computation.3 | loop fusion | bytes 262148 | tf_op jit(solution)/shard_map/dynamic_slice | solution.py:238
  2.3 0.0 collective-permute-done.1
  2.3 1.2 %collective-permute-start.2 = (f32[256,128]{1,0:T(8,128)S(1)}, f32[256,128]{1,0:T(8,128)S(1)}, u32[]{:S(2)}, u32[]{:S(2)}) collective-permute-start(f32[256,128]{1,0:T(8,128)S(1)} %dynamic-slice_select_fusion), channel_id=1, source_target_pairs={{0,6},{1,7},{2,4},{3,5},{4,2},{5,3},{6,0},{7,1},{8,14},{9,15},{10,... | collective-permute-start | bytes 393224 | tf_op jit(solution)/shard_map/ppermute | solution.py:231
  3.5 1.2 %collective-permute-start.3 = (f32[256,128]{1,0:T(8,128)S(1)}, f32[256,128]{1,0:T(8,128)S(1)}, u32[]{:S(2)}, u32[]{:S(2)}) collective-permute-start(f32[256,128]{1,0:T(8,128)S(1)} %dynamic-slice_select_fusion), channel_id=1, source_target_pairs={{0,4},{1,5},{2,6},{3,7},{4,0},{5,1},{6,2},{7,3},{8,12},{9,13},{10,... | collective-permute-start | bytes 393224 | tf_op jit(solution)/shard_map/ppermute | solution.py:231
  4.8 0.3 %collective-permute-start.4 = (f32[256,128]{1,0:T(8,128)S(1)}, f32[256,128]{1,0:T(8,128)S(1)}, u32[]{:S(2)}, u32[]{:S(2)}) collective-permute-start(f32[256,128]{1,0:T(8,128)S(1)} %dynamic-slice_select_fusion), channel_id=1, source_target_pairs={{0,2},{1,3},{2,0},{3,1},{4,6},{5,7},{6,4},{7,5},{8,10},{9,11},{10,... | collective-permute-start | bytes 393224 | tf_op jit(solution)/shard_map/ppermute | solution.py:231
  5.0 1.0 %constant_dynamic-slice_fusion.1 = f32[512,128]{1,0:T(8,128)S(1)} fusion(f32[1024,128]{1,0:T(8,128)} %points_ref.1, s32[]{:T(128)S(6)} %select_n.47), kind=kLoop, calls=%fused_computation.4 | loop fusion | bytes 524292 | tf_op jit(solution)/shard_map/dynamic_slice | solution.py:265
  6.0 1.8 %collective-permute-start = (f32[512,128]{1,0:T(8,128)S(1)}, f32[512,128]{1,0:T(8,128)S(1)}, u32[]{:S(2)}, u32[]{:S(2)}) collective-permute-start(f32[512,128]{1,0:T(8,128)S(1)} %constant_dynamic-slice_fusion.1), channel_id=1, source_target_pairs={{4,1},{6,9},{0,17},{2,25},{8,3},{10,11},{12,19},{14,27},{22,5},{18... | collective-permute-start | bytes 786440 | tf_op jit(solution)/shard_map/ppermute | solution.py:266
  7.8 0.7 %convert_element_type.3 = f32[512]{0:T(512)S(1)} convert(s32[512]{0:T(512)} %param.9) | non-fusion elementwise | flops 512 | bytes 4096 | tf_op jit(solution)/shard_map/convert_element_type | solution.py:267
  8.5 0.7 %pad_maximum_fusion = f32[1664]{0:T(1024)S(1)} fusion(f32[1024]{0:T(1024)} %param.13, f32[128]{0:T(128)} %param.12, f32[512]{0:T(512)S(1)} %convert_element_type.3), kind=kLoop, calls=%fused_computation.2 | loop fusion | flops 3328 | bytes 13312 | tf_op jit(solution)/shard_map/concatenate | solution.py:267
  9.2 0.0 collective-permute-done.2
  9.2 5.1 %collective-permute-done.3 = f32[256,128]{1,0:T(8,128)S(1)} collective-permute-done((f32[256,128]{1,0:T(8,128)S(1)}, f32[256,128]{1,0:T(8,128)S(1)}, u32[]{:S(2)}, u32[]{:S(2)}) %collective-permute-start.3) | collective-permute-done | bytes 131104 | tf_op jit(solution)/shard_map/ppermute | solution.py:231
  14.3 0.0 collective-permute-done.4
  14.4 0.5 %collective-permute-start.5 = (f32[256,128]{1,0:T(8,128)S(1)}, f32[256,128]{1,0:T(8,128)S(1)}, u32[]{:S(2)}, u32[]{:S(2)}) collective-permute-start(f32[256,128]{1,0:T(8,128)S(1)} %select_select_fusion.own_ref), channel_id=1, source_target_pairs={{0,1},{1,0},{2,3},{3,2},{4,5},{5,4},{6,7},{7,6},{8,9},{9,8},{10,11... | collective-permute-start | bytes 393224 | tf_op jit(solution)/shard_map/ppermute | solution.py:231
  14.9 0.0 copy-done
  14.9 0.0 copy-done.1
  14.9 0.7 %shard_map.73 = (bf16[512,1536]{1,0:T(8,128)(2,1)S(1)}, bf16[1536,512]{1,0:T(8,128)(2,1)S(1)}, bf16[512,512]{1,0:T(8,128)(2,1)S(1)}, bf16[1024,512]{1,0:T(8,128)(2,1)S(1)}, f32[1024,1]{1,0:T(8,128)S(1)}) custom-call(f32[512,512]{1,0:T(8,128)S(1)} %copy-done.1, f32[1024,128]{1,0:T(8,128)S(1)} %copy-done, f32[1,1664]{1,0:T(1,128)S(1)} %broadcast_in_dim.3.vectors_ref), custom_call_target="tpu_custom_call" | custom-call | flops 100000000 | bytes 4000000 | tf_op jit(solution)/shard_map/pallas_call | solution.py:271
  15.7 0.2 %collective-permute-done.5.other_ref = f32[256,128]{1,0:T(8,128)S(1)} collective-permute-done((f32[256,128]{1,0:T(8,128)S(1)}, f32[256,128]{1,0:T(8,128)S(1)}, u32[]{:S(2)}, u32[]{:S(2)}) %collective-permute-start.5) | collective-permute-done | bytes 131104 | tf_op jit(solution)/shard_map/ppermute | solution.py:231
  15.9 2.4 %shard_map.74 = (bf16[1024,1536]{1,0:T(8,128)(2,1)S(1)}, bf16[512,512]{1,0:T(8,128)(2,1)S(1)}, f32[512,1]{1,0:T(8,128)S(1)}) custom-call(f32[256,128]{1,0:T(8,128)S(1)} %select_select_fusion.own_ref, f32[256,128]{1,0:T(8,128)S(1)} %collective-permute-done.5.other_ref, f32[1,1664]{1,0:T(1,128)S(1)} %broadcast_in_dim.3.vectors_ref, ...), custom_call_target="tpu_custom_call" | custom-call | flops 1 | bytes 1 | tf_op jit(solution)/shard_map/pallas_call | solution.py:283
  18.3 0.0 collective-permute-done.sent_ref
  18.3 4.2 %shard_map.75 = f32[1024,512]{1,0:T(8,128)} custom-call(f32[512,128]{1,0:T(8,128)S(1)} %collective-permute-done.sent_ref, f32[1,1664]{1,0:T(1,128)S(1)} %broadcast_in_dim.3.vectors_ref, bf16[512,1536]{1,0:T(8,128)(2,1)S(1)} %get-tuple-element.22.factor_left_ref, bf16[1024,512]{1,0:T(8,128)(2,1)S(1)} %get-tuple-element.23.left_ref, ...), custom_call_target="tpu_custom_call" | custom-call | flops 4000000000 | bytes 8000000 | tf_op jit(solution)/shard_map/pallas_call | solution.py:291
  (3 shorter events, 0.1 us)
Async XLA Ops:
  0.0 14.9 %copy-start = (f32[1024,128]{1,0:T(8,128)S(1)}, f32[1024,128]{1,0:T(8,128)}, u32[]{:S(2)}) copy-start(f32[1024,128]{1,0:T(8,128)} %points_ref.1) | copy-start | bytes 1572868
  0.0 14.9 %copy-start.1 = (f32[512,512]{1,0:T(8,128)S(1)}, f32[512,512]{1,0:T(8,128)}, u32[]{:S(2)}) copy-start(f32[512,512]{1,0:T(8,128)} %factor_ref.1) | copy-start | bytes 3145732
  0.0 2.3 %collective-permute-start.1 = (f32[512,128]{1,0:T(8,128)}, f32[512,128]{1,0:T(8,128)S(1)}, u32[]{:S(2)}, u32[]{:S(2)}) collective-permute-start(f32[512,128]{1,0:T(8,128)} %param.8), channel_id=1, source_target_pairs={{0,1},{1,0},{2,3},{3,2},{4,5},{5,4},{6,7},{7,6},{8,9},{9,8},{10,11... | collective-permute-start | bytes 786440 | tf_op jit(solution)/shard_map/ppermute | solution.py:231
  2.3 6.9 %collective-permute-start.2 = (f32[256,128]{1,0:T(8,128)S(1)}, f32[256,128]{1,0:T(8,128)S(1)}, u32[]{:S(2)}, u32[]{:S(2)}) collective-permute-start(f32[256,128]{1,0:T(8,128)S(1)} %dynamic-slice_select_fusion), channel_id=1, source_target_pairs={{0,6},{1,7},{2,4},{3,5},{4,2},{5,3},{6,0},{7,1},{8,14},{9,15},{10,... | collective-permute-start | bytes 393224 | tf_op jit(solution)/shard_map/ppermute | solution.py:231
  3.5 10.8 %collective-permute-start.3 = (f32[256,128]{1,0:T(8,128)S(1)}, f32[256,128]{1,0:T(8,128)S(1)}, u32[]{:S(2)}, u32[]{:S(2)}) collective-permute-start(f32[256,128]{1,0:T(8,128)S(1)} %dynamic-slice_select_fusion), channel_id=1, source_target_pairs={{0,4},{1,5},{2,6},{3,7},{4,0},{5,1},{6,2},{7,3},{8,12},{9,13},{10,... | collective-permute-start | bytes 393224 | tf_op jit(solution)/shard_map/ppermute | solution.py:231
  4.8 9.6 %collective-permute-start.4 = (f32[256,128]{1,0:T(8,128)S(1)}, f32[256,128]{1,0:T(8,128)S(1)}, u32[]{:S(2)}, u32[]{:S(2)}) collective-permute-start(f32[256,128]{1,0:T(8,128)S(1)} %dynamic-slice_select_fusion), channel_id=1, source_target_pairs={{0,2},{1,3},{2,0},{3,1},{4,6},{5,7},{6,4},{7,5},{8,10},{9,11},{10,... | collective-permute-start | bytes 393224 | tf_op jit(solution)/shard_map/ppermute | solution.py:231
  6.0 12.3 %collective-permute-start = (f32[512,128]{1,0:T(8,128)S(1)}, f32[512,128]{1,0:T(8,128)S(1)}, u32[]{:S(2)}, u32[]{:S(2)}) collective-permute-start(f32[512,128]{1,0:T(8,128)S(1)} %constant_dynamic-slice_fusion.1), channel_id=1, source_target_pairs={{4,1},{6,9},{0,17},{2,25},{8,3},{10,11},{12,19},{14,27},{22,5},{18... | collective-permute-start | bytes 786440 | tf_op jit(solution)/shard_map/ppermute | solution.py:266
  14.4 1.5 %collective-permute-start.5 = (f32[256,128]{1,0:T(8,128)S(1)}, f32[256,128]{1,0:T(8,128)S(1)}, u32[]{:S(2)}, u32[]{:S(2)}) collective-permute-start(f32[256,128]{1,0:T(8,128)S(1)} %select_select_fusion.own_ref), channel_id=1, source_target_pairs={{0,1},{1,0},{2,3},{3,2},{4,5},{5,4},{6,7},{7,6},{8,9},{9,8},{10,11... | collective-permute-start | bytes 393224 | tf_op jit(solution)/shard_map/ppermute | solution.py:231

commit v11 on v10

--- a/solution.py
+++ b/solution.py
@@ -98,7 +98,7 @@
     high, low = turned[:features].astype(bf16), turned[features:].astype(bf16)
     right = pack_right(high, low)
     right_half = half_square(high, low, 0)
-    chunks = 4
+    chunks = 8
     count = left_ref.shape[0] // chunks
     places = [slice(number * count, (number + 1) * count) for number in range(chunks)]
     crossed = [product(left_ref[place, :], right) for place in places]
@@ -131,11 +131,12 @@
     ids = (square, square)
     on_diagonal = lax.broadcasted_iota(jnp.int32, ids, 0) == lax.broadcasted_iota(jnp.int32, ids, 1)
 
-    crossed = product(chosen_ref[...], right)
+    blocks = [slice(first, first + block) for first in range(0, panel, block)]
+    crossed = [product(chosen_ref[place, :], right) for place in blocks]
     tiles = [product(left_ref[place, :], right) for place in places]
-    store_right(kern_ref, 0, kern(crossed, chosen_half_ref[...], right_half))
-    for first in range(0, panel, block):
-        last = first + block
+    for number, place in enumerate(blocks):
+        first, last = place.start, place.stop
+        store_right(kern_ref, first, kern(crossed[number], chosen_half_ref[place, :], right_half))
         store_right(cols_ref, first, product(factor_left_ref[first:last, : 3 * last], kern_ref[: 3 * last, :]))
     copies = []
     for number, place in enumerate(places):

time: 22.7 us -> 22.7 us (level)
  no operation moved by 1% of the time
where the time goes in v11:
time: 22.7 us; the launch traced here: 22.4 us
  Pallas kernels  7.26 us (32%)
  starting transfers between devices  5.73 us (25%)
  waiting for transfers between devices  5.38 us (24%)
  local copies, waits for them, and re-layouts  1.9 us (8%)
  other arithmetic  1.42 us (6%)
  between operations  0.75 us (3%)
    ppermute x5, waiting for transfers between devices, swap(): return lax.ppermute(value, 'col', [(i, i ^ bit) for i in range(cols)])  5.37 us
    pallas_call x1, Pallas kernels, on_device(): pl.pallas_call(functools.partial(update_kernel, rows, cols), out_shape=sh...  4.15 us
    ppermute x5, starting transfers between devices, swap(): return lax.ppermute(value, 'col', [(i, i ^ bit) for i in range(cols)])  3.94 us
    pallas_call x1, Pallas kernels, on_device(): pl.pallas_call(rows_kernel, out_shape=[shape((row_count, 3 * panel), bf16...  2.36 us
    ppermute x1, starting transfers between devices, on_device(): sent = lax.ppermute(own_half, ('row', 'col'), column_pairs(rows, cols))  1.79 us
    dynamic_slice x1, local copies, waits for them, and re-layouts, on_device(): own_half = lax.dynamic_slice_in_dim(points, part * col_count, col_count, 0)  0.97 us
    dynamic_slice x1, local copies, waits for them, and re-layouts, gather_panel(): mine = lax.dynamic_slice_in_dim(panel_pool, core * half_rows, half_rows, 0)  0.92 us
    pallas_call x1, Pallas kernels, on_device(): pl.pallas_call(parts_kernel, out_shape=[shape((panel, 3 * panel), bf16),...  0.74 us
  transfers between devices with their start and end apart: 6, of which 2 were waited for; matrix products, arithmetic and copies ran while one was open for 15% of the time, Pallas kernels for 14%

profile of v11, /device:TPU:29, one launch (start us, length us, event | category | flops | bytes accessed | tf_op | source)
XLA Modules:
  0.0 22.4 jit_solution(3587801653110964105)
XLA Ops:
  0.0 0.0 copy-start
  0.0 0.0 copy-start.1
  0.0 0.7 %collective-permute-start.1 = (f32[512,128]{1,0:T(8,128)}, f32[512,128]{1,0:T(8,128)S(1)}, u32[]{:S(2)}, u32[]{:S(2)}) collective-permute-start(f32[512,128]{1,0:T(8,128)} %param.8), channel_id=1, source_target_pairs={{0,1},{1,0},{2,3},{3,2},{4,5},{5,4},{6,7},{7,6},{8,9},{9,8},{10,11... | collective-permute-start | bytes 786440 | tf_op jit(solution)/shard_map/ppermute | solution.py:232
  1.4 0.9 %constant_dynamic-slice_fusion = f32[256,128]{1,0:T(8,128)S(1)} fusion(f32[512,128]{1,0:T(8,128)} %param.8, s32[]{:T(128)S(6)} %select_n.50), kind=kLoop, calls=%fused_computation.3 | loop fusion | bytes 262148 | tf_op jit(solution)/shard_map/dynamic_slice | solution.py:239
  2.3 0.0 collective-permute-done.1
  2.3 1.2 %collective-permute-start.2 = (f32[256,128]{1,0:T(8,128)S(1)}, f32[256,128]{1,0:T(8,128)S(1)}, u32[]{:S(2)}, u32[]{:S(2)}) collective-permute-start(f32[256,128]{1,0:T(8,128)S(1)} %dynamic-slice_select_fusion), channel_id=1, source_target_pairs={{0,6},{1,7},{2,4},{3,5},{4,2},{5,3},{6,0},{7,1},{8,14},{9,15},{10,... | collective-permute-start | bytes 393224 | tf_op jit(solution)/shard_map/ppermute | solution.py:232
  3.5 1.2 %collective-permute-start.3 = (f32[256,128]{1,0:T(8,128)S(1)}, f32[256,128]{1,0:T(8,128)S(1)}, u32[]{:S(2)}, u32[]{:S(2)}) collective-permute-start(f32[256,128]{1,0:T(8,128)S(1)} %dynamic-slice_select_fusion), channel_id=1, source_target_pairs={{0,4},{1,5},{2,6},{3,7},{4,0},{5,1},{6,2},{7,3},{8,12},{9,13},{10,... | collective-permute-start | bytes 393224 | tf_op jit(solution)/shard_map/ppermute | solution.py:232
  4.8 0.3 %collective-permute-start.4 = (f32[256,128]{1,0:T(8,128)S(1)}, f32[256,128]{1,0:T(8,128)S(1)}, u32[]{:S(2)}, u32[]{:S(2)}) collective-permute-start(f32[256,128]{1,0:T(8,128)S(1)} %dynamic-slice_select_fusion), channel_id=1, source_target_pairs={{0,2},{1,3},{2,0},{3,1},{4,6},{5,7},{6,4},{7,5},{8,10},{9,11},{10,... | collective-permute-start | bytes 393224 | tf_op jit(solution)/shard_map/ppermute | solution.py:232
  5.0 1.0 %constant_dynamic-slice_fusion.1 = f32[512,128]{1,0:T(8,128)S(1)} fusion(f32[1024,128]{1,0:T(8,128)} %points_ref.1, s32[]{:T(128)S(6)} %select_n.47), kind=kLoop, calls=%fused_computation.4 | loop fusion | bytes 524292 | tf_op jit(solution)/shard_map/dynamic_slice | solution.py:266
  6.0 1.8 %collective-permute-start = (f32[512,128]{1,0:T(8,128)S(1)}, f32[512,128]{1,0:T(8,128)S(1)}, u32[]{:S(2)}, u32[]{:S(2)}) collective-permute-start(f32[512,128]{1,0:T(8,128)S(1)} %constant_dynamic-slice_fusion.1), channel_id=1, source_target_pairs={{4,1},{6,9},{0,17},{2,25},{8,3},{10,11},{12,19},{14,27},{22,5},{18... | collective-permute-start | bytes 786440 | tf_op jit(solution)/shard_map/ppermute | solution.py:267
  7.8 0.7 %convert_element_type.3 = f32[512]{0:T(512)S(1)} convert(s32[512]{0:T(512)} %param.9) | non-fusion elementwise | flops 512 | bytes 4096 | tf_op jit(solution)/shard_map/convert_element_type | solution.py:268
  8.5 0.7 %pad_maximum_fusion = f32[1664]{0:T(1024)S(1)} fusion(f32[1024]{0:T(1024)} %param.13, f32[128]{0:T(128)} %param.12, f32[512]{0:T(512)S(1)} %convert_element_type.3), kind=kLoop, calls=%fused_computation.2 | loop fusion | flops 3328 | bytes 13312 | tf_op jit(solution)/shard_map/concatenate | solution.py:268
  9.2 0.0 collective-permute-done.2
  9.2 5.1 %collective-permute-done.3 = f32[256,128]{1,0:T(8,128)S(1)} collective-permute-done((f32[256,128]{1,0:T(8,128)S(1)}, f32[256,128]{1,0:T(8,128)S(1)}, u32[]{:S(2)}, u32[]{:S(2)}) %collective-permute-start.3) | collective-permute-done | bytes 131104 | tf_op jit(solution)/shard_map/ppermute | solution.py:232
  14.3 0.0 collective-permute-done.4
  14.4 0.5 %collective-permute-start.5 = (f32[256,128]{1,0:T(8,128)S(1)}, f32[256,128]{1,0:T(8,128)S(1)}, u32[]{:S(2)}, u32[]{:S(2)}) collective-permute-start(f32[256,128]{1,0:T(8,128)S(1)} %select_select_fusion.own_ref), channel_id=1, source_target_pairs={{0,1},{1,0},{2,3},{3,2},{4,5},{5,4},{6,7},{7,6},{8,9},{9,8},{10,11... | collective-permute-start | bytes 393224 | tf_op jit(solution)/shard_map/ppermute | solution.py:232
  14.9 0.0 copy-done
  14.9 0.0 copy-done.1
  14.9 0.7 %shard_map.73 = (bf16[512,1536]{1,0:T(8,128)(2,1)S(1)}, bf16[1536,512]{1,0:T(8,128)(2,1)S(1)}, bf16[512,512]{1,0:T(8,128)(2,1)S(1)}, bf16[1024,512]{1,0:T(8,128)(2,1)S(1)}, f32[1024,1]{1,0:T(8,128)S(1)}) custom-call(f32[512,512]{1,0:T(8,128)S(1)} %copy-done.1, f32[1024,128]{1,0:T(8,128)S(1)} %copy-done, f32[1,1664]{1,0:T(1,128)S(1)} %broadcast_in_dim.3.vectors_ref), custom_call_target="tpu_custom_call" | custom-call | flops 100000000 | bytes 4000000 | tf_op jit(solution)/shard_map/pallas_call | solution.py:272
  15.7 0.2 %collective-permute-done.5.other_ref = f32[256,128]{1,0:T(8,128)S(1)} collective-permute-done((f32[256,128]{1,0:T(8,128)S(1)}, f32[256,128]{1,0:T(8,128)S(1)}, u32[]{:S(2)}, u32[]{:S(2)}) %collective-permute-start.5) | collective-permute-done | bytes 131104 | tf_op jit(solution)/shard_map/ppermute | solution.py:232
  15.9 2.4 %shard_map.74 = (bf16[1024,1536]{1,0:T(8,128)(2,1)S(1)}, bf16[512,512]{1,0:T(8,128)(2,1)S(1)}, f32[512,1]{1,0:T(8,128)S(1)}) custom-call(f32[256,128]{1,0:T(8,128)S(1)} %select_select_fusion.own_ref, f32[256,128]{1,0:T(8,128)S(1)} %collective-permute-done.5.other_ref, f32[1,1664]{1,0:T(1,128)S(1)} %broadcast_in_dim.3.vectors_ref, ...), custom_call_target="tpu_custom_call" | custom-call | flops 1 | bytes 1 | tf_op jit(solution)/shard_map/pallas_call | solution.py:284
  18.3 0.0 collective-permute-done.sent_ref
  18.3 4.2 %shard_map.75 = f32[1024,512]{1,0:T(8,128)} custom-call(f32[512,128]{1,0:T(8,128)S(1)} %collective-permute-done.sent_ref, f32[1,1664]{1,0:T(1,128)S(1)} %broadcast_in_dim.3.vectors_ref, bf16[512,1536]{1,0:T(8,128)(2,1)S(1)} %get-tuple-element.22.factor_left_ref, bf16[1024,512]{1,0:T(8,128)(2,1)S(1)} %get-tuple-element.23.left_ref, ...), custom_call_target="tpu_custom_call" | custom-call | flops 4000000000 | bytes 8000000 | tf_op jit(solution)/shard_map/pallas_call | solution.py:292
  (3 shorter events, 0.1 us)
Async XLA Ops:
  0.0 14.9 %copy-start = (f32[1024,128]{1,0:T(8,128)S(1)}, f32[1024,128]{1,0:T(8,128)}, u32[]{:S(2)}) copy-start(f32[1024,128]{1,0:T(8,128)} %points_ref.1) | copy-start | bytes 1572868
  0.0 14.9 %copy-start.1 = (f32[512,512]{1,0:T(8,128)S(1)}, f32[512,512]{1,0:T(8,128)}, u32[]{:S(2)}) copy-start(f32[512,512]{1,0:T(8,128)} %factor_ref.1) | copy-start | bytes 3145732
  0.0 2.3 %collective-permute-start.1 = (f32[512,128]{1,0:T(8,128)}, f32[512,128]{1,0:T(8,128)S(1)}, u32[]{:S(2)}, u32[]{:S(2)}) collective-permute-start(f32[512,128]{1,0:T(8,128)} %param.8), channel_id=1, source_target_pairs={{0,1},{1,0},{2,3},{3,2},{4,5},{5,4},{6,7},{7,6},{8,9},{9,8},{10,11... | collective-permute-start | bytes 786440 | tf_op jit(solution)/shard_map/ppermute | solution.py:232
  2.3 6.9 %collective-permute-start.2 = (f32[256,128]{1,0:T(8,128)S(1)}, f32[256,128]{1,0:T(8,128)S(1)}, u32[]{:S(2)}, u32[]{:S(2)}) collective-permute-start(f32[256,128]{1,0:T(8,128)S(1)} %dynamic-slice_select_fusion), channel_id=1, source_target_pairs={{0,6},{1,7},{2,4},{3,5},{4,2},{5,3},{6,0},{7,1},{8,14},{9,15},{10,... | collective-permute-start | bytes 393224 | tf_op jit(solution)/shard_map/ppermute | solution.py:232
  3.5 10.8 %collective-permute-start.3 = (f32[256,128]{1,0:T(8,128)S(1)}, f32[256,128]{1,0:T(8,128)S(1)}, u32[]{:S(2)}, u32[]{:S(2)}) collective-permute-start(f32[256,128]{1,0:T(8,128)S(1)} %dynamic-slice_select_fusion), channel_id=1, source_target_pairs={{0,4},{1,5},{2,6},{3,7},{4,0},{5,1},{6,2},{7,3},{8,12},{9,13},{10,... | collective-permute-start | bytes 393224 | tf_op jit(solution)/shard_map/ppermute | solution.py:232
  4.8 9.6 %collective-permute-start.4 = (f32[256,128]{1,0:T(8,128)S(1)}, f32[256,128]{1,0:T(8,128)S(1)}, u32[]{:S(2)}, u32[]{:S(2)}) collective-permute-start(f32[256,128]{1,0:T(8,128)S(1)} %dynamic-slice_select_fusion), channel_id=1, source_target_pairs={{0,2},{1,3},{2,0},{3,1},{4,6},{5,7},{6,4},{7,5},{8,10},{9,11},{10,... | collective-permute-start | bytes 393224 | tf_op jit(solution)/shard_map/ppermute | solution.py:232
  6.0 12.3 %collective-permute-start = (f32[512,128]{1,0:T(8,128)S(1)}, f32[512,128]{1,0:T(8,128)S(1)}, u32[]{:S(2)}, u32[]{:S(2)}) collective-permute-start(f32[512,128]{1,0:T(8,128)S(1)} %constant_dynamic-slice_fusion.1), channel_id=1, source_target_pairs={{4,1},{6,9},{0,17},{2,25},{8,3},{10,11},{12,19},{14,27},{22,5},{18... | collective-permute-start | bytes 786440 | tf_op jit(solution)/shard_map/ppermute | solution.py:267
  14.4 1.5 %collective-permute-start.5 = (f32[256,128]{1,0:T(8,128)S(1)}, f32[256,128]{1,0:T(8,128)S(1)}, u32[]{:S(2)}, u32[]{:S(2)}) collective-permute-start(f32[256,128]{1,0:T(8,128)S(1)} %select_select_fusion.own_ref), channel_id=1, source_target_pairs={{0,1},{1,0},{2,3},{3,2},{4,5},{5,4},{6,7},{7,6},{8,9},{9,8},{10,11... | collective-permute-start | bytes 393224 | tf_op jit(solution)/shard_map/ppermute | solution.py:232

commit v12 on v10

--- a/solution.py
+++ b/solution.py
@@ -244,11 +244,13 @@
     while low < cols:
         high = min(4 * low, cols)
         away = apart & (high - low)
-        steps = range(high - low, 0, -low)
-        received = [swap(held, bits, cols) for bits in steps]
+        steps = [(2 * low, 3 * low), (3 * low, 2 * low), (low, low)] if high == 4 * low else [(low, low)]
+        received = [
+            lax.ppermute(held, "col", [(i, i ^ step[i % 2]) for i in range(cols)]) for step in steps
+        ]
         received, beside = lax.optimization_barrier((received, beside))
-        for bits, value in zip(steps, received):
-            held = jnp.where(away == bits, value, held)
+        for step, value in zip(steps, received):
+            held = jnp.where(away == jnp.where(core == 0, step[0], step[1]), value, held)
         low = high
     return [held, swap(held, 1, cols)], beside
 

time: 22.7 us -> 22.3 us (0.982)
  starting transfers between devices: 5.73 us -> 5.27 us
    ppermute x0 -> x3, waiting for transfers between devices: none -> 4.92 us  [gather_panel(): lax.ppermute(held, 'col', [(i, i ^ step[i % 2]) for i in range(cols)])]
    ppermute x5 -> x2, waiting for transfers between devices: 5.37 us -> 0.56 us  [swap(): return lax.ppermute(value, 'col', [(i, i ^ bit) for i in range(cols)])]
    ppermute x5 -> x2, starting transfers between devices: 3.94 us -> 0.78 us  [swap(): return lax.ppermute(value, 'col', [(i, i ^ bit) for i in range(cols)])]
    ppermute x0 -> x3, starting transfers between devices: none -> 2.71 us  [gather_panel(): lax.ppermute(held, 'col', [(i, i ^ step[i % 2]) for i in range(cols)])]
where the time goes in v12:
time: 22.3 us; the launch traced here: 22.1 us
  Pallas kernels  7.26 us (33%)
  waiting for transfers between devices  5.48 us (25%)
  starting transfers between devices  5.27 us (24%)
  local copies, waits for them, and re-layouts  1.9 us (9%)
  other arithmetic  1.42 us (6%)
  between operations  0.76 us (3%)
    ppermute x3, waiting for transfers between devices, gather_panel(): lax.ppermute(held, 'col', [(i, i ^ step[i % 2]) for i in range(cols)])  4.92 us
    pallas_call x1, Pallas kernels, on_device(): pl.pallas_call(functools.partial(update_kernel, rows, cols), out_shape=sh...  4.16 us
    ppermute x3, starting transfers between devices, gather_panel(): lax.ppermute(held, 'col', [(i, i ^ step[i % 2]) for i in range(cols)])  2.71 us
    pallas_call x1, Pallas kernels, on_device(): pl.pallas_call(rows_kernel, out_shape=[shape((row_count, 3 * panel), bf16...  2.36 us
    ppermute x1, starting transfers between devices, on_device(): sent = lax.ppermute(own_half, ('row', 'col'), column_pairs(rows, cols))  1.77 us
    dynamic_slice x1, local copies, waits for them, and re-layouts, on_device(): own_half = lax.dynamic_slice_in_dim(points, part * col_count, col_count, 0)  0.97 us
    dynamic_slice x1, local copies, waits for them, and re-layouts, gather_panel(): mine = lax.dynamic_slice_in_dim(panel_pool, core * half_rows, half_rows, 0)  0.92 us
    ppermute x2, starting transfers between devices, swap(): return lax.ppermute(value, 'col', [(i, i ^ bit) for i in range(cols)])  0.78 us
  transfers between devices with their start and end apart: 6, of which 2 were waited for; matrix products, arithmetic and copies ran while one was open for 15% of the time, Pallas kernels for 14%

profile of v12, /device:TPU:29, one launch (start us, length us, event | category | flops | bytes accessed | tf_op | source)
XLA Modules:
  0.0 22.1 jit_solution(1925768558728188948)
XLA Ops:
  0.0 0.0 copy-start
  0.0 0.0 copy-start.1
  0.0 0.7 %collective-permute-start.1 = (f32[512,128]{1,0:T(8,128)}, f32[512,128]{1,0:T(8,128)S(1)}, u32[]{:S(2)}, u32[]{:S(2)}) collective-permute-start(f32[512,128]{1,0:T(8,128)} %param.8), channel_id=1, source_target_pairs={{0,1},{1,0},{2,3},{3,2},{4,5},{5,4},{6,7},{7,6},{8,9},{9,8},{10,11... | collective-permute-start | bytes 786440 | tf_op jit(solution)/shard_map/ppermute | solution.py:231
  1.4 0.9 %constant_dynamic-slice_fusion = f32[256,128]{1,0:T(8,128)S(1)} fusion(f32[512,128]{1,0:T(8,128)} %param.8, s32[]{:T(128)S(6)} %select_n.58), kind=kLoop, calls=%fused_computation.3 | loop fusion | bytes 262148 | tf_op jit(solution)/shard_map/dynamic_slice | solution.py:238
  2.3 0.0 collective-permute-done.1
  2.3 1.2 %collective-permute-start.2 = (f32[256,128]{1,0:T(8,128)S(1)}, f32[256,128]{1,0:T(8,128)S(1)}, u32[]{:S(2)}, u32[]{:S(2)}) collective-permute-start(f32[256,128]{1,0:T(8,128)S(1)} %dynamic-slice_select_fusion), channel_id=1, source_target_pairs={{0,4},{1,7},{2,6},{3,5},{4,0},{5,3},{6,2},{7,1},{8,12},{9,15},{10,... | collective-permute-start | bytes 393224 | tf_op jit(solution)/shard_map/ppermute | solution.py:249
  3.5 1.2 %collective-permute-start.3 = (f32[256,128]{1,0:T(8,128)S(1)}, f32[256,128]{1,0:T(8,128)S(1)}, u32[]{:S(2)}, u32[]{:S(2)}) collective-permute-start(f32[256,128]{1,0:T(8,128)S(1)} %dynamic-slice_select_fusion), channel_id=1, source_target_pairs={{0,6},{1,5},{2,4},{3,7},{4,2},{5,1},{6,0},{7,3},{8,14},{9,13},{10,... | collective-permute-start | bytes 393224 | tf_op jit(solution)/shard_map/ppermute | solution.py:249
  4.8 0.3 %collective-permute-start.4 = (f32[256,128]{1,0:T(8,128)S(1)}, f32[256,128]{1,0:T(8,128)S(1)}, u32[]{:S(2)}, u32[]{:S(2)}) collective-permute-start(f32[256,128]{1,0:T(8,128)S(1)} %dynamic-slice_select_fusion), channel_id=1, source_target_pairs={{0,2},{1,3},{2,0},{3,1},{4,6},{5,7},{6,4},{7,5},{8,10},{9,11},{10,... | collective-permute-start | bytes 393224 | tf_op jit(solution)/shard_map/ppermute | solution.py:249
  5.0 1.0 %constant_dynamic-slice_fusion.1 = f32[512,128]{1,0:T(8,128)S(1)} fusion(f32[1024,128]{1,0:T(8,128)} %points_ref.1, s32[]{:T(128)S(6)} %select_n.55), kind=kLoop, calls=%fused_computation.4 | loop fusion | bytes 524292 | tf_op jit(solution)/shard_map/dynamic_slice | solution.py:267
  6.0 1.8 %collective-permute-start = (f32[512,128]{1,0:T(8,128)S(1)}, f32[512,128]{1,0:T(8,128)S(1)}, u32[]{:S(2)}, u32[]{:S(2)}) collective-permute-start(f32[512,128]{1,0:T(8,128)S(1)} %constant_dynamic-slice_fusion.1), channel_id=1, source_target_pairs={{4,1},{6,9},{0,17},{2,25},{8,3},{10,11},{12,19},{14,27},{22,5},{18... | collective-permute-start | bytes 786440 | tf_op jit(solution)/shard_map/ppermute | solution.py:268
  7.8 0.7 %convert_element_type.3 = f32[512]{0:T(512)S(1)} convert(s32[512]{0:T(512)} %param.9) | non-fusion elementwise | flops 512 | bytes 4096 | tf_op jit(solution)/shard_map/convert_element_type | solution.py:269
  8.5 0.7 %pad_maximum_fusion = f32[1664]{0:T(1024)S(1)} fusion(f32[1024]{0:T(1024)} %param.13, f32[128]{0:T(128)} %param.12, f32[512]{0:T(512)S(1)} %convert_element_type.3), kind=kLoop, calls=%fused_computation.2 | loop fusion | flops 3328 | bytes 13312 | tf_op jit(solution)/shard_map/concatenate | solution.py:269
  9.2 0.0 collective-permute-done.2
  9.2 4.9 %collective-permute-done.3 = f32[256,128]{1,0:T(8,128)S(1)} collective-permute-done((f32[256,128]{1,0:T(8,128)S(1)}, f32[256,128]{1,0:T(8,128)S(1)}, u32[]{:S(2)}, u32[]{:S(2)}) %collective-permute-start.3) | collective-permute-done | bytes 131104 | tf_op jit(solution)/shard_map/ppermute | solution.py:249
  14.1 0.0 collective-permute-done.4
  14.1 0.1 collective-permute-start.5
  14.3 0.0 copy-done
  14.3 0.0 copy-done.1
  14.3 0.7 %shard_map.73 = (bf16[512,1536]{1,0:T(8,128)(2,1)S(1)}, bf16[1536,512]{1,0:T(8,128)(2,1)S(1)}, bf16[512,512]{1,0:T(8,128)(2,1)S(1)}, bf16[1024,512]{1,0:T(8,128)(2,1)S(1)}, f32[1024,1]{1,0:T(8,128)S(1)}) custom-call(f32[512,512]{1,0:T(8,128)S(1)} %copy-done.1, f32[1024,128]{1,0:T(8,128)S(1)} %copy-done, f32[1,1664]{1,0:T(1,128)S(1)} %broadcast_in_dim.3.vectors_ref), custom_call_target="tpu_custom_call" | custom-call | flops 100000000 | bytes 4000000 | tf_op jit(solution)/shard_map/pallas_call | solution.py:273
  15.0 0.6 %collective-permute-done.5.other_ref = f32[256,128]{1,0:T(8,128)S(1)} collective-permute-done((f32[256,128]{1,0:T(8,128)S(1)}, f32[256,128]{1,0:T(8,128)S(1)}, u32[]{:S(2)}, u32[]{:S(2)}) %collective-permute-start.5) | collective-permute-done | bytes 131104 | tf_op jit(solution)/shard_map/ppermute | solution.py:231
  15.6 2.4 %shard_map.74 = (bf16[1024,1536]{1,0:T(8,128)(2,1)S(1)}, bf16[512,512]{1,0:T(8,128)(2,1)S(1)}, f32[512,1]{1,0:T(8,128)S(1)}) custom-call(f32[256,128]{1,0:T(8,128)S(1)} %select_select_fusion.own_ref, f32[256,128]{1,0:T(8,128)S(1)} %collective-permute-done.5.other_ref, f32[1,1664]{1,0:T(1,128)S(1)} %broadcast_in_dim.3.vectors_ref, ...), custom_call_target="tpu_custom_call" | custom-call | flops 1 | bytes 1 | tf_op jit(solution)/shard_map/pallas_call | solution.py:285
  17.9 0.0 collective-permute-done.sent_ref
  17.9 4.2 %shard_map.75 = f32[1024,512]{1,0:T(8,128)} custom-call(f32[512,128]{1,0:T(8,128)S(1)} %collective-permute-done.sent_ref, f32[1,1664]{1,0:T(1,128)S(1)} %broadcast_in_dim.3.vectors_ref, bf16[512,1536]{1,0:T(8,128)(2,1)S(1)} %get-tuple-element.22.factor_left_ref, bf16[1024,512]{1,0:T(8,128)(2,1)S(1)} %get-tuple-element.23.left_ref, ...), custom_call_target="tpu_custom_call" | custom-call | flops 4000000000 | bytes 8000000 | tf_op jit(solution)/shard_map/pallas_call | solution.py:293
  (3 shorter events, 0.1 us)
Async XLA Ops:
  0.0 14.3 %copy-start = (f32[1024,128]{1,0:T(8,128)S(1)}, f32[1024,128]{1,0:T(8,128)}, u32[]{:S(2)}) copy-start(f32[1024,128]{1,0:T(8,128)} %points_ref.1) | copy-start | bytes 1572868
  0.0 14.3 %copy-start.1 = (f32[512,512]{1,0:T(8,128)S(1)}, f32[512,512]{1,0:T(8,128)}, u32[]{:S(2)}) copy-start(f32[512,512]{1,0:T(8,128)} %factor_ref.1) | copy-start | bytes 3145732
  0.0 2.3 %collective-permute-start.1 = (f32[512,128]{1,0:T(8,128)}, f32[512,128]{1,0:T(8,128)S(1)}, u32[]{:S(2)}, u32[]{:S(2)}) collective-permute-start(f32[512,128]{1,0:T(8,128)} %param.8), channel_id=1, source_target_pairs={{0,1},{1,0},{2,3},{3,2},{4,5},{5,4},{6,7},{7,6},{8,9},{9,8},{10,11... | collective-permute-start | bytes 786440 | tf_op jit(solution)/shard_map/ppermute | solution.py:231
  2.3 6.9 %collective-permute-start.2 = (f32[256,128]{1,0:T(8,128)S(1)}, f32[256,128]{1,0:T(8,128)S(1)}, u32[]{:S(2)}, u32[]{:S(2)}) collective-permute-start(f32[256,128]{1,0:T(8,128)S(1)} %dynamic-slice_select_fusion), channel_id=1, source_target_pairs={{0,4},{1,7},{2,6},{3,5},{4,0},{5,3},{6,2},{7,1},{8,12},{9,15},{10,... | collective-permute-start | bytes 393224 | tf_op jit(solution)/shard_map/ppermute | solution.py:249
  3.5 10.6 %collective-permute-start.3 = (f32[256,128]{1,0:T(8,128)S(1)}, f32[256,128]{1,0:T(8,128)S(1)}, u32[]{:S(2)}, u32[]{:S(2)}) collective-permute-start(f32[256,128]{1,0:T(8,128)S(1)} %dynamic-slice_select_fusion), channel_id=1, source_target_pairs={{0,6},{1,5},{2,4},{3,7},{4,2},{5,1},{6,0},{7,3},{8,14},{9,13},{10,... | collective-permute-start | bytes 393224 | tf_op jit(solution)/shard_map/ppermute | solution.py:249
  4.8 9.3 %collective-permute-start.4 = (f32[256,128]{1,0:T(8,128)S(1)}, f32[256,128]{1,0:T(8,128)S(1)}, u32[]{:S(2)}, u32[]{:S(2)}) collective-permute-start(f32[256,128]{1,0:T(8,128)S(1)} %dynamic-slice_select_fusion), channel_id=1, source_target_pairs={{0,2},{1,3},{2,0},{3,1},{4,6},{5,7},{6,4},{7,5},{8,10},{9,11},{10,... | collective-permute-start | bytes 393224 | tf_op jit(solution)/shard_map/ppermute | solution.py:249
  6.0 11.9 %collective-permute-start = (f32[512,128]{1,0:T(8,128)S(1)}, f32[512,128]{1,0:T(8,128)S(1)}, u32[]{:S(2)}, u32[]{:S(2)}) collective-permute-start(f32[512,128]{1,0:T(8,128)S(1)} %constant_dynamic-slice_fusion.1), channel_id=1, source_target_pairs={{4,1},{6,9},{0,17},{2,25},{8,3},{10,11},{12,19},{14,27},{22,5},{18... | collective-permute-start | bytes 786440 | tf_op jit(solution)/shard_map/ppermute | solution.py:268
  14.1 1.4 %collective-permute-start.5 = (f32[256,128]{1,0:T(8,128)S(1)}, f32[256,128]{1,0:T(8,128)S(1)}, u32[]{:S(2)}, u32[]{:S(2)}) collective-permute-start(f32[256,128]{1,0:T(8,128)S(1)} %select_select_fusion.own_ref), channel_id=1, source_target_pairs={{0,1},{1,0},{2,3},{3,2},{4,5},{5,4},{6,7},{7,6},{8,9},{9,8},{10,11... | collective-permute-start | bytes 393224 | tf_op jit(solution)/shard_map/ppermute | solution.py:231

commit v13 on v12

--- a/solution.py
+++ b/solution.py
@@ -244,7 +244,7 @@
     while low < cols:
         high = min(4 * low, cols)
         away = apart & (high - low)
-        steps = [(2 * low, 3 * low), (3 * low, 2 * low), (low, low)] if high == 4 * low else [(low, low)]
+        steps = [(2 * low, low), (3 * low, 2 * low), (low, 3 * low)] if high == 4 * low else [(low, low)]
         received = [
             lax.ppermute(held, "col", [(i, i ^ step[i % 2]) for i in range(cols)]) for step in steps
         ]

time: 22.3 us -> 22.3 us (level)
  no operation moved by 1% of the time
where the time goes in v13:
time: 22.3 us; the launch traced here: 22.1 us
  Pallas kernels  7.27 us (33%)
  waiting for transfers between devices  5.47 us (25%)
  starting transfers between devices  5.25 us (24%)
  local copies, waits for them, and re-layouts  1.9 us (9%)
  other arithmetic  1.42 us (6%)
  between operations  0.79 us (4%)
    ppermute x3, waiting for transfers between devices, gather_panel(): lax.ppermute(held, 'col', [(i, i ^ step[i % 2]) for i in range(cols)])  4.9 us
    pallas_call x1, Pallas kernels, on_device(): pl.pallas_call(functools.partial(update_kernel, rows, cols), out_shape=sh...  4.16 us
    ppermute x3, starting transfers between devices, gather_panel(): lax.ppermute(held, 'col', [(i, i ^ step[i % 2]) for i in range(cols)])  2.71 us
    pallas_call x1, Pallas kernels, on_device(): pl.pallas_call(rows_kernel, out_shape=[shape((row_count, 3 * panel), bf16...  2.36 us
    ppermute x1, starting transfers between devices, on_device(): sent = lax.ppermute(own_half, ('row', 'col'), column_pairs(rows, cols))  1.79 us
    dynamic_slice x1, local copies, waits for them, and re-layouts, on_device(): own_half = lax.dynamic_slice_in_dim(points, part * col_count, col_count, 0)  0.97 us
    dynamic_slice x1, local copies, waits for them, and re-layouts, gather_panel(): mine = lax.dynamic_slice_in_dim(panel_pool, core * half_rows, half_rows, 0)  0.92 us
    ppermute x2, starting transfers between devices, swap(): return lax.ppermute(value, 'col', [(i, i ^ bit) for i in range(cols)])  0.75 us
  transfers between devices with their start and end apart: 6, of which 2 were waited for; matrix products, arithmetic and copies ran while one was open for 15% of the time, Pallas kernels for 14%

profile of v13, /device:TPU:29, one launch (start us, length us, event | category | flops | bytes accessed | tf_op | source)
XLA Modules:
  0.0 22.1 jit_solution(3672883630734006379)
XLA Ops:
  0.0 0.0 copy-start
  0.0 0.0 copy-start.1
  0.0 0.7 %collective-permute-start.1 = (f32[512,128]{1,0:T(8,128)}, f32[512,128]{1,0:T(8,128)S(1)}, u32[]{:S(2)}, u32[]{:S(2)}) collective-permute-start(f32[512,128]{1,0:T(8,128)} %param.8), channel_id=1, source_target_pairs={{0,1},{1,0},{2,3},{3,2},{4,5},{5,4},{6,7},{7,6},{8,9},{9,8},{10,11... | collective-permute-start | bytes 786440 | tf_op jit(solution)/shard_map/ppermute | solution.py:231
  1.4 0.9 %constant_dynamic-slice_fusion = f32[256,128]{1,0:T(8,128)S(1)} fusion(f32[512,128]{1,0:T(8,128)} %param.8, s32[]{:T(128)S(6)} %select_n.60), kind=kLoop, calls=%fused_computation.3 | loop fusion | bytes 262148 | tf_op jit(solution)/shard_map/dynamic_slice | solution.py:238
  2.3 0.0 collective-permute-done.1
  2.3 1.3 %collective-permute-start.2 = (f32[256,128]{1,0:T(8,128)S(1)}, f32[256,128]{1,0:T(8,128)S(1)}, u32[]{:S(2)}, u32[]{:S(2)}) collective-permute-start(f32[256,128]{1,0:T(8,128)S(1)} %dynamic-slice_select_fusion), channel_id=1, source_target_pairs={{0,4},{1,3},{2,6},{3,1},{4,0},{5,7},{6,2},{7,5},{8,12},{9,11},{10,... | collective-permute-start | bytes 393224 | tf_op jit(solution)/shard_map/ppermute | solution.py:249
  3.6 0.2 %collective-permute-start.3 = (f32[256,128]{1,0:T(8,128)S(1)}, f32[256,128]{1,0:T(8,128)S(1)}, u32[]{:S(2)}, u32[]{:S(2)}) collective-permute-start(f32[256,128]{1,0:T(8,128)S(1)} %dynamic-slice_select_fusion), channel_id=1, source_target_pairs={{0,6},{1,5},{2,4},{3,7},{4,2},{5,1},{6,0},{7,3},{8,14},{9,13},{10,... | collective-permute-start | bytes 393224 | tf_op jit(solution)/shard_map/ppermute | solution.py:249
  3.8 1.2 %collective-permute-start.4 = (f32[256,128]{1,0:T(8,128)S(1)}, f32[256,128]{1,0:T(8,128)S(1)}, u32[]{:S(2)}, u32[]{:S(2)}) collective-permute-start(f32[256,128]{1,0:T(8,128)S(1)} %dynamic-slice_select_fusion), channel_id=1, source_target_pairs={{0,2},{1,7},{2,0},{3,5},{4,6},{5,3},{6,4},{7,1},{8,10},{9,15},{10,... | collective-permute-start | bytes 393224 | tf_op jit(solution)/shard_map/ppermute | solution.py:249
  5.0 1.0 %constant_dynamic-slice_fusion.1 = f32[512,128]{1,0:T(8,128)S(1)} fusion(f32[1024,128]{1,0:T(8,128)} %points_ref.1, s32[]{:T(128)S(6)} %select_n.57), kind=kLoop, calls=%fused_computation.4 | loop fusion | bytes 524292 | tf_op jit(solution)/shard_map/dynamic_slice | solution.py:267
  6.0 1.8 %collective-permute-start = (f32[512,128]{1,0:T(8,128)S(1)}, f32[512,128]{1,0:T(8,128)S(1)}, u32[]{:S(2)}, u32[]{:S(2)}) collective-permute-start(f32[512,128]{1,0:T(8,128)S(1)} %constant_dynamic-slice_fusion.1), channel_id=1, source_target_pairs={{4,1},{6,9},{0,17},{2,25},{8,3},{10,11},{12,19},{14,27},{22,5},{18... | collective-permute-start | bytes 786440 | tf_op jit(solution)/shard_map/ppermute | solution.py:268
  7.8 0.7 %convert_element_type.3 = f32[512]{0:T(512)S(1)} convert(s32[512]{0:T(512)} %param.9) | non-fusion elementwise | flops 512 | bytes 4096 | tf_op jit(solution)/shard_map/convert_element_type | solution.py:269
  8.5 0.7 %pad_maximum_fusion = f32[1664]{0:T(1024)S(1)} fusion(f32[1024]{0:T(1024)} %param.13, f32[128]{0:T(128)} %param.12, f32[512]{0:T(512)S(1)} %convert_element_type.3), kind=kLoop, calls=%fused_computation.2 | loop fusion | flops 3328 | bytes 13312 | tf_op jit(solution)/shard_map/concatenate | solution.py:269
  9.2 0.0 collective-permute-done.2
  9.2 4.9 %collective-permute-done.3 = f32[256,128]{1,0:T(8,128)S(1)} collective-permute-done((f32[256,128]{1,0:T(8,128)S(1)}, f32[256,128]{1,0:T(8,128)S(1)}, u32[]{:S(2)}, u32[]{:S(2)}) %collective-permute-start.3) | collective-permute-done | bytes 131104 | tf_op jit(solution)/shard_map/ppermute | solution.py:249
  14.1 0.0 collective-permute-done.4
  14.1 0.1 collective-permute-start.5
  14.2 0.0 copy-done
  14.2 0.0 copy-done.1
  14.2 0.7 %shard_map.73 = (bf16[512,1536]{1,0:T(8,128)(2,1)S(1)}, bf16[1536,512]{1,0:T(8,128)(2,1)S(1)}, bf16[512,512]{1,0:T(8,128)(2,1)S(1)}, bf16[1024,512]{1,0:T(8,128)(2,1)S(1)}, f32[1024,1]{1,0:T(8,128)S(1)}) custom-call(f32[512,512]{1,0:T(8,128)S(1)} %copy-done.1, f32[1024,128]{1,0:T(8,128)S(1)} %copy-done, f32[1,1664]{1,0:T(1,128)S(1)} %broadcast_in_dim.3.vectors_ref), custom_call_target="tpu_custom_call" | custom-call | flops 100000000 | bytes 4000000 | tf_op jit(solution)/shard_map/pallas_call | solution.py:273
  15.0 0.6 %collective-permute-done.5.other_ref = f32[256,128]{1,0:T(8,128)S(1)} collective-permute-done((f32[256,128]{1,0:T(8,128)S(1)}, f32[256,128]{1,0:T(8,128)S(1)}, u32[]{:S(2)}, u32[]{:S(2)}) %collective-permute-start.5) | collective-permute-done | bytes 131104 | tf_op jit(solution)/shard_map/ppermute | solution.py:231
  15.6 2.4 %shard_map.74 = (bf16[1024,1536]{1,0:T(8,128)(2,1)S(1)}, bf16[512,512]{1,0:T(8,128)(2,1)S(1)}, f32[512,1]{1,0:T(8,128)S(1)}) custom-call(f32[256,128]{1,0:T(8,128)S(1)} %select_select_fusion.own_ref, f32[256,128]{1,0:T(8,128)S(1)} %collective-permute-done.5.other_ref, f32[1,1664]{1,0:T(1,128)S(1)} %broadcast_in_dim.3.vectors_ref, ...), custom_call_target="tpu_custom_call" | custom-call | flops 1 | bytes 1 | tf_op jit(solution)/shard_map/pallas_call | solution.py:285
  17.9 0.0 collective-permute-done.sent_ref
  17.9 4.2 %shard_map.75 = f32[1024,512]{1,0:T(8,128)} custom-call(f32[512,128]{1,0:T(8,128)S(1)} %collective-permute-done.sent_ref, f32[1,1664]{1,0:T(1,128)S(1)} %broadcast_in_dim.3.vectors_ref, bf16[512,1536]{1,0:T(8,128)(2,1)S(1)} %get-tuple-element.22.factor_left_ref, bf16[1024,512]{1,0:T(8,128)(2,1)S(1)} %get-tuple-element.23.left_ref, ...), custom_call_target="tpu_custom_call" | custom-call | flops 4000000000 | bytes 8000000 | tf_op jit(solution)/shard_map/pallas_call | solution.py:293
  (3 shorter events, 0.1 us)
Async XLA Ops:
  0.0 14.2 %copy-start = (f32[1024,128]{1,0:T(8,128)S(1)}, f32[1024,128]{1,0:T(8,128)}, u32[]{:S(2)}) copy-start(f32[1024,128]{1,0:T(8,128)} %points_ref.1) | copy-start | bytes 1572868
  0.0 14.2 %copy-start.1 = (f32[512,512]{1,0:T(8,128)S(1)}, f32[512,512]{1,0:T(8,128)}, u32[]{:S(2)}) copy-start(f32[512,512]{1,0:T(8,128)} %factor_ref.1) | copy-start | bytes 3145732
  0.0 2.3 %collective-permute-start.1 = (f32[512,128]{1,0:T(8,128)}, f32[512,128]{1,0:T(8,128)S(1)}, u32[]{:S(2)}, u32[]{:S(2)}) collective-permute-start(f32[512,128]{1,0:T(8,128)} %param.8), channel_id=1, source_target_pairs={{0,1},{1,0},{2,3},{3,2},{4,5},{5,4},{6,7},{7,6},{8,9},{9,8},{10,11... | collective-permute-start | bytes 786440 | tf_op jit(solution)/shard_map/ppermute | solution.py:231
  2.3 6.9 %collective-permute-start.2 = (f32[256,128]{1,0:T(8,128)S(1)}, f32[256,128]{1,0:T(8,128)S(1)}, u32[]{:S(2)}, u32[]{:S(2)}) collective-permute-start(f32[256,128]{1,0:T(8,128)S(1)} %dynamic-slice_select_fusion), channel_id=1, source_target_pairs={{0,4},{1,3},{2,6},{3,1},{4,0},{5,7},{6,2},{7,5},{8,12},{9,11},{10,... | collective-permute-start | bytes 393224 | tf_op jit(solution)/shard_map/ppermute | solution.py:249
  3.6 10.5 %collective-permute-start.3 = (f32[256,128]{1,0:T(8,128)S(1)}, f32[256,128]{1,0:T(8,128)S(1)}, u32[]{:S(2)}, u32[]{:S(2)}) collective-permute-start(f32[256,128]{1,0:T(8,128)S(1)} %dynamic-slice_select_fusion), channel_id=1, source_target_pairs={{0,6},{1,5},{2,4},{3,7},{4,2},{5,1},{6,0},{7,3},{8,14},{9,13},{10,... | collective-permute-start | bytes 393224 | tf_op jit(solution)/shard_map/ppermute | solution.py:249
  3.8 10.3 %collective-permute-start.4 = (f32[256,128]{1,0:T(8,128)S(1)}, f32[256,128]{1,0:T(8,128)S(1)}, u32[]{:S(2)}, u32[]{:S(2)}) collective-permute-start(f32[256,128]{1,0:T(8,128)S(1)} %dynamic-slice_select_fusion), channel_id=1, source_target_pairs={{0,2},{1,7},{2,0},{3,5},{4,6},{5,3},{6,4},{7,1},{8,10},{9,15},{10,... | collective-permute-start | bytes 393224 | tf_op jit(solution)/shard_map/ppermute | solution.py:249
  6.0 11.9 %collective-permute-start = (f32[512,128]{1,0:T(8,128)S(1)}, f32[512,128]{1,0:T(8,128)S(1)}, u32[]{:S(2)}, u32[]{:S(2)}) collective-permute-start(f32[512,128]{1,0:T(8,128)S(1)} %constant_dynamic-slice_fusion.1), channel_id=1, source_target_pairs={{4,1},{6,9},{0,17},{2,25},{8,3},{10,11},{12,19},{14,27},{22,5},{18... | collective-permute-start | bytes 786440 | tf_op jit(solution)/shard_map/ppermute | solution.py:268
  14.1 1.4 %collective-permute-start.5 = (f32[256,128]{1,0:T(8,128)S(1)}, f32[256,128]{1,0:T(8,128)S(1)}, u32[]{:S(2)}, u32[]{:S(2)}) collective-permute-start(f32[256,128]{1,0:T(8,128)S(1)} %select_select_fusion.own_ref), channel_id=1, source_target_pairs={{0,1},{1,0},{2,3},{3,2},{4,5},{5,4},{6,7},{7,6},{8,9},{9,8},{10,11... | collective-permute-start | bytes 393224 | tf_op jit(solution)/shard_map/ppermute | solution.py:231
